TPU v7x, 32 devices: a whole 2x2x4 slice. The times are simulated.
32 devices in a mesh: dp: 4 (over y, x), seq: 8 (over z, core).
Axes of the slice: x: 2, y: 2, z: 4, core: 2. Of those that a mesh axis runs over, the one named last changes fastest.
Arguments:
- tokens: int32 [16384], P(('dp', 'seq')), parts along dimension 0, may hold values from 0 to 3
- dilations: int32 [2], replicated, may hold values from 1 to 64, as said below
- embed: float32 [4, 256], replicated, may hold values from -6 to 6
- conv_weight: float32 [2, 3, 256, 512], replicated, may hold values from -0.1875 to 0.1875
- mix_weight: float32 [2, 256, 512], replicated, may hold values from -0.1875 to 0.1875
- gate_bias: float32 [2, 512], replicated, may hold values from -3 to 3
- out_weight: float32 [2, 256, 256], replicated, may hold values from -0.375 to 0.375
- cot_fwd: float32 [16384, 256], P(('dp', 'seq')), parts along dimension 0, may hold values from -6 to 6
- cot_rev: float32 [16384, 256], P(('dp', 'seq')), parts along dimension 0, may hold values from -6 to 6
Outputs:
- out_fwd: float32 [16384, 256], P(('dp', 'seq')), parts along dimension 0
- out_rev: float32 [16384, 256], P(('dp', 'seq')), parts along dimension 0
- grad_embed: float32 [16, 256], P('dp'), parts along dimension 0
- grad_conv: float32 [8, 3, 256, 512], P('dp'), parts along dimension 0
- grad_mix: float32 [8, 256, 512], P('dp'), parts along dimension 0
- grad_bias: float32 [8, 512], P('dp'), parts along dimension 0
- grad_out: float32 [8, 256, 256], P('dp'), parts along dimension 0
There are 4 independent parts, one for each index of `dp`. A program takes and returns all parts, laid end to end along the dimension named above; an argument that names none is the same for every part. Nothing has to cross between parts.
Inputs may be any that keep to these rules, and one draw needn't show every extreme that they name: `dilations`: exactly one layer's dilation equals 64; the others lie below it.
All inputs are finite; a program needn't handle non-finite values.
Results may differ from a plain program's by a relative error of at most 0.00012.
Values sent between devices are 32-bit elements; how exact they have to be, the bound alone decides.
No kernel may reach another device: no remote copies, remote signals or barrier semaphores. Data moves between devices by JAX's collectives and lax.ppermute only.
A program may use at most 128 MiB of HBM per device.

v0:
```python
import jax
import jax.numpy as jnp
from jax import lax
from jax.experimental import pallas as pl
from jax.experimental.pallas import tpu as pltpu
from jax.sharding import PartitionSpec as P

CONTEXTS = 96
INNER = 64
EDGE = 16
LOCAL = INNER + EDGE
TAPS = 3 * LOCAL
HALO = 128
F32 = jnp.float32
BF16 = jnp.bfloat16
VMEM_LIMIT = 40 * 1024 * 1024


def split(x):
    high = x.astype(BF16)
    return high, (x - high.astype(F32)).astype(BF16)


def dot(a, b, ca=1, cb=0):
    return lax.dot_general(a, b, (((ca,), (cb,)), ((), ())), preferred_element_type=F32)


def dot2(exact, pair, ca=1, cb=0):
    return dot(exact, pair[0], ca, cb) + dot(exact, pair[1], ca, cb)


def dot3(a, b, ca=1, cb=0):
    return dot(a[0], b[0], ca, cb) + (dot(a[0], b[1], ca, cb) + dot(a[1], b[0], ca, cb))


def dot3_few(a, b):
    rows = a[0].shape[0]
    both = dot(jnp.concatenate([a[0].astype(F32), a[1].astype(F32)], axis=0).astype(BF16), b[0])
    return both[:rows] + (both[rows:] + dot(a[0], b[1]))


def letters(index):
    inner = index < 64
    left = (index >= 64) & (index < 80)
    low = index & 3
    mid = (index >> 2) & 3
    l = jnp.where(inner, (index >> 4) & 3, jnp.where(left, -1, mid))
    m = jnp.where(inner | left, mid, low)
    r = jnp.where(inner | left, low, -1)
    return l, m, r


def mirrored(index):
    low = 3 - (index & 3)
    mid = 3 - ((index >> 2) & 3)
    high = 3 - ((index >> 4) & 3)
    inner = low * 16 + mid * 4 + high
    left = 80 + low * 4 + mid
    right = 64 + low * 4 + mid
    return jnp.where(index < 64, inner, jnp.where(index < 80, left, right))


def permutation():
    rows = lax.broadcasted_iota(jnp.int32, (CONTEXTS, CONTEXTS), 0)
    cols = lax.broadcasted_iota(jnp.int32, (CONTEXTS, CONTEXTS), 1)
    return (mirrored(rows) == cols).astype(F32).astype(BF16)


def letter_hot():
    rows = lax.broadcasted_iota(jnp.int32, (CONTEXTS, 32), 0)
    cols = lax.broadcasted_iota(jnp.int32, (CONTEXTS, 32), 1)
    l, m, r = letters(rows)
    kind = cols >> 3
    value = jnp.where(kind == 0, l, jnp.where(kind == 1, m, jnp.where(kind == 2, r, 3 - m)))
    return (value == (cols & 7)).astype(F32).astype(BF16)


def gates(mixed):
    channels = mixed.shape[1] // 2
    tanh_part = jnp.tanh(mixed[:, :channels])
    sig_part = 0.5 + 0.5 * jnp.tanh(0.5 * mixed[:, channels:])
    return tanh_part, sig_part


def gate_grads(grad_hidden, tanh_part, sig_part):
    scaled = grad_hidden * sig_part
    return scaled * (1.0 - tanh_part * tanh_part), scaled * tanh_part * (1.0 - sig_part)


class Fetch:
    def __init__(self, sems):
        self.sems = sems
        self.copies = []

    def start(self, source, target):
        copy = pltpu.make_async_copy(source, target, self.sems.at[len(self.copies)])
        copy.start()
        self.copies.append(copy)
        return len(self.copies) - 1

    def wait(self, *which):
        for at in which:
            self.copies[at].wait()


def padded_base(embed):
    return jnp.concatenate([embed[...], jnp.zeros((4, embed.shape[1]), F32)], axis=0)


def left_side():
    return lax.axis_index("seq") * 2 < lax.axis_size("seq")


def local_rows(rows):
    edge = jnp.where(left_side(), rows[INNER : INNER + EDGE], rows[INNER + EDGE : INNER + 2 * EDGE])
    return jnp.concatenate([rows[:INNER], edge], axis=0)


def join_four_kernel(first, second, third, fourth, after, out):
    for at, part in enumerate((first, second, third, fourth)):
        out[at : at + 1, :] = part[...]


def touch_kernel(value, after, *outs):
    begin = 0
    for out in outs:
        out[...] = value[begin : begin + out.shape[0], :]
        begin += out.shape[0]


def first_tables_kernel(
    tokens_in, embed_in, conv_in, mix_in, out_in, own, taps, conv, mix, out_w, embed, sems,
):
    fetch = Fetch(sems)
    fetch.start(embed_in, embed)
    first = [fetch.start(conv_in.at[0, k], conv.at[k]) for k in range(3)]
    first += [fetch.start(mix_in.at[0], mix)]
    rest = [fetch.start(tokens_in, own), fetch.start(out_in.at[0], out_w)]
    fetch.wait(0)
    base = split(padded_base(embed))
    for k in range(4):
        fetch.wait(first[k])
        taps[k * 8 : (k + 1) * 8, :] = dot3_few(base, split(conv[k] if k < 3 else mix[...]))
    fetch.wait(*rest)


def second_tables_kernel(
    taps, embed, bias, turn, conv_in, mix_in, out_in, cot_fwd_in, cot_rev_in, after,
    table, local, mixed_table, pre_high, pre_low, cot_high, cot_low, conv, mix, out_w,
    cots, sems,
):
    length = cots.shape[1]
    fetch = Fetch(sems)
    second = [fetch.start(conv_in.at[1, k], conv.at[k]) for k in range(3)]
    second += [fetch.start(mix_in.at[1], mix)]
    last = [fetch.start(out_in.at[1], out_w)]
    last += [fetch.start(cot_in, cots.at[strand]) for strand, cot_in in enumerate((cot_fwd_in, cot_rev_in))]
    hot = letter_hot()
    mixed = dot2(hot, split(taps[...])) + bias[0:1, :]
    tanh_part, sig_part = gates(mixed)
    own = dot2(hot[:, 8:16], split(padded_base(embed)))
    level = own + dot3_few(split(tanh_part * sig_part), split(turn[...]))
    table[...] = level
    local[...] = local_rows(level)
    mixed_table[...] = mixed
    level = split(level)
    swap = permutation()
    partner = tuple(dot(swap, piece).astype(BF16) for piece in level)
    pre_high[TAPS:, :] = jnp.zeros((pre_high.shape[0] - TAPS, pre_high.shape[1]), BF16)
    pre_low[TAPS:, :] = jnp.zeros((pre_low.shape[0] - TAPS, pre_low.shape[1]), BF16)
    for k in (0, 2, 1):
        fetch.wait(second[k])
        value = dot3_few(level, split(conv[k]))
        if k == 1:
            fetch.wait(second[3])
            value = value + dot3_few(partner, split(mix[...])) + bias[1:2, :]
        high, low = split(local_rows(value))
        pre_high[k * LOCAL : (k + 1) * LOCAL, :] = high
        pre_low[k * LOCAL : (k + 1) * LOCAL, :] = low
    for strand in range(2):
        rows = slice(strand * length, (strand + 1) * length)
        fetch.wait(last[1 + strand])
        cot_high[rows, :], cot_low[rows, :] = split(cots[strand])
    fetch.wait(last[0])


def windows(parts, count):
    length = parts[0].shape[1]
    place = lax.axis_index("seq")
    last = count - 1

    def block(at):
        total, begin = None, 0
        for part in parts:
            rows = lax.broadcasted_iota(jnp.int32, part.shape, 0) + begin
            piece = jnp.sum(jnp.where(rows == (place ^ at), part[...], 0), axis=0, keepdims=True)
            total = piece if total is None else total + piece
            begin += part.shape[0]
        return total

    def window(at):
        before = jnp.where(at == 0, -1, block(jnp.maximum(at - 1, 0))[:, length - HALO :])
        after = jnp.where(at == last, -1, block(jnp.minimum(at + 1, last))[:, :HALO])
        return [before, block(at), after]

    fwd = jnp.concatenate(window(place), axis=1)
    rev = jnp.concatenate(window(last - place), axis=1)
    rev = jnp.where(rev < 0, -1, 3 - rev)
    tiles = rev.shape[1] // 128
    blocks = [rev[:, i * 128 : (i + 1) * 128] for i in reversed(range(tiles))]
    blocks += [jnp.zeros((8 - tiles, 128), jnp.int32)]
    stacked = jnp.concatenate(blocks, axis=0).astype(F32).astype(BF16)
    rows = lax.broadcasted_iota(jnp.int32, (128, 128), 0)
    cols = lax.broadcasted_iota(jnp.int32, (128, 128), 1)
    flip = (rows + cols == 127).astype(F32).astype(BF16)
    turned = dot(stacked, flip).astype(jnp.int32)
    rev = jnp.concatenate([turned[i : i + 1, :] for i in range(tiles)], axis=1)
    return fwd, rev


def local_contexts(window, first, second, length):
    width = window.shape[1]
    base = jnp.broadcast_to(window, (8, width))
    l = pltpu.roll(base, first, 1)
    r = pltpu.roll(base, width - first, 1)
    index = jnp.where(l < 0, INNER + base * 4 + r, jnp.where(r < 0, INNER + l * 4 + base, l * 16 + base * 4 + r))
    index = jnp.where(base < 0, LOCAL, index)
    before = pltpu.roll(index, second, 1)
    after = pltpu.roll(index, width - second, 1)
    return [x[0:1, HALO : HALO + length] for x in (before, index, after)]


def hot_rows(index):
    rows = lax.broadcasted_iota(jnp.int32, (LOCAL, index.shape[1]), 0)
    return (rows == index).astype(F32).astype(BF16)


def deal(quarters, keep, send):
    bit = lax.axis_index("seq") & 1
    keep[...] = quarters[pl.ds(bit * 2, 2)]
    send[...] = quarters[pl.ds((1 - bit) * 2, 2)]


def forward_kernel(count, dil, *refs):
    steps = count.bit_length() - 2
    parts, refs = refs[:steps], refs[steps:]
    (pre_high, pre_low, cot_high, cot_low, keep, send, hidden_high, hidden_low, hots, slopes, quarters) = refs
    length = parts[0].shape[1]
    channels = cot_high.shape[1]
    pre = (pre_high[...], pre_low[...])
    both = windows(parts, count)
    pad = jnp.zeros((pre_high.shape[0] - TAPS, length), BF16)
    total_o = total_c = None
    for strand in range(2):
        index = local_contexts(both[strand], dil[0], dil[1], length)
        hot = jnp.concatenate([hot_rows(x) for x in index] + [pad], axis=0)
        hots[strand] = hot
        mixed = dot2(hot, pre, 0, 0)
        tanh_part, sig_part = gates(mixed)
        product = tanh_part * sig_part
        hidden = split(product)
        rows = slice(strand * length, (strand + 1) * length)
        hidden_high[rows, :] = hidden[0]
        hidden_low[rows, :] = hidden[1]
        slopes[rows, :channels] = sig_part - product * tanh_part
        slopes[rows, channels:] = product - product * sig_part
        cot = (cot_high[rows, :], cot_low[rows, :])
        part_o = dot3(hidden, cot, 0, 0)
        part_c = dot2(hot[LOCAL : 2 * LOCAL], cot)
        total_o = part_o if total_o is None else total_o + part_o
        total_c = part_c if total_c is None else total_c + part_c
    side = channels // 4
    for q in range(4):
        lanes = slice((q >> 1) * 128, (q >> 1) * 128 + 128)
        quarters[q, :side, :] = total_o[q * side : (q + 1) * side, :128]
        quarters[q, side : 2 * side, :] = total_o[q * side : (q + 1) * side, 128:]
        for begin, rows, at in ((0, INNER // 2, 2 * side), (INNER, EDGE // 2, 2 * side + INNER // 2)):
            begin += (q & 1) * rows
            quarters[q, at : at + rows, :] = total_c[begin : begin + rows, lanes]
    deal(quarters, keep, send)


def taps_kernel(hots, slopes, cot_high, cot_low, out_w, keep, send, quarters):
    length = hots.shape[2]
    weight = split(out_w[...])
    total = None
    for strand in range(2):
        rows = slice(strand * length, (strand + 1) * length)
        grad = dot3((cot_high[rows, :], cot_low[rows, :]), weight, 1, 1)
        part = dot2(hots[strand], split(slopes[rows, :] * jnp.concatenate([grad, grad], axis=1)))
        total = part if total is None else total + part
    for q in range(4):
        quarters[q] = total[:TAPS, q * 128 : (q + 1) * 128]
    deal(quarters, keep, send)


def halve_kernel(kept, received, keep, send):
    bit = (lax.axis_index("seq") >> 1) & 1
    send[...] = kept[1 - bit] + received[1 - bit]
    keep[...] = kept[bit] + received[bit]


def add_after_kernel(kept, received, after, out):
    out[...] = kept[...] + received[...]


def halve_after_kernel(kept, received, after, keep, send):
    halve_kernel(kept, received, keep, send)


def outputs_kernel(hots, hidden_high, hidden_low, local, out_w, after, out_fwd, out_rev, values, sems):
    length = hots.shape[2]
    fetch = Fetch(sems)
    weight = split(out_w[...])
    level = split(local[...])
    for strand, out in enumerate((out_fwd, out_rev)):
        rows = slice(strand * length, (strand + 1) * length)
        own = dot2(hots[strand, LOCAL : 2 * LOCAL, :], level, 0, 0)
        values[strand] = own + dot3((hidden_high[rows, :], hidden_low[rows, :]), weight)
        fetch.start(values.at[strand], out)
    fetch.wait(0, 1)


def prepare_kernel(
    first_conv, first_mix, second_conv, second_mix, out_w, table, mixed_table, after,
    first_high, first_low, second_high, second_low, turn_high, turn_low,
    level_high, level_low, partner_high, partner_low, hidden_high, hidden_low, slopes, hot,
):
    level = split(table[...])
    swap = permutation()
    level_high[...], level_low[...] = level
    partner_high[...], partner_low[...] = tuple(dot(swap, piece).astype(BF16) for piece in level)
    for conv, mix, high, low in (
        (second_conv, second_mix, second_high, second_low),
        (first_conv, first_mix, first_high, first_low),
    ):
        for k in range(4):
            high[k], low[k] = split((conv[k] if k < 3 else mix[...]).T)
    turn_high[...], turn_low[...] = split(out_w[...].T)
    tanh_part, sig_part = gates(mixed_table[...])
    product = tanh_part * sig_part
    hidden_high[...], hidden_low[...] = split(product)
    channels = product.shape[1]
    slopes[:, :channels] = sig_part - product * tanh_part
    slopes[:, channels:] = product - product * sig_part
    hot[...] = letter_hot()


def merge(mine, theirs, inner, edge):
    left = left_side()
    both = mine[inner, :] + theirs[inner, :]
    own, other = mine[edge, :], theirs[edge, :]
    return both, jnp.where(left, own, other), jnp.where(left, other, own)


def merge_blocks(mine, theirs, out, sizes):
    at = to = 0
    for inner, edge in sizes:
        pieces = merge(mine, theirs, slice(at, at + inner), slice(at + inner, at + inner + edge))
        out[to : to + inner, :] = pieces[0]
        out[to + inner : to + inner + edge, :] = pieces[1]
        out[to + inner + edge : to + inner + 2 * edge, :] = pieces[2]
        at, to = at + inner + edge, to + inner + 2 * edge


def merge_taps_kernel(mine, theirs, after, out):
    merge_blocks(mine, theirs, out, [(INNER, EDGE)] * 3)


def merge_rest_kernel(mine, theirs, after, out):
    merge_blocks(mine, theirs, out, [(mine.shape[0] - EDGE // 2, EDGE // 2)])


def gather_quarters(pieces, quarters):
    place = lax.axis_index("seq")
    low, high = place & 1, (place >> 1) & 1
    for parts, x, y in zip(pieces, (0, 0, 1, 1), (0, 1, 0, 1)):
        begin = 0
        for part in parts:
            rows = part.shape[0]
            quarters[(low ^ x) * 2 + (high ^ y), begin : begin + rows, :] = part[...]
            begin += rows


def columns_kernel(own, cores, *refs):
    pieces = [refs[:1], refs[1:3]] if own else [refs[:1]]
    refs = refs[sum(len(piece) for piece in pieces) :]
    level_high, level_low, partner_high, partner_low, second_high, second_low, *refs = refs
    if not own:
        partial, g_conv_in, g_mix_in, *refs = refs
    g_conv_out, g_mix_out, bias, total, taps, g_conv, g_mix, out_sems = refs
    place = lax.axis_index("seq")
    low, high = place & 1, (place >> 1) & 1
    high = high if own else 1 - high
    store = Fetch(out_sems)
    level = (level_high[...], level_low[...])
    partner = (partner_high[...], partner_low[...])
    grad_level = None if own else partial[...]
    for at, core in enumerate(cores):
        begin = 0
        for piece in pieces[at]:
            rows = piece.shape[0]
            taps[begin : begin + rows, :] = piece[...]
            begin += rows
        column = pl.multiple_of(((low ^ core) * 2 + high) * 128, 128)
        block = pl.ds(column, 128)

        def weight(k):
            return second_high[k, block, :], second_low[k, block, :]

        pairs = [split(taps[k * CONTEXTS : (k + 1) * CONTEXTS, :]) for k in range(3)]
        for k, pair in enumerate(pairs):
            g_conv[at, k] = dot3(level, pair, 0, 0)
            store.start(g_conv.at[at, k], g_conv_out.at[1, k, :, block])
        g_mix[at] = dot3(partner, pairs[1], 0, 0)
        store.start(g_mix.at[at], g_mix_out.at[1, :, block])
        bias[at : at + 1, :] = jnp.sum(taps[CONTEXTS : 2 * CONTEXTS, :], axis=0, keepdims=True)
        part = dot2(permutation(), split(dot3_few(pairs[1], weight(3))))
        for k, pair in enumerate(pairs):
            part = part + dot3_few(pair, weight(k))
        grad_level = part if grad_level is None else grad_level + part
    total[...] = grad_level
    store.wait(*range(len(store.copies)))


def first_layer_kernel(
    piece_00, piece_01, piece_10, piece_11, partial, bias_own, bias_other, bias_far, embed,
    first_high, first_low, turn_high, turn_low, hidden_high, hidden_low, slopes, hot_in,
    g_conv_in, g_mix_in, g_conv_out, g_mix_out, g_embed_out, g_bias_out, g_out_out,
    quarters, bias_rows, g_conv, g_mix, g_embed, g_bias, g_out, out_sems,
):
    channels = embed.shape[1]
    store = Fetch(out_sems)
    gather_quarters([(piece,) for piece in (piece_00, piece_01, piece_10, piece_11)], quarters)
    side = channels // 4
    rest = []
    for begin, rows in ((0, INNER // 2), (INNER // 2, EDGE // 2), (INNER // 2 + EDGE // 2, EDGE // 2)):
        begin += 2 * side
        halves = [[quarters[2 * h + i, begin : begin + rows, :] for i in range(2)] for h in range(2)]
        rest.append(jnp.concatenate([jnp.concatenate(x, axis=0) for x in halves], axis=1))
    grad_level = split(partial[...] + jnp.concatenate(rest, axis=0))
    grad_hidden = dot3_few(grad_level, (turn_high[...], turn_low[...]))
    grad_mixed = slopes[...] * jnp.concatenate([grad_hidden, grad_hidden], axis=1)
    hot = hot_in[...]
    by_letter = dot2(hot, split(grad_mixed), 0, 0)
    base = split(padded_base(embed))
    stacked = jnp.concatenate([base[0].astype(F32), base[0].astype(F32), base[1].astype(F32)], axis=0).astype(BF16)
    pieces = []
    for k in range(4):
        piece = split(by_letter[k * 8 : (k + 1) * 8, :])
        pieces.append(piece)
        high, low = piece[0].astype(F32), piece[1].astype(F32)
        value = dot(stacked, jnp.concatenate([high, low, high], axis=0).astype(BF16), 0, 0)
        if k < 3:
            g_conv[k] = value
            store.start(g_conv.at[k], g_conv_out.at[0, k])
        else:
            g_mix[...] = value
            store.start(g_mix, g_mix_out.at[0])
    g_out[0] = dot3((hidden_high[...], hidden_low[...]), grad_level, 0, 0)
    for q in range(4):
        for h in range(2):
            g_out[1, q * side : (q + 1) * side, h * 128 : (h + 1) * 128] = quarters[q, h * side : (h + 1) * side, :]
    store.start(g_out, g_out_out)
    place = lax.axis_index("seq")
    low, high = place & 1, (place >> 1) & 1
    for row, x, y in (
        (bias_own[0:1, :], 0, 0), (bias_own[1:2, :], 1, 0), (bias_other[...], 0, 1), (bias_far[...], 1, 1)
    ):
        bias_rows[(low ^ x) * 2 + (high ^ y)] = row
    g_bias[0:1, :] = jnp.sum(grad_mixed, axis=0, keepdims=True)
    g_bias[1:2, :] = jnp.concatenate([bias_rows[q] for q in range(4)], axis=1)
    store.start(g_bias, g_bias_out)
    grad_base = dot2(hot[:, 8:16], grad_level, 0, 0)
    for k in range(4):
        grad_base = grad_base + dot3_few(pieces[k], (first_high[k], first_low[k]))
    g_embed[...] = grad_base[:4, :]
    store.start(g_embed, g_embed_out)
    store.wait(*range(len(store.copies)))


VMEM, SMEM, HBM = pltpu.VMEM, pltpu.SMEM, pltpu.HBM


def call(kernel, ins, outs, scratch=(), aliases=None, micros=0.001):
    run = pl.pallas_call(
        kernel,
        out_shape=[space(shape, kind) for shape, kind, space in outs],
        in_specs=[pl.BlockSpec(memory_space=space) for space in ins],
        out_specs=[pl.BlockSpec(memory_space=space) for _, _, space in outs],
        scratch_shapes=list(scratch),
        input_output_aliases=aliases or {},
        cost_estimate=pl.CostEstimate(flops=int(micros * 1.1e9), bytes_accessed=int(micros * 3e6), transcendentals=0),
        compiler_params=pltpu.CompilerParams(vmem_limit_bytes=VMEM_LIMIT),
    )

    def placed(*args):
        return run(*[pltpu.with_memory_space_constraint(x, HBM) if space is HBM else x for x, space in zip(args, ins)])

    return placed


def swapped(value, mask):
    pairs = [(source, source ^ mask) for source in range(lax.axis_size("seq"))]
    return lax.ppermute(value, "seq", pairs)


def crossed(piece, count, rest):
    mask = 4
    while mask < count // 2:
        piece = piece + swapped(piece, mask)
        mask *= 2
    return rest(piece, swapped(piece, mask))


def on_device(
    tokens, dilations, embed, conv_weight, mix_weight, gate_bias, out_weight, cot_fwd, cot_rev
):
    channels = embed.shape[1]
    wide = 2 * channels
    length = tokens.shape[0]
    count = lax.axis_size("seq")
    sems = pltpu.SemaphoreType.DMA
    square = (channels, channels)

    row = tokens.reshape(1, length)
    near = [swapped(row, mask) for mask in (1, 2, 3)]
    layer_weights = [(conv_weight.shape[1:], F32, VMEM), (mix_weight.shape[1:], F32, VMEM)]
    own, taps, first_conv, first_mix, turn = call(
        first_tables_kernel,
        [HBM] * 5,
        [(row.shape, row.dtype, VMEM), ((32, wide), F32, VMEM), *layer_weights, (square, F32, VMEM)],
        [VMEM(embed.shape, F32), sems((7,))],
        micros=1.7,
    )(row, embed, conv_weight, mix_weight, out_weight)
    known = call(join_four_kernel, [VMEM] * 5, [((4, length), row.dtype, VMEM)])(own, *near, taps)[0]
    parts = [known, swapped(known, 4)]
    deep = -(-TAPS // 128) * 128
    (table, local, mixed_table, pre_high, pre_low, cot_high, cot_low,
     second_conv, second_mix, last_weight) = call(
        second_tables_kernel,
        [VMEM] * 4 + [HBM] * 5 + [VMEM],
        [((CONTEXTS, channels), F32, VMEM), ((LOCAL, channels), F32, VMEM), ((CONTEXTS, wide), F32, VMEM)]
        + [((deep, wide), BF16, VMEM)] * 2
        + [((2 * length, channels), BF16, VMEM)] * 2
        + layer_weights
        + [(square, F32, VMEM)],
        [VMEM((2, length, channels), F32), sems((7,))],
        micros=3.0,
    )(taps, embed, gate_bias, turn, conv_weight, mix_weight, out_weight, cot_fwd, cot_rev, known)
    mask = 8
    while mask < count:
        known = jnp.concatenate([known, parts[-1]], axis=0)
        parts.append(swapped(known, mask))
        mask *= 2

    rows_x, rows_y = TAPS, channels // 2 + LOCAL // 2
    keep_y, send_y, hidden_high, hidden_low, hots, slopes = call(
        lambda *refs: forward_kernel(count, *refs),
        [SMEM] + [VMEM] * (len(parts) + 4),
        [((2, rows_y, 128), F32, VMEM)] * 2
        + [((2 * length, channels), BF16, VMEM)] * 2
        + [((2, deep, length), BF16, VMEM), ((2 * length, wide), F32, VMEM)],
        [VMEM((4, rows_y, 128), F32)],
        micros=2.0,
    )(dilations, *parts, pre_high, pre_low, cot_high, cot_low)
    keep_x, send_x = call(
        taps_kernel,
        [VMEM] * 5,
        [((2, rows_x, 128), F32, VMEM)] * 2,
        [VMEM((4, rows_x, 128), F32)],
        micros=1.5,
    )(hots, slopes, cot_high, cot_low, last_weight)

    def halved(keep, received, after):
        outs = [(keep.shape[1:], F32, VMEM)] * 2
        return call(halve_after_kernel, [VMEM] * 3, outs)(keep, received, after)

    def added(kept, received, after, space=VMEM):
        return call(add_after_kernel, [VMEM] * 2 + [space], [(kept.shape, F32, VMEM)])(kept, received, after)[0]

    def touched(value, after, cuts=1):
        shape = (value.shape[0] // cuts, value.shape[1])
        return call(touch_kernel, [VMEM] * 2, [(shape, value.dtype, VMEM)] * cuts)(value, after)

    keep_y, send_y = halved(keep_y, swapped(send_y, 1), keep_x)
    keep_x, send_x = halved(keep_x, swapped(send_x, 1), keep_y)
    sum_y = added(keep_y, swapped(send_y, 2), keep_x)
    out_fwd, out_rev = call(
        outputs_kernel,
        [VMEM] * 6,
        [((length, channels), F32, HBM)] * 2,
        [VMEM((2, length, channels), F32), sems((2,))],
        micros=2.0,
    )(hots, hidden_high, hidden_low, local, last_weight, sum_y)
    sum_x = added(keep_x, swapped(send_x, 2), out_rev, HBM)
    first_high, first_low, second_high, second_low, turn_high, turn_low, *tables = call(
        prepare_kernel,
        [VMEM] * 8,
        [((4, wide, channels), BF16, VMEM)] * 4
        + [(square, BF16, VMEM)] * 2
        + [((CONTEXTS, channels), BF16, VMEM)] * 6
        + [((CONTEXTS, wide), F32, VMEM), ((CONTEXTS, 32), BF16, VMEM)],
        micros=1.4,
    )(first_conv, first_mix, second_conv, second_mix, turn, table, mixed_table, sum_x)
    levels, tables = tables[:4], tables[4:]

    def merged(kernel, rows, mine, theirs, after):
        return call(kernel, [VMEM] * 3, [((rows, 128), F32, VMEM)])(mine, theirs, after)[0]

    merged_x, merged_y = 3 * CONTEXTS, rows_y + EDGE // 2
    piece_y = crossed(sum_y, count, lambda x, y: merged(merge_rest_kernel, merged_y, x, y, turn_low))
    piece_x = crossed(sum_x, count, lambda x, y: merged(merge_taps_kernel, merged_x, x, y, piece_y))
    other_y = swapped(piece_y, 2)
    core_x = [swapped(x, 1) for x in touched(piece_x, other_y, 2)]

    def columns(own, cores, pieces, before=(), micros=0.05):
        inner = len(pieces) + 6
        return call(
            lambda *refs: columns_kernel(own, cores, *refs),
            [VMEM] * inner + ([VMEM] + [HBM] * 2 if before else []),
            [
                (conv_weight.shape, F32, HBM),
                (mix_weight.shape, F32, HBM),
                ((len(cores), 128), F32, VMEM),
                ((CONTEXTS, channels), F32, VMEM),
            ],
            [
                VMEM((merged_x, 128), F32),
                VMEM((len(cores), 3, channels, 128), F32),
                VMEM((len(cores), channels, 128), F32),
                sems((4 * len(cores),)),
            ],
            aliases={inner + 1: 0, inner + 2: 1} if before else None,
            micros=micros,
        )(*pieces, *levels, second_high, second_low, *before)

    core_y, far_y = swapped(piece_y, 1), swapped(other_y, 1)
    g_conv, g_mix, bias_own, partial = columns(True, (0, 1), (piece_x, *core_x))
    other_x = swapped(piece_x, 2)
    rest_y = touched(far_y, partial)[0]
    far_x = [swapped(x, 1) for x in touched(other_x, rest_y)]
    g_conv, g_mix, bias_other, partial = columns(False, (0,), (other_x,), (partial, g_conv, g_mix))
    g_conv, g_mix, bias_far, partial = columns(False, (1,), far_x, (partial, g_conv, g_mix), micros=1.2)
    g_conv, g_mix, g_embed, g_bias, g_out = call(
        first_layer_kernel,
        [VMEM] * 17 + [HBM] * 2,
        [
            (conv_weight.shape, F32, HBM),
            (mix_weight.shape, F32, HBM),
            (embed.shape, F32, HBM),
            (gate_bias.shape, F32, HBM),
            (out_weight.shape, F32, HBM),
        ],
        [
            VMEM((4, merged_y, 128), F32),
            VMEM((4, 1, 128), F32),
            VMEM(conv_weight.shape[1:], F32),
            VMEM(mix_weight.shape[1:], F32),
            VMEM(embed.shape, F32),
            VMEM(gate_bias.shape, F32),
            VMEM(out_weight.shape, F32),
            sems((7,)),
        ],
        aliases={17: 0, 18: 1},
        micros=2.2,
    )(
        piece_y, other_y, core_y, rest_y, partial, bias_own, bias_other, bias_far, embed,
        first_high, first_low, turn_high, turn_low, *tables, g_conv, g_mix,
    )
    return (out_fwd, out_rev, g_embed, g_conv, g_mix, g_bias, g_out)


def solution(mesh):
    in_specs = (
        P(("dp", "seq")),
        P(),
        P(),
        P(),
        P(),
        P(),
        P(),
        P(("dp", "seq"), None),
        P(("dp", "seq"), None),
    )
    out_specs = (
        P(("dp", "seq"), None),
        P(("dp", "seq"), None),
        P("dp", None),
        P("dp", None, None, None),
        P("dp", None, None),
        P("dp", None),
        P("dp", None, None),
    )
    return jax.shard_map(
        on_device, mesh=mesh, in_specs=in_specs, out_specs=out_specs, check_vma=False
    )
```

profile of v0, /device:TPU:0, one launch (start us, length us, event | category | flops | bytes accessed | tf_op | source)
XLA Modules:
  0.0 45.0 jit_solution(8620839693959288378)
XLA Ops:
  1.2 2.6 %collective-permute-start.1 = (s32[1,512]{1,0:T(1,128)}, s32[1,512]{1,0:T(1,128)S(1)}, u32[]{:S(2)}, u32[]{:S(2)}) collective-permute-start(s32[1,512]{1,0:T(1,128)} %bitcast.2), channel_id=1, source_target_pairs={{0,2},{1,3},{2,0},{3,1},{4,6},{5,7},{6,4},{7,5},{8,10},{9,11},{10,... | collective-permute-start | bytes 6152 | tf_op jit(solution)/shard_map/ppermute | solution.py:505
  3.9 1.9 %shard_map.144 = (s32[1,512]{1,0:T(1,128)S(1)}, f32[32,512]{1,0:T(8,128)S(1)}, f32[3,256,512]{2,1,0:T(8,128)S(1)}, f32[256,512]{1,0:T(8,128)S(1)}, f32[256,256]{1,0:T(8,128)S(1)}) custom-call(s32[1,512]{1,0:T(1,128)} %bitcast.4, f32[4,256]{1,0:T(4,128)} %embed.3, f32[2,3,256,512]{3,2,1,0:T(8,128)} %conv_in.3, f32[2,256,512]{2,1,0:T(8,128)} %mix_in.3, ...), custom_call_target="tpu_custom_call" | custom-call | flops 1870000000 | bytes 5100000 | tf_op jit(solution)/shard_map/pallas_call | solution.py:498
  5.8 1.2 %collective-permute-done.2.fourth = s32[1,512]{1,0:T(1,128)S(1)} collective-permute-done((s32[1,512]{1,0:T(1,128)}, s32[1,512]{1,0:T(1,128)S(1)}, u32[]{:S(2)}, u32[]{:S(2)}) %collective-permute-start.2) | collective-permute-done | bytes 2080 | tf_op jit(solution)/shard_map/ppermute | solution.py:505
  7.0 2.6 %collective-permute-start.3 = (s32[4,512]{1,0:T(4,128)S(1)}, s32[4,512]{1,0:T(4,128)S(1)}, u32[]{:S(2)}, u32[]{:S(2)}) collective-permute-start(s32[4,512]{1,0:T(4,128)S(1)} %shard_map.145.after.refs_1_), channel_id=1, source_target_pairs={{0,4},{1,5},{2,6},{3,7},{4,0},{5,1},{6,2},{7,3},{8,12},{9,13},{10,... | collective-permute-start | bytes 24584 | tf_op jit(solution)/shard_map/ppermute | solution.py:505
  9.6 2.7 %shard_map.146 = (f32[96,256]{1,0:T(8,128)S(1)}, f32[80,256]{1,0:T(8,128)S(1)}, f32[96,512]{1,0:T(8,128)S(1)}, bf16[256,512]{1,0:T(8,128)(2,1)S(1)}, bf16[256,51...) custom-call(f32[32,512]{1,0:T(8,128)S(1)} %get-tuple-element.70.afte, ...), custom_call_target="tpu_custom_call" | custom-call | flops 3300000000 | bytes 9000000 | tf_op jit(solution)/shard_map/pallas_call | solution.py:498
  12.4 2.6 %shard_map.147 = (f32[2,168,128]{2,1,0:T(8,128)S(1)}, f32[2,168,128]{2,1,0:T(8,128)S(1)}, bf16[1024,256]{1,0:T(8,128)(2,1)S(1)}, bf16[1024,256]{1,0:T(8,128)(2,1...) custom-call(s32[2]{0:T(128)S(1)} %copy-done.2, s32[4,512]{1,0:T(4,128)S(1)} %shard_map.145.after.refs_1_, ...), custom_call_target="tpu_custom_call" | custom-call | flops 2200000000 | bytes 6000000 | tf_op jit(solution)/shard_map/pallas_call | solution.py:498
  15.1 1.7 %shard_map.148 = (f32[2,240,128]{2,1,0:T(8,128)S(1)}, f32[2,240,128]{2,1,0:T(8,128)S(1)}) custom-call(bf16[2,256,512]{2,1,0:T(8,128)(2,1)S(1)} %get-tuple-element.76.hots, f32[1024,512]{1,0:T(8,128)S(1)} %get-tuple-element.83.slopes, bf16[1024,256]{1,0:T(8,128)(2,1)S(1)} %get-tuple-element.74.refs_5_.cot_high, ...), custom_call_target="tpu_custom_call" | custom-call | flops 1650000000 | bytes 4500000 | tf_op jit(solution)/shard_map/pallas_call | solution.py:498
  16.9 0.6 %collective-permute-start.6 = (f32[2,240,128]{2,1,0:T(8,128)S(1)}, f32[2,240,128]{2,1,0:T(8,128)S(1)}, u32[]{:S(2)}, u32[]{:S(2)}) collective-permute-start(f32[2,240,128]{2,1,0:T(8,128)S(1)} %get-tuple-element.87), channel_id=1, source_target_pairs={{0,1},{1,0},{2,3},{3,2},{4,5},{5,4},{6,7},{7,6},{8,9},{9,8},{10,11... | collective-permute-start | bytes 737288 | tf_op jit(solution)/shard_map/ppermute | solution.py:505
  17.4 0.7 %collective-permute-start.5 = (f32[168,128]{1,0:T(8,128)S(1)}, f32[168,128]{1,0:T(8,128)S(1)}, u32[]{:S(2)}, u32[]{:S(2)}) collective-permute-start(f32[168,128]{1,0:T(8,128)S(1)} %get-tuple-element.86), channel_id=1, source_target_pairs={{0,2},{1,3},{2,0},{3,1},{4,6},{5,7},{6,4},{7,5},{8,10},{9,11},{10,... | collective-permute-start | bytes 258056 | tf_op jit(solution)/shard_map/ppermute | solution.py:505
  18.6 1.1 %collective-permute-start.8 = (f32[240,128]{1,0:T(8,128)S(1)}, f32[240,128]{1,0:T(8,128)S(1)}, u32[]{:S(2)}, u32[]{:S(2)}) collective-permute-start(f32[240,128]{1,0:T(8,128)S(1)} %get-tuple-element.97), channel_id=1, source_target_pairs={{0,2},{1,3},{2,0},{3,1},{4,6},{5,7},{6,4},{7,5},{8,10},{9,11},{10,... | collective-permute-start | bytes 368648 | tf_op jit(solution)/shard_map/ppermute | solution.py:505
  19.6 2.8 %collective-permute-done.5.received = f32[168,128]{1,0:T(8,128)S(1)} collective-permute-done((f32[168,128]{1,0:T(8,128)S(1)}, f32[168,128]{1,0:T(8,128)S(1)}, u32[]{:S(2)}, u32[]{:S(2)}) %collective-permute-start.5) | collective-permute-done | bytes 86048 | tf_op jit(solution)/shard_map/ppermute | solution.py:505
  22.4 1.9 %collective-permute-start.7 = (f32[168,128]{1,0:T(8,128)S(1)}, f32[168,128]{1,0:T(8,128)S(1)}, u32[]{:S(2)}, u32[]{:S(2)}) collective-permute-start(f32[168,128]{1,0:T(8,128)S(1)} %shard_map.151.after.mine), channel_id=1, source_target_pairs={{0,4},{1,5},{2,6},{3,7},{4,0},{5,1},{6,2},{7,3},{8,12},{9,13},{10,... | collective-permute-start | bytes 258056 | tf_op jit(solution)/shard_map/ppermute | solution.py:505
  24.3 1.9 %shard_map.152 = (f32[512,256]{1,0:T(8,128)}, f32[512,256]{1,0:T(8,128)}) custom-call(bf16[2,256,512]{2,1,0:T(8,128)(2,1)S(1)} %get-tuple-element.76.hots, bf16[1024,256]{1,0:T(8,128)(2,1)S(1)} %get-tuple-element.77.hidden_high, bf16[1024,256]{1,0:T(8,128)(2,1)S(1)} %get-tuple-element.78.hidden_low, f32[80,256]{1,0:T(8,128)S(1)} %get-tuple-element.79.local, ...), custom_call_target="tpu_custom_call" | custom-call | flops 2200000000 | bytes 6000000 | tf_op jit(solution)/shard_map/pallas_call | solution.py:498
  26.2 1.2 %collective-permute-start.12 = (f32[240,128]{1,0:T(8,128)S(1)}, f32[240,128]{1,0:T(8,128)S(1)}, u32[]{:S(2)}, u32[]{:S(2)}) collective-permute-start(f32[240,128]{1,0:T(8,128)S(1)} %shard_map.153.after.mine), channel_id=1, source_target_pairs={{0,4},{1,5},{2,6},{3,7},{4,0},{5,1},{6,2},{7,3},{8,12},{9,13},{10,... | collective-permute-start | bytes 368648 | tf_op jit(solution)/shard_map/ppermute | solution.py:505
  27.4 1.3 %shard_map.154 = (bf16[4,512,256]{2,1,0:T(8,128)(2,1)S(1)}, bf16[4,512,256]{2,1,0:T(8,128)(2,1)S(1)}, bf16[4,512,256]{2,1,0:T(8,128)(2,1)S(1)}, bf16[4,512,256]{...) custom-call(f32[3,256,512]{2,1,0:T(8,128)S(1)} %get-tuple-element.91, ...), custom_call_target="tpu_custom_call" | custom-call | flops 1540000000 | bytes 4200000 | tf_op jit(solution)/shard_map/pallas_call | solution.py:498
  28.7 2.3 %collective-permute-done.7.theirs = f32[168,128]{1,0:T(8,128)S(1)} collective-permute-done((f32[168,128]{1,0:T(8,128)S(1)}, f32[168,128]{1,0:T(8,128)S(1)}, u32[]{:S(2)}, u32[]{:S(2)}) %collective-permute-start.7) | collective-permute-done | bytes 86048 | tf_op jit(solution)/shard_map/ppermute | solution.py:505
  31.1 3.0 %collective-permute-done.12.theirs = f32[240,128]{1,0:T(8,128)S(1)} collective-permute-done((f32[240,128]{1,0:T(8,128)S(1)}, f32[240,128]{1,0:T(8,128)S(1)}, u32[]{:S(2)}, u32[]{:S(2)}) %collective-permute-start.12) | collective-permute-done | bytes 122912 | tf_op jit(solution)/shard_map/ppermute | solution.py:505
  34.2 1.4 %collective-permute-done.9.after.piece_01 = f32[176,128]{1,0:T(8,128)S(1)} collective-permute-done((f32[176,128]{1,0:T(8,128)S(1)}, f32[176,128]{1,0:T(8,128)S(1)}, u32[]{:S(2)}, u32[]{:S(2)}) %collective-permute-start.9) | collective-permute-done | bytes 90144 | tf_op jit(solution)/shard_map/ppermute | solution.py:505
  35.6 0.6 %collective-permute-start.13 = (f32[144,128]{1,0:T(8,128)S(1)}, f32[144,128]{1,0:T(8,128)S(1)}, u32[]{:S(2)}, u32[]{:S(2)}) collective-permute-start(f32[144,128]{1,0:T(8,128)S(1)} %get-tuple-element.99), channel_id=1, source_target_pairs={{0,1},{1,0},{2,3},{3,2},{4,5},{5,4},{6,7},{7,6},{8,9},{9,8},{10,11... | collective-permute-start | bytes 221192 | tf_op jit(solution)/shard_map/ppermute | solution.py:505
  36.3 0.8 %collective-permute-done.13.refs_1_ = f32[144,128]{1,0:T(8,128)S(1)} collective-permute-done((f32[144,128]{1,0:T(8,128)S(1)}, f32[144,128]{1,0:T(8,128)S(1)}, u32[]{:S(2)}, u32[]{:S(2)}) %collective-permute-start.13) | collective-permute-done | bytes 73760 | tf_op jit(solution)/shard_map/ppermute | solution.py:505
  37.5 1.9 %shard_map.158 = (f32[2,3,256,512]{3,2,1,0:T(8,128)}, f32[2,256,512]{2,1,0:T(8,128)}, f32[2,128]{1,0:T(2,128)S(1)}, f32[96,256]{1,0:T(8,128)S(1)}) custom-call(f32[288,128]{1,0:T(8,128)S(1)} %shard_map.156.value.refs_0_, f32[144,128]{1,0:T(8,128)S(1)} %collective-permute-done.13.refs_1_, f32[144,128]{1,0:T(8,128)S(1)} %collective-permute-done.14.refs_2_, ...), custom_call_target="tpu_custom_call" | custom-call | flops 55000000 | bytes 150000 | tf_op jit(solution)/shard_map/pallas_call | solution.py:498
  40.0 1.3 %shard_map.161 = (f32[2,3,256,512]{3,2,1,0:T(8,128)}, f32[2,256,512]{2,1,0:T(8,128)}, f32[1,128]{1,0:T(1,128)S(1)}, f32[96,256]{1,0:T(8,128)S(1)}) custom-call(f32[288,128]{1,0:T(8,128)S(1)} %collective-permute-done.15.value.refs_0_, bf16[96,256]{1,0:T(8,128)(2,1)S(1)} %get-tuple-element.101.refs_3_.refs_1_, ...), custom_call_target="tpu_custom_call", output_to_operand_aliasing={{0}: (8, {}), {1}: (9, {})} | custom-call | flops 55000000 | bytes 150000 | tf_op jit(solution)/shard_map/pallas_call | solution.py:498
  41.3 1.3 %shard_map.162 = (f32[2,3,256,512]{3,2,1,0:T(8,128)}, f32[2,256,512]{2,1,0:T(8,128)}, f32[1,128]{1,0:T(1,128)S(1)}, f32[96,256]{1,0:T(8,128)S(1)}) custom-call(f32[288,128]{1,0:T(8,128)S(1)} %collective-permute-done.16.refs_0_, bf16[96,256]{1,0:T(8,128)(2,1)S(1)} %get-tuple-element.101.refs_3_.refs_1_, ...), custom_call_target="tpu_custom_call", output_to_operand_aliasing={{0}: (8, {}), {1}: (9, {})} | custom-call | flops 1320000000 | bytes 3600000 | tf_op jit(solution)/shard_map/pallas_call | solution.py:498
  42.7 2.3 %shard_map.163 = (f32[2,3,256,512]{3,2,1,0:T(8,128)}, f32[2,256,512]{2,1,0:T(8,128)}, f32[4,256]{1,0:T(4,128)}, f32[2,512]{1,0:T(2,128)}, f32[2,256,256]{2,1,0:T(8,128)}) custom-call(f32[176,128]{1,0:T(8,128)S(1)} %shard_map.155.after.piece_00, f32[176,128]{1,0:T(8,128)S(1)} %collective-permute-done.9.after.piece_01, ...), custom_call_target="tpu_custom_call", output_to_operand_aliasing={{0}: (17, {}), {1}: (18, {})} | custom-call | flops 2420000000 | bytes 6600000 | tf_op jit(solution)/shard_map/pallas_call | solution.py:498
  (36 shorter events, 2.4 us)
Async XLA Ops:
  0.6 9.0 %copy-start = (f32[2,512]{1,0:T(2,128)S(1)}, f32[2,512]{1,0:T(2,128)}, u32[]{:S(2)}) copy-start(f32[2,512]{1,0:T(2,128)} %bias.1) | copy-start | bytes 12292
  0.6 9.0 %copy-start.1 = (f32[4,256]{1,0:T(4,128)S(1)}, f32[4,256]{1,0:T(4,128)}, u32[]{:S(2)}) copy-start(f32[4,256]{1,0:T(4,128)} %embed.3) | copy-start | bytes 12292
  0.7 5.2 %collective-permute-start = (s32[1,512]{1,0:T(1,128)}, s32[1,512]{1,0:T(1,128)S(1)}, u32[]{:S(2)}, u32[]{:S(2)}) collective-permute-start(s32[1,512]{1,0:T(1,128)} %bitcast.1), channel_id=1, source_target_pairs={{0,1},{1,0},{2,3},{3,2},{4,5},{5,4},{6,7},{7,6},{8,9},{9,8},{10,11... | collective-permute-start | bytes 6152 | tf_op jit(solution)/shard_map/ppermute | solution.py:505
  1.2 4.6 %collective-permute-start.1 = (s32[1,512]{1,0:T(1,128)}, s32[1,512]{1,0:T(1,128)S(1)}, u32[]{:S(2)}, u32[]{:S(2)}) collective-permute-start(s32[1,512]{1,0:T(1,128)} %bitcast.2), channel_id=1, source_target_pairs={{0,2},{1,3},{2,0},{3,1},{4,6},{5,7},{6,4},{7,5},{8,10},{9,11},{10,... | collective-permute-start | bytes 6152 | tf_op jit(solution)/shard_map/ppermute | solution.py:505
  3.8 3.2 %collective-permute-start.2 = (s32[1,512]{1,0:T(1,128)}, s32[1,512]{1,0:T(1,128)S(1)}, u32[]{:S(2)}, u32[]{:S(2)}) collective-permute-start(s32[1,512]{1,0:T(1,128)} %bitcast.3), channel_id=1, source_target_pairs={{0,3},{1,2},{2,1},{3,0},{4,7},{5,6},{6,5},{7,4},{8,11},{9,10},{10,... | collective-permute-start | bytes 6152 | tf_op jit(solution)/shard_map/ppermute | solution.py:505
  7.0 5.3 %collective-permute-start.3 = (s32[4,512]{1,0:T(4,128)S(1)}, s32[4,512]{1,0:T(4,128)S(1)}, u32[]{:S(2)}, u32[]{:S(2)}) collective-permute-start(s32[4,512]{1,0:T(4,128)S(1)} %shard_map.145.after.refs_1_), channel_id=1, source_target_pairs={{0,4},{1,5},{2,6},{3,7},{4,0},{5,1},{6,2},{7,3},{8,12},{9,13},{10,... | collective-permute-start | bytes 24584 | tf_op jit(solution)/shard_map/ppermute | solution.py:505
  9.6 2.7 %copy-start.2 = (s32[2]{0:T(128)S(1)}, s32[2]{0:T(128)}, u32[]{:S(2)}) copy-start(s32[2]{0:T(128)} %refs_0_.1) | copy-start | bytes 28
  15.0 2.4 %collective-permute-start.4 = (f32[2,168,128]{2,1,0:T(8,128)S(1)}, f32[2,168,128]{2,1,0:T(8,128)S(1)}, u32[]{:S(2)}, u32[]{:S(2)}) collective-permute-start(f32[2,168,128]{2,1,0:T(8,128)S(1)} %get-tuple-element.82), channel_id=1, source_target_pairs={{0,1},{1,0},{2,3},{3,2},{4,5},{5,4},{6,7},{7,6},{8,9},{9,8},{10,11... | collective-permute-start | bytes 516104 | tf_op jit(solution)/shard_map/ppermute | solution.py:505
  16.9 1.7 %collective-permute-start.6 = (f32[2,240,128]{2,1,0:T(8,128)S(1)}, f32[2,240,128]{2,1,0:T(8,128)S(1)}, u32[]{:S(2)}, u32[]{:S(2)}) collective-permute-start(f32[2,240,128]{2,1,0:T(8,128)S(1)} %get-tuple-element.87), channel_id=1, source_target_pairs={{0,1},{1,0},{2,3},{3,2},{4,5},{5,4},{6,7},{7,6},{8,9},{9,8},{10,11... | collective-permute-start | bytes 737288 | tf_op jit(solution)/shard_map/ppermute | solution.py:505
  17.4 5.0 %collective-permute-start.5 = (f32[168,128]{1,0:T(8,128)S(1)}, f32[168,128]{1,0:T(8,128)S(1)}, u32[]{:S(2)}, u32[]{:S(2)}) collective-permute-start(f32[168,128]{1,0:T(8,128)S(1)} %get-tuple-element.86), channel_id=1, source_target_pairs={{0,2},{1,3},{2,0},{3,1},{4,6},{5,7},{6,4},{7,5},{8,10},{9,11},{10,... | collective-permute-start | bytes 258056 | tf_op jit(solution)/shard_map/ppermute | solution.py:505
  18.6 7.6 %collective-permute-start.8 = (f32[240,128]{1,0:T(8,128)S(1)}, f32[240,128]{1,0:T(8,128)S(1)}, u32[]{:S(2)}, u32[]{:S(2)}) collective-permute-start(f32[240,128]{1,0:T(8,128)S(1)} %get-tuple-element.97), channel_id=1, source_target_pairs={{0,2},{1,3},{2,0},{3,1},{4,6},{5,7},{6,4},{7,5},{8,10},{9,11},{10,... | collective-permute-start | bytes 368648 | tf_op jit(solution)/shard_map/ppermute | solution.py:505
  22.4 8.5 %collective-permute-start.7 = (f32[168,128]{1,0:T(8,128)S(1)}, f32[168,128]{1,0:T(8,128)S(1)}, u32[]{:S(2)}, u32[]{:S(2)}) collective-permute-start(f32[168,128]{1,0:T(8,128)S(1)} %shard_map.151.after.mine), channel_id=1, source_target_pairs={{0,4},{1,5},{2,6},{3,7},{4,0},{5,1},{6,2},{7,3},{8,12},{9,13},{10,... | collective-permute-start | bytes 258056 | tf_op jit(solution)/shard_map/ppermute | solution.py:505
  26.2 7.9 %collective-permute-start.12 = (f32[240,128]{1,0:T(8,128)S(1)}, f32[240,128]{1,0:T(8,128)S(1)}, u32[]{:S(2)}, u32[]{:S(2)}) collective-permute-start(f32[240,128]{1,0:T(8,128)S(1)} %shard_map.153.after.mine), channel_id=1, source_target_pairs={{0,4},{1,5},{2,6},{3,7},{4,0},{5,1},{6,2},{7,3},{8,12},{9,13},{10,... | collective-permute-start | bytes 368648 | tf_op jit(solution)/shard_map/ppermute | solution.py:505
  31.0 4.6 %collective-permute-start.9 = (f32[176,128]{1,0:T(8,128)S(1)}, f32[176,128]{1,0:T(8,128)S(1)}, u32[]{:S(2)}, u32[]{:S(2)}) collective-permute-start(f32[176,128]{1,0:T(8,128)S(1)} %shard_map.155.after.piece_00), channel_id=1, source_target_pairs={{0,2},{1,3},{2,0},{3,1},{4,6},{5,7},{6,4},{7,5},{8,10},{9,11},{10,... | collective-permute-start | bytes 270344 | tf_op jit(solution)/shard_map/ppermute | solution.py:505
  34.1 5.3 %collective-permute-start.15 = (f32[288,128]{1,0:T(8,128)S(1)}, f32[288,128]{1,0:T(8,128)S(1)}, u32[]{:S(2)}, u32[]{:S(2)}) collective-permute-start(f32[288,128]{1,0:T(8,128)S(1)} %shard_map.156.value.refs_0_), channel_id=1, source_target_pairs={{0,2},{1,3},{2,0},{3,1},{4,6},{5,7},{6,4},{7,5},{8,10},{9,11},{10,... | collective-permute-start | bytes 442376 | tf_op jit(solution)/shard_map/ppermute | solution.py:505
  35.6 3.8 %collective-permute-start.11 = (f32[176,128]{1,0:T(8,128)S(1)}, f32[176,128]{1,0:T(8,128)S(1)}, u32[]{:S(2)}, u32[]{:S(2)}) collective-permute-start(f32[176,128]{1,0:T(8,128)S(1)} %collective-permute-done.9.after.piece_01), channel_id=1, source_target_pairs={{0,1},{1,0},{2,3},{3,2},{4,5},{5,4},{6,7},{7,6},{8,9},{9,8},{10,11... | collective-permute-start | bytes 270344 | tf_op jit(solution)/shard_map/ppermute | solution.py:505
  35.6 1.5 %collective-permute-start.13 = (f32[144,128]{1,0:T(8,128)S(1)}, f32[144,128]{1,0:T(8,128)S(1)}, u32[]{:S(2)}, u32[]{:S(2)}) collective-permute-start(f32[144,128]{1,0:T(8,128)S(1)} %get-tuple-element.99), channel_id=1, source_target_pairs={{0,1},{1,0},{2,3},{3,2},{4,5},{5,4},{6,7},{7,6},{8,9},{9,8},{10,11... | collective-permute-start | bytes 221192 | tf_op jit(solution)/shard_map/ppermute | solution.py:505
  36.2 1.3 %collective-permute-start.14 = (f32[144,128]{1,0:T(8,128)S(1)}, f32[144,128]{1,0:T(8,128)S(1)}, u32[]{:S(2)}, u32[]{:S(2)}) collective-permute-start(f32[144,128]{1,0:T(8,128)S(1)} %get-tuple-element.100), channel_id=1, source_target_pairs={{0,1},{1,0},{2,3},{3,2},{4,5},{5,4},{6,7},{7,6},{8,9},{9,8},{10,11... | collective-permute-start | bytes 221192 | tf_op jit(solution)/shard_map/ppermute | solution.py:505
  39.4 1.9 %collective-permute-start.16 = (f32[288,128]{1,0:T(8,128)S(1)}, f32[288,128]{1,0:T(8,128)S(1)}, u32[]{:S(2)}, u32[]{:S(2)}) collective-permute-start(f32[288,128]{1,0:T(8,128)S(1)} %shard_map.160), channel_id=1, source_target_pairs={{0,1},{1,0},{2,3},{3,2},{4,5},{5,4},{6,7},{7,6},{8,9},{9,8},{10,11... | collective-permute-start | bytes 442376 | tf_op jit(solution)/shard_map/ppermute | solution.py:505
  39.7 3.0 %collective-permute-start.10 = (f32[176,128]{1,0:T(8,128)S(1)}, f32[176,128]{1,0:T(8,128)S(1)}, u32[]{:S(2)}, u32[]{:S(2)}) collective-permute-start(f32[176,128]{1,0:T(8,128)S(1)} %shard_map.155.after.piece_00), channel_id=1, source_target_pairs={{0,1},{1,0},{2,3},{3,2},{4,5},{5,4},{6,7},{7,6},{8,9},{9,8},{10,11... | collective-permute-start | bytes 270344 | tf_op jit(solution)/shard_map/ppermute | solution.py:505
where the time goes:
time: 45.1 us; the launch traced here: 45 us
  Pallas kernels  19.1 us (42%)
  starting transfers between devices  12.6 us (28%)
  waiting for transfers between devices  12.4 us (27%)
  between operations  0.85 us (2%)
    pallas_call x20, Pallas kernels, placed(): run(*[pltpu.with_memory_space_constraint(x, HBM) if space is HBM else x f...  19.1 us
    ppermute x17, starting transfers between devices, swapped(): return lax.ppermute(value, 'seq', pairs)  12.6 us
    ppermute x17, waiting for transfers between devices, swapped(): return lax.ppermute(value, 'seq', pairs)  12.4 us
  transfers between devices with their start and end apart: 17, of which 8 were waited for; matrix products, arithmetic and copies ran while one was open for 0% of the time, Pallas kernels for 32%

commit v1 on v0

--- a/solution.py
+++ b/solution.py
@@ -129,32 +129,39 @@
 
 
 def first_tables_kernel(
-    tokens_in, embed_in, conv_in, mix_in, out_in, own, taps, conv, mix, out_w, embed, sems,
+    tokens_in, embed_in, conv_in, mix_in, out_in, cot_fwd_in, cot_rev_in,
+    own, taps, conv, mix, turn, last_weight, cot_high, cot_low, grad_hidden, embed, cots, sems,
 ):
+    length = cots.shape[1]
     fetch = Fetch(sems)
     fetch.start(embed_in, embed)
     first = [fetch.start(conv_in.at[0, k], conv.at[k]) for k in range(3)]
     first += [fetch.start(mix_in.at[0], mix)]
-    rest = [fetch.start(tokens_in, own), fetch.start(out_in.at[0], out_w)]
+    last = [fetch.start(out_in.at[1], last_weight)]
+    last += [fetch.start(cot_in, cots.at[strand]) for strand, cot_in in enumerate((cot_fwd_in, cot_rev_in))]
+    rest = [fetch.start(tokens_in, own), fetch.start(out_in.at[0], turn)]
     fetch.wait(0)
     base = split(padded_base(embed))
     for k in range(4):
         fetch.wait(first[k])
         taps[k * 8 : (k + 1) * 8, :] = dot3_few(base, split(conv[k] if k < 3 else mix[...]))
+    fetch.wait(last[0])
+    weight = split(last_weight[...])
+    for strand in range(2):
+        rows = slice(strand * length, (strand + 1) * length)
+        fetch.wait(last[1 + strand])
+        cot = split(cots[strand])
+        cot_high[rows, :], cot_low[rows, :] = cot
+        grad_hidden[rows, :] = dot3(cot, weight, 1, 1)
     fetch.wait(*rest)
 
 
 def second_tables_kernel(
-    taps, embed, bias, turn, conv_in, mix_in, out_in, cot_fwd_in, cot_rev_in, after,
-    table, local, mixed_table, pre_high, pre_low, cot_high, cot_low, conv, mix, out_w,
-    cots, sems,
+    taps, embed, bias, turn, conv_in, mix_in, after, table, local, mixed_table, pre_high, pre_low, conv, mix, sems,
 ):
-    length = cots.shape[1]
     fetch = Fetch(sems)
     second = [fetch.start(conv_in.at[1, k], conv.at[k]) for k in range(3)]
     second += [fetch.start(mix_in.at[1], mix)]
-    last = [fetch.start(out_in.at[1], out_w)]
-    last += [fetch.start(cot_in, cots.at[strand]) for strand, cot_in in enumerate((cot_fwd_in, cot_rev_in))]
     hot = letter_hot()
     mixed = dot2(hot, split(taps[...])) + bias[0:1, :]
     tanh_part, sig_part = gates(mixed)
@@ -177,11 +184,6 @@
         high, low = split(local_rows(value))
         pre_high[k * LOCAL : (k + 1) * LOCAL, :] = high
         pre_low[k * LOCAL : (k + 1) * LOCAL, :] = low
-    for strand in range(2):
-        rows = slice(strand * length, (strand + 1) * length)
-        fetch.wait(last[1 + strand])
-        cot_high[rows, :], cot_low[rows, :] = split(cots[strand])
-    fetch.wait(last[0])
 
 
 def windows(parts, count):
@@ -280,13 +282,12 @@
     deal(quarters, keep, send)
 
 
-def taps_kernel(hots, slopes, cot_high, cot_low, out_w, keep, send, quarters):
+def taps_kernel(hots, slopes, grad_hidden, keep, send, quarters):
     length = hots.shape[2]
-    weight = split(out_w[...])
     total = None
     for strand in range(2):
         rows = slice(strand * length, (strand + 1) * length)
-        grad = dot3((cot_high[rows, :], cot_low[rows, :]), weight, 1, 1)
+        grad = grad_hidden[rows, :]
         part = dot2(hots[strand], split(slopes[rows, :] * jnp.concatenate([grad, grad], axis=1)))
         total = part if total is None else total + part
     for q in range(4):
@@ -382,55 +383,77 @@
             begin += rows
 
 
-def columns_kernel(own, cores, *refs):
-    pieces = [refs[:1], refs[1:3]] if own else [refs[:1]]
-    refs = refs[sum(len(piece) for piece in pieces) :]
-    level_high, level_low, partner_high, partner_low, second_high, second_low, *refs = refs
-    if not own:
-        partial, g_conv_in, g_mix_in, *refs = refs
-    g_conv_out, g_mix_out, bias, total, taps, g_conv, g_mix, out_sems = refs
+def quarter_columns(taps, column, levels, seconds, g_conv, g_mix, bias):
+    level_high, level_low, partner_high, partner_low = levels
+    level = (level_high[...], level_low[...])
+    partner = (partner_high[...], partner_low[...])
+    weights = [tuple(ref[k, pl.ds(column, 128), :] for ref in seconds) for k in range(4)]
+    pairs = [split(taps[k * CONTEXTS : (k + 1) * CONTEXTS, :]) for k in range(3)]
+    for k, pair in enumerate(pairs):
+        g_conv[k] = dot3(level, pair, 0, 0)
+    g_mix[...] = dot3(partner, pairs[1], 0, 0)
+    bias[...] = jnp.sum(taps[CONTEXTS : 2 * CONTEXTS, :], axis=0, keepdims=True)
+    part = dot2(permutation(), split(dot3_few(pairs[1], weights[3])))
+    for k, pair in enumerate(pairs):
+        part = part + dot3_few(pair, weights[k])
+    return part
+
+
+def column_of(core, chip):
     place = lax.axis_index("seq")
     low, high = place & 1, (place >> 1) & 1
-    high = high if own else 1 - high
+    return pl.multiple_of(((low ^ core) * 2 + (high ^ chip)) * 128, 128)
+
+
+def store_columns(store, column, g_conv, g_mix, g_conv_out, g_mix_out):
+    block = pl.ds(column, 128)
+    for k in range(3):
+        store.start(g_conv.at[k], g_conv_out.at[1, k, :, block])
+    store.start(g_mix, g_mix_out.at[1, :, block])
+
+
+def own_columns_kernel(own_piece, core_first, core_second, *refs):
+    levels, seconds, refs = refs[:4], refs[4:6], refs[6:]
+    g_conv_out, g_mix_out, bias, total, taps, g_conv, g_mix, out_sems = refs
     store = Fetch(out_sems)
-    level = (level_high[...], level_low[...])
-    partner = (partner_high[...], partner_low[...])
-    grad_level = None if own else partial[...]
-    for at, core in enumerate(cores):
-        begin = 0
-        for piece in pieces[at]:
-            rows = piece.shape[0]
-            taps[begin : begin + rows, :] = piece[...]
-            begin += rows
-        column = pl.multiple_of(((low ^ core) * 2 + high) * 128, 128)
-        block = pl.ds(column, 128)
-
-        def weight(k):
-            return second_high[k, block, :], second_low[k, block, :]
-
-        pairs = [split(taps[k * CONTEXTS : (k + 1) * CONTEXTS, :]) for k in range(3)]
-        for k, pair in enumerate(pairs):
-            g_conv[at, k] = dot3(level, pair, 0, 0)
-            store.start(g_conv.at[at, k], g_conv_out.at[1, k, :, block])
-        g_mix[at] = dot3(partner, pairs[1], 0, 0)
-        store.start(g_mix.at[at], g_mix_out.at[1, :, block])
-        bias[at : at + 1, :] = jnp.sum(taps[CONTEXTS : 2 * CONTEXTS, :], axis=0, keepdims=True)
-        part = dot2(permutation(), split(dot3_few(pairs[1], weight(3))))
-        for k, pair in enumerate(pairs):
-            part = part + dot3_few(pair, weight(k))
+    half = core_first.shape[0]
+    taps[0] = own_piece[...]
+    taps[1, :half, :] = core_first[...]
+    taps[1, half:, :] = core_second[...]
+    grad_level = None
+    for core in range(2):
+        column = column_of(core, 0)
+        part = quarter_columns(
+            taps.at[core], column, levels, seconds, g_conv.at[core], g_mix.at[core], bias.at[core : core + 1]
+        )
+        store_columns(store, column, g_conv.at[core], g_mix.at[core], g_conv_out, g_mix_out)
         grad_level = part if grad_level is None else grad_level + part
     total[...] = grad_level
     store.wait(*range(len(store.copies)))
 
 
+def other_columns_kernel(piece, *refs):
+    levels, seconds, refs = refs[:4], refs[4:6], refs[6:]
+    partial, g_conv_in, g_mix_in, g_conv_out, g_mix_out, bias, total, g_conv, g_mix, out_sems = refs
+    store = Fetch(out_sems)
+    column = column_of(0, 1)
+    total[...] = partial[...] + quarter_columns(piece, column, levels, seconds, g_conv, g_mix, bias)
+    store_columns(store, column, g_conv, g_mix, g_conv_out, g_mix_out)
+    store.wait(*range(len(store.copies)))
+
+
 def first_layer_kernel(
-    piece_00, piece_01, piece_10, piece_11, partial, bias_own, bias_other, bias_far, embed,
+    far_piece, level_high, level_low, partner_high, partner_low, second_high, second_low,
+    piece_00, piece_01, piece_10, piece_11, partial, bias_own, bias_other, embed,
     first_high, first_low, turn_high, turn_low, hidden_high, hidden_low, slopes, hot_in,
     g_conv_in, g_mix_in, g_conv_out, g_mix_out, g_embed_out, g_bias_out, g_out_out,
-    quarters, bias_rows, g_conv, g_mix, g_embed, g_bias, g_out, out_sems,
+    quarters, bias_rows, bias_far, far_conv, far_mix, g_conv, g_mix, g_embed, g_bias, g_out, out_sems,
 ):
     channels = embed.shape[1]
     store = Fetch(out_sems)
+    column = column_of(1, 1)
+    levels = (level_high, level_low, partner_high, partner_low)
+    far_part = quarter_columns(far_piece, column, levels, (second_high, second_low), far_conv, far_mix, bias_far)
     gather_quarters([(piece,) for piece in (piece_00, piece_01, piece_10, piece_11)], quarters)
     side = channels // 4
     rest = []
@@ -438,9 +461,10 @@
         begin += 2 * side
         halves = [[quarters[2 * h + i, begin : begin + rows, :] for i in range(2)] for h in range(2)]
         rest.append(jnp.concatenate([jnp.concatenate(x, axis=0) for x in halves], axis=1))
-    grad_level = split(partial[...] + jnp.concatenate(rest, axis=0))
+    grad_level = split(partial[...] + far_part + jnp.concatenate(rest, axis=0))
     grad_hidden = dot3_few(grad_level, (turn_high[...], turn_low[...]))
     grad_mixed = slopes[...] * jnp.concatenate([grad_hidden, grad_hidden], axis=1)
+    store_columns(store, column, far_conv, far_mix, g_conv_out, g_mix_out)
     hot = hot_in[...]
     by_letter = dot2(hot, split(grad_mixed), 0, 0)
     base = split(padded_base(embed))
@@ -526,28 +550,28 @@
     row = tokens.reshape(1, length)
     near = [swapped(row, mask) for mask in (1, 2, 3)]
     layer_weights = [(conv_weight.shape[1:], F32, VMEM), (mix_weight.shape[1:], F32, VMEM)]
-    own, taps, first_conv, first_mix, turn = call(
+    own, taps, first_conv, first_mix, turn, last_weight, cot_high, cot_low, grad_hidden = call(
         first_tables_kernel,
-        [HBM] * 5,
-        [(row.shape, row.dtype, VMEM), ((32, wide), F32, VMEM), *layer_weights, (square, F32, VMEM)],
-        [VMEM(embed.shape, F32), sems((7,))],
-        micros=1.7,
-    )(row, embed, conv_weight, mix_weight, out_weight)
+        [HBM] * 7,
+        [(row.shape, row.dtype, VMEM), ((32, wide), F32, VMEM), *layer_weights]
+        + [(square, F32, VMEM)] * 2
+        + [((2 * length, channels), BF16, VMEM)] * 2
+        + [((2 * length, channels), F32, VMEM)],
+        [VMEM(embed.shape, F32), VMEM((2, length, channels), F32), sems((10,))],
+        micros=2.7,
+    )(row, embed, conv_weight, mix_weight, out_weight, cot_fwd, cot_rev)
     known = call(join_four_kernel, [VMEM] * 5, [((4, length), row.dtype, VMEM)])(own, *near, taps)[0]
     parts = [known, swapped(known, 4)]
     deep = -(-TAPS // 128) * 128
-    (table, local, mixed_table, pre_high, pre_low, cot_high, cot_low,
-     second_conv, second_mix, last_weight) = call(
+    table, local, mixed_table, pre_high, pre_low, second_conv, second_mix = call(
         second_tables_kernel,
-        [VMEM] * 4 + [HBM] * 5 + [VMEM],
+        [VMEM] * 4 + [HBM] * 2 + [VMEM],
         [((CONTEXTS, channels), F32, VMEM), ((LOCAL, channels), F32, VMEM), ((CONTEXTS, wide), F32, VMEM)]
         + [((deep, wide), BF16, VMEM)] * 2
-        + [((2 * length, channels), BF16, VMEM)] * 2
-        + layer_weights
-        + [(square, F32, VMEM)],
-        [VMEM((2, length, channels), F32), sems((7,))],
-        micros=3.0,
-    )(taps, embed, gate_bias, turn, conv_weight, mix_weight, out_weight, cot_fwd, cot_rev, known)
+        + layer_weights,
+        [sems((4,))],
+        micros=2.5,
+    )(taps, embed, gate_bias, turn, conv_weight, mix_weight, known)
     mask = 8
     while mask < count:
         known = jnp.concatenate([known, parts[-1]], axis=0)
@@ -566,11 +590,11 @@
     )(dilations, *parts, pre_high, pre_low, cot_high, cot_low)
     keep_x, send_x = call(
         taps_kernel,
-        [VMEM] * 5,
+        [VMEM] * 3,
         [((2, rows_x, 128), F32, VMEM)] * 2,
         [VMEM((4, rows_x, 128), F32)],
         micros=1.5,
-    )(hots, slopes, cot_high, cot_low, last_weight)
+    )(hots, slopes, grad_hidden)
 
     def halved(keep, received, after):
         outs = [(keep.shape[1:], F32, VMEM)] * 2
@@ -614,58 +638,56 @@
     other_y = swapped(piece_y, 2)
     core_x = [swapped(x, 1) for x in touched(piece_x, other_y, 2)]
 
-    def columns(own, cores, pieces, before=(), micros=0.05):
-        inner = len(pieces) + 6
-        return call(
-            lambda *refs: columns_kernel(own, cores, *refs),
-            [VMEM] * inner + ([VMEM] + [HBM] * 2 if before else []),
-            [
-                (conv_weight.shape, F32, HBM),
-                (mix_weight.shape, F32, HBM),
-                ((len(cores), 128), F32, VMEM),
-                ((CONTEXTS, channels), F32, VMEM),
-            ],
-            [
-                VMEM((merged_x, 128), F32),
-                VMEM((len(cores), 3, channels, 128), F32),
-                VMEM((len(cores), channels, 128), F32),
-                sems((4 * len(cores),)),
-            ],
-            aliases={inner + 1: 0, inner + 2: 1} if before else None,
-            micros=micros,
-        )(*pieces, *levels, second_high, second_low, *before)
-
     core_y, far_y = swapped(piece_y, 1), swapped(other_y, 1)
-    g_conv, g_mix, bias_own, partial = columns(True, (0, 1), (piece_x, *core_x))
+    shared = (*levels, second_high, second_low)
+    large = [(conv_weight.shape, F32, HBM), (mix_weight.shape, F32, HBM)]
+    level_out = ((CONTEXTS, channels), F32, VMEM)
+    quarter_conv, quarter_mix = (3, channels, 128), (channels, 128)
+    g_conv, g_mix, bias_own, partial = call(
+        own_columns_kernel,
+        [VMEM] * 9,
+        [*large, ((2, 128), F32, VMEM), level_out],
+        [
+            VMEM((2, merged_x, 128), F32),
+            VMEM((2, *quarter_conv), F32),
+            VMEM((2, *quarter_mix), F32),
+            sems((8,)),
+        ],
+        micros=0.05,
+    )(piece_x, *core_x, *shared)
     other_x = swapped(piece_x, 2)
     rest_y = touched(far_y, partial)[0]
-    far_x = [swapped(x, 1) for x in touched(other_x, rest_y)]
-    g_conv, g_mix, bias_other, partial = columns(False, (0,), (other_x,), (partial, g_conv, g_mix))
-    g_conv, g_mix, bias_far, partial = columns(False, (1,), far_x, (partial, g_conv, g_mix), micros=1.2)
+    core_y = touched(core_y, rest_y)[0]
+    far_x = swapped(touched(other_x, core_y)[0], 1)
+    g_conv, g_mix, bias_other, partial = call(
+        other_columns_kernel,
+        [VMEM] * 8 + [HBM] * 2,
+        [*large, ((1, 128), F32, VMEM), level_out],
+        [VMEM(quarter_conv, F32), VMEM(quarter_mix, F32), sems((4,))],
+        aliases={8: 0, 9: 1},
+        micros=0.05,
+    )(other_x, *shared, partial, g_conv, g_mix)
     g_conv, g_mix, g_embed, g_bias, g_out = call(
         first_layer_kernel,
-        [VMEM] * 17 + [HBM] * 2,
-        [
-            (conv_weight.shape, F32, HBM),
-            (mix_weight.shape, F32, HBM),
-            (embed.shape, F32, HBM),
-            (gate_bias.shape, F32, HBM),
-            (out_weight.shape, F32, HBM),
-        ],
+        [VMEM] * 23 + [HBM] * 2,
+        [*large] + [(shape, F32, HBM) for shape in (embed.shape, gate_bias.shape, out_weight.shape)],
         [
             VMEM((4, merged_y, 128), F32),
             VMEM((4, 1, 128), F32),
+            VMEM((1, 128), F32),
+            VMEM(quarter_conv, F32),
+            VMEM(quarter_mix, F32),
             VMEM(conv_weight.shape[1:], F32),
             VMEM(mix_weight.shape[1:], F32),
             VMEM(embed.shape, F32),
             VMEM(gate_bias.shape, F32),
             VMEM(out_weight.shape, F32),
-            sems((7,)),
+            sems((11,)),
         ],
-        aliases={17: 0, 18: 1},
-        micros=2.2,
+        aliases={23: 0, 24: 1},
+        micros=2.7,
     )(
-        piece_y, other_y, core_y, rest_y, partial, bias_own, bias_other, bias_far, embed,
+        far_x, *shared, piece_y, other_y, core_y, rest_y, partial, bias_own, bias_other, embed,
         first_high, first_low, turn_high, turn_low, *tables, g_conv, g_mix,
     )
     return (out_fwd, out_rev, g_embed, g_conv, g_mix, g_bias, g_out)

time: 45.1 us -> 44.1 us (0.978); the launches traced: 45 us -> 43.5 us
  waiting for transfers between devices: 12.4 us -> 6.18 us
  starting transfers between devices: 12.6 us -> 17.9 us
  Pallas kernels: 19.1 us -> 18.5 us
    ppermute x17, waiting for transfers between devices: 12.4 us -> 6.18 us  [swapped(): return lax.ppermute(value, 'seq', pairs)]
    ppermute x17, starting transfers between devices: 12.6 us -> 17.9 us  [swapped(): return lax.ppermute(value, 'seq', pairs)]
    pallas_call x20, Pallas kernels: 19.1 us -> 18.5 us  [placed(): run(*[pltpu.with_memory_space_constraint(x, HBM) if space is HBM else x f...]
  transfers between devices with their start and end apart: 17 -> 17, of which waited for: 8 -> 5; matrix products, arithmetic and copies ran while one was open for 0% -> 0% of each run, Pallas kernels for 32% -> 29%
where the time goes in v1:
time: 44.1 us; the launch traced here: 43.5 us
  Pallas kernels  18.5 us (42%)
  starting transfers between devices  17.9 us (41%)
  waiting for transfers between devices  6.18 us (14%)
  between operations  0.87 us (2%)
    pallas_call x20, Pallas kernels, placed(): run(*[pltpu.with_memory_space_constraint(x, HBM) if space is HBM else x f...  18.5 us
    ppermute x17, starting transfers between devices, swapped(): return lax.ppermute(value, 'seq', pairs)  17.9 us
    ppermute x17, waiting for transfers between devices, swapped(): return lax.ppermute(value, 'seq', pairs)  6.18 us
  transfers between devices with their start and end apart: 17, of which 5 were waited for; matrix products, arithmetic and copies ran while one was open for 0% of the time, Pallas kernels for 29%

profile of v1, /device:TPU:0, one launch (start us, length us, event | category | flops | bytes accessed | tf_op | source)
XLA Modules:
  0.0 43.5 jit_solution(17457860485159432486)
XLA Ops:
  0.7 2.5 %collective-permute-start.2 = (s32[1,512]{1,0:T(1,128)}, s32[1,512]{1,0:T(1,128)S(1)}, u32[]{:S(2)}, u32[]{:S(2)}) collective-permute-start(s32[1,512]{1,0:T(1,128)} %bitcast.1), channel_id=1, source_target_pairs={{0,3},{1,2},{2,1},{3,0},{4,7},{5,6},{6,5},{7,4},{8,11},{9,10},{10,... | collective-permute-start | bytes 6152 | tf_op jit(solution)/shard_map/ppermute | solution.py:529
  3.2 0.6 %collective-permute-start.1 = (s32[1,512]{1,0:T(1,128)}, s32[1,512]{1,0:T(1,128)S(1)}, u32[]{:S(2)}, u32[]{:S(2)}) collective-permute-start(s32[1,512]{1,0:T(1,128)} %bitcast.2), channel_id=1, source_target_pairs={{0,2},{1,3},{2,0},{3,1},{4,6},{5,7},{6,4},{7,5},{8,10},{9,11},{10,... | collective-permute-start | bytes 6152 | tf_op jit(solution)/shard_map/ppermute | solution.py:529
  3.9 3.2 %shard_map.144 = (s32[1,512]{1,0:T(1,128)S(1)}, f32[32,512]{1,0:T(8,128)S(1)}, f32[3,256,512]{2,1,0:T(8,128)S(1)}, f32[256,512]{1,0:T(8,128)S(1)}, f32[256,256]{...) custom-call(s32[1,512]{1,0:T(1,128)} %bitcast.4, ...), custom_call_target="tpu_custom_call" | custom-call | flops 2969999872 | bytes 8100000 | tf_op jit(solution)/shard_map/pallas_call | solution.py:522
  7.1 2.8 %collective-permute-start.3 = (s32[4,512]{1,0:T(4,128)S(1)}, s32[4,512]{1,0:T(4,128)S(1)}, u32[]{:S(2)}, u32[]{:S(2)}) collective-permute-start(s32[4,512]{1,0:T(4,128)S(1)} %shard_map.145.after.refs_1_), channel_id=1, source_target_pairs={{0,4},{1,5},{2,6},{3,7},{4,0},{5,1},{6,2},{7,3},{8,12},{9,13},{10,... | collective-permute-start | bytes 24584 | tf_op jit(solution)/shard_map/ppermute | solution.py:529
  9.9 2.4 %shard_map.146 = (f32[96,256]{1,0:T(8,128)S(1)}, f32[80,256]{1,0:T(8,128)S(1)}, f32[96,512]{1,0:T(8,128)S(1)}, bf16[256,512]{1,0:T(8,128)(2,1)S(1)}, bf16[256,51...) custom-call(f32[32,512]{1,0:T(8,128)S(1)} %get-tuple-element.67.after.taps, ...), custom_call_target="tpu_custom_call" | custom-call | flops 2750000128 | bytes 7500000 | tf_op jit(solution)/shard_map/pallas_call | solution.py:522
  12.3 2.6 %shard_map.147 = (f32[2,168,128]{2,1,0:T(8,128)S(1)}, f32[2,168,128]{2,1,0:T(8,128)S(1)}, bf16[1024,256]{1,0:T(8,128)(2,1)S(1)}, bf16[1024,256]{1,0:T(8,128)(2,1...) custom-call(s32[2]{0:T(128)S(1)} %copy-done.2, s32[4,512]{1,0:T(4,128)S(1)} %shard_map.145.after.refs_1_, ...), custom_call_target="tpu_custom_call" | custom-call | flops 2200000000 | bytes 6000000 | tf_op jit(solution)/shard_map/pallas_call | solution.py:522
  15.0 0.9 %shard_map.148 = (f32[2,240,128]{2,1,0:T(8,128)S(1)}, f32[2,240,128]{2,1,0:T(8,128)S(1)}) custom-call(bf16[2,256,512]{2,1,0:T(8,128)(2,1)S(1)} %get-tuple-element.73.hots, f32[1024,512]{1,0:T(8,128)S(1)} %get-tuple-element.80.slopes, f32[1024,256]{1,0:T(8,128)S(1)} %get-tuple-element.81.grad_hidden), custom_call_target="tpu_custom_call" | custom-call | flops 1650000000 | bytes 4500000 | tf_op jit(solution)/shard_map/pallas_call | solution.py:522
  15.9 0.6 %collective-permute-start.6 = (f32[2,240,128]{2,1,0:T(8,128)S(1)}, f32[2,240,128]{2,1,0:T(8,128)S(1)}, u32[]{:S(2)}, u32[]{:S(2)}) collective-permute-start(f32[2,240,128]{2,1,0:T(8,128)S(1)} %get-tuple-element.85), channel_id=1, source_target_pairs={{0,1},{1,0},{2,3},{3,2},{4,5},{5,4},{6,7},{7,6},{8,9},{9,8},{10,11... | collective-permute-start | bytes 737288 | tf_op jit(solution)/shard_map/ppermute | solution.py:529
  16.5 1.6 %collective-permute-start.5 = (f32[168,128]{1,0:T(8,128)S(1)}, f32[168,128]{1,0:T(8,128)S(1)}, u32[]{:S(2)}, u32[]{:S(2)}) collective-permute-start(f32[168,128]{1,0:T(8,128)S(1)} %get-tuple-element.84), channel_id=1, source_target_pairs={{0,2},{1,3},{2,0},{3,1},{4,6},{5,7},{6,4},{7,5},{8,10},{9,11},{10,... | collective-permute-start | bytes 258056 | tf_op jit(solution)/shard_map/ppermute | solution.py:529
  18.1 1.1 %collective-permute-start.7 = (f32[240,128]{1,0:T(8,128)S(1)}, f32[240,128]{1,0:T(8,128)S(1)}, u32[]{:S(2)}, u32[]{:S(2)}) collective-permute-start(f32[240,128]{1,0:T(8,128)S(1)} %get-tuple-element.89), channel_id=1, source_target_pairs={{0,2},{1,3},{2,0},{3,1},{4,6},{5,7},{6,4},{7,5},{8,10},{9,11},{10,... | collective-permute-start | bytes 368648 | tf_op jit(solution)/shard_map/ppermute | solution.py:529
  19.3 2.3 %collective-permute-done.5.received = f32[168,128]{1,0:T(8,128)S(1)} collective-permute-done((f32[168,128]{1,0:T(8,128)S(1)}, f32[168,128]{1,0:T(8,128)S(1)}, u32[]{:S(2)}, u32[]{:S(2)}) %collective-permute-start.5) | collective-permute-done | bytes 86048 | tf_op jit(solution)/shard_map/ppermute | solution.py:529
  21.6 2.2 %collective-permute-start.9 = (f32[168,128]{1,0:T(8,128)S(1)}, f32[168,128]{1,0:T(8,128)S(1)}, u32[]{:S(2)}, u32[]{:S(2)}) collective-permute-start(f32[168,128]{1,0:T(8,128)S(1)} %shard_map.151.after.mine), channel_id=1, source_target_pairs={{0,4},{1,5},{2,6},{3,7},{4,0},{5,1},{6,2},{7,3},{8,12},{9,13},{10,... | collective-permute-start | bytes 258056 | tf_op jit(solution)/shard_map/ppermute | solution.py:529
  23.8 1.9 %shard_map.152 = (f32[512,256]{1,0:T(8,128)}, f32[512,256]{1,0:T(8,128)}) custom-call(bf16[2,256,512]{2,1,0:T(8,128)(2,1)S(1)} %get-tuple-element.73.hots, bf16[1024,256]{1,0:T(8,128)(2,1)S(1)} %get-tuple-element.74.hidden_high, bf16[1024,256]{1,0:T(8,128)(2,1)S(1)} %get-tuple-element.75.hidden_low, f32[80,256]{1,0:T(8,128)S(1)} %get-tuple-element.76.local, ...), custom_call_target="tpu_custom_call" | custom-call | flops 2200000000 | bytes 6000000 | tf_op jit(solution)/shard_map/pallas_call | solution.py:522
  25.7 0.8 %collective-permute-start.8 = (f32[240,128]{1,0:T(8,128)S(1)}, f32[240,128]{1,0:T(8,128)S(1)}, u32[]{:S(2)}, u32[]{:S(2)}) collective-permute-start(f32[240,128]{1,0:T(8,128)S(1)} %shard_map.153.after.mine), channel_id=1, source_target_pairs={{0,4},{1,5},{2,6},{3,7},{4,0},{5,1},{6,2},{7,3},{8,12},{9,13},{10,... | collective-permute-start | bytes 368648 | tf_op jit(solution)/shard_map/ppermute | solution.py:529
  26.5 1.2 %shard_map.154 = (bf16[4,512,256]{2,1,0:T(8,128)(2,1)S(1)}, bf16[4,512,256]{2,1,0:T(8,128)(2,1)S(1)}, bf16[4,512,256]{2,1,0:T(8,128)(2,1)S(1)}, bf16[4,512,256]{...) custom-call(f32[3,256,512]{2,1,0:T(8,128)S(1)} %get-tuple-element.90, ...), custom_call_target="tpu_custom_call" | custom-call | flops 1540000000 | bytes 4200000 | tf_op jit(solution)/shard_map/pallas_call | solution.py:522
  27.8 3.8 %collective-permute-start.12 = (f32[176,128]{1,0:T(8,128)S(1)}, f32[176,128]{1,0:T(8,128)S(1)}, u32[]{:S(2)}, u32[]{:S(2)}) collective-permute-start(f32[176,128]{1,0:T(8,128)S(1)} %shard_map.155.after.piece_00), channel_id=1, source_target_pairs={{0,2},{1,3},{2,0},{3,1},{4,6},{5,7},{6,4},{7,5},{8,10},{9,11},{10,... | collective-permute-start | bytes 270344 | tf_op jit(solution)/shard_map/ppermute | solution.py:529
  31.6 1.7 %collective-permute-done.8.theirs = f32[240,128]{1,0:T(8,128)S(1)} collective-permute-done((f32[240,128]{1,0:T(8,128)S(1)}, f32[240,128]{1,0:T(8,128)S(1)}, u32[]{:S(2)}, u32[]{:S(2)}) %collective-permute-start.8) | collective-permute-done | bytes 122912 | tf_op jit(solution)/shard_map/ppermute | solution.py:529
  33.5 1.2 %collective-permute-done.12.after.piece_01 = f32[176,128]{1,0:T(8,128)S(1)} collective-permute-done((f32[176,128]{1,0:T(8,128)S(1)}, f32[176,128]{1,0:T(8,128)S(1)}, u32[]{:S(2)}, u32[]{:S(2)}) %collective-permute-start.12) | collective-permute-done | bytes 90144 | tf_op jit(solution)/shard_map/ppermute | solution.py:529
  34.7 0.5 %collective-permute-start.11 = (f32[176,128]{1,0:T(8,128)S(1)}, f32[176,128]{1,0:T(8,128)S(1)}, u32[]{:S(2)}, u32[]{:S(2)}) collective-permute-start(f32[176,128]{1,0:T(8,128)S(1)} %shard_map.155.after.piece_00), channel_id=1, source_target_pairs={{0,1},{1,0},{2,3},{3,2},{4,5},{5,4},{6,7},{7,6},{8,9},{9,8},{10,11... | collective-permute-start | bytes 270344 | tf_op jit(solution)/shard_map/ppermute | solution.py:529
  35.3 0.5 %collective-permute-start.15 = (f32[144,128]{1,0:T(8,128)S(1)}, f32[144,128]{1,0:T(8,128)S(1)}, u32[]{:S(2)}, u32[]{:S(2)}) collective-permute-start(f32[144,128]{1,0:T(8,128)S(1)} %get-tuple-element.98), channel_id=1, source_target_pairs={{0,1},{1,0},{2,3},{3,2},{4,5},{5,4},{6,7},{7,6},{8,9},{9,8},{10,11... | collective-permute-start | bytes 221192 | tf_op jit(solution)/shard_map/ppermute | solution.py:529
  35.8 0.8 %collective-permute-done.14.core_first = f32[144,128]{1,0:T(8,128)S(1)} collective-permute-done((f32[144,128]{1,0:T(8,128)S(1)}, f32[144,128]{1,0:T(8,128)S(1)}, u32[]{:S(2)}, u32[]{:S(2)}) %collective-permute-start.14) | collective-permute-done | bytes 73760 | tf_op jit(solution)/shard_map/ppermute | solution.py:529
  36.7 1.7 %shard_map.158 = (f32[2,3,256,512]{3,2,1,0:T(8,128)}, f32[2,256,512]{2,1,0:T(8,128)}, f32[2,128]{1,0:T(2,128)S(1)}, f32[96,256]{1,0:T(8,128)S(1)}) custom-call(f32[288,128]{1,0:T(8,128)S(1)} %shard_map.156.value.own_piece, f32[144,128]{1,0:T(8,128)S(1)} %collective-permute-done.14.core_first, f32[144,128]{1,0:T(8,128)S(1)} %collective-permute-done.15.core_second, ...), custom_call_target="tpu_custom_call" | custom-call | flops 55000000 | bytes 150000 | tf_op jit(solution)/shard_map/pallas_call | solution.py:522
  39.0 1.3 %shard_map.162 = (f32[2,3,256,512]{3,2,1,0:T(8,128)}, f32[2,256,512]{2,1,0:T(8,128)}, f32[1,128]{1,0:T(1,128)S(1)}, f32[96,256]{1,0:T(8,128)S(1)}) custom-call(f32[288,128]{1,0:T(8,128)S(1)} %collective-permute-done.10.value.piece, bf16[96,256]{1,0:T(8,128)(2,1)S(1)} %get-tuple-element.99.refs_0_.level_high, ...), custom_call_target="tpu_custom_call", output_to_operand_aliasing={{0}: (8, {}), {1}: (9, {})} | custom-call | flops 55000000 | bytes 150000 | tf_op jit(solution)/shard_map/pallas_call | solution.py:522
  40.3 3.1 %shard_map.163 = (f32[2,3,256,512]{3,2,1,0:T(8,128)}, f32[2,256,512]{2,1,0:T(8,128)}, f32[4,256]{1,0:T(4,128)}, f32[2,512]{1,0:T(2,128)}, f32[2,256,256]{2,1,0:T(8,128)}) custom-call(f32[288,128]{1,0:T(8,128)S(1)} %collective-permute-done.16.far_piece, ...), custom_call_target="tpu_custom_call", output_to_operand_aliasing={{0}: (23, {}), {1}: (24, {})} | custom-call | flops 2969999872 | bytes 8100000 | tf_op jit(solution)/shard_map/pallas_call | solution.py:522
  (36 shorter events, 1.2 us)
Async XLA Ops:
  0.6 9.3 %copy-start = (f32[2,512]{1,0:T(2,128)S(1)}, f32[2,512]{1,0:T(2,128)}, u32[]{:S(2)}) copy-start(f32[2,512]{1,0:T(2,128)} %bias.1) | copy-start | bytes 12292
  0.6 9.3 %copy-start.1 = (f32[4,256]{1,0:T(4,128)S(1)}, f32[4,256]{1,0:T(4,128)}, u32[]{:S(2)}) copy-start(f32[4,256]{1,0:T(4,128)} %embed.3) | copy-start | bytes 12292
  0.7 6.4 %collective-permute-start.2 = (s32[1,512]{1,0:T(1,128)}, s32[1,512]{1,0:T(1,128)S(1)}, u32[]{:S(2)}, u32[]{:S(2)}) collective-permute-start(s32[1,512]{1,0:T(1,128)} %bitcast.1), channel_id=1, source_target_pairs={{0,3},{1,2},{2,1},{3,0},{4,7},{5,6},{6,5},{7,4},{8,11},{9,10},{10,... | collective-permute-start | bytes 6152 | tf_op jit(solution)/shard_map/ppermute | solution.py:529
  3.2 3.9 %collective-permute-start.1 = (s32[1,512]{1,0:T(1,128)}, s32[1,512]{1,0:T(1,128)S(1)}, u32[]{:S(2)}, u32[]{:S(2)}) collective-permute-start(s32[1,512]{1,0:T(1,128)} %bitcast.2), channel_id=1, source_target_pairs={{0,2},{1,3},{2,0},{3,1},{4,6},{5,7},{6,4},{7,5},{8,10},{9,11},{10,... | collective-permute-start | bytes 6152 | tf_op jit(solution)/shard_map/ppermute | solution.py:529
  3.8 3.2 %collective-permute-start = (s32[1,512]{1,0:T(1,128)}, s32[1,512]{1,0:T(1,128)S(1)}, u32[]{:S(2)}, u32[]{:S(2)}) collective-permute-start(s32[1,512]{1,0:T(1,128)} %bitcast.3), channel_id=1, source_target_pairs={{0,1},{1,0},{2,3},{3,2},{4,5},{5,4},{6,7},{7,6},{8,9},{9,8},{10,11... | collective-permute-start | bytes 6152 | tf_op jit(solution)/shard_map/ppermute | solution.py:529
  7.1 5.2 %collective-permute-start.3 = (s32[4,512]{1,0:T(4,128)S(1)}, s32[4,512]{1,0:T(4,128)S(1)}, u32[]{:S(2)}, u32[]{:S(2)}) collective-permute-start(s32[4,512]{1,0:T(4,128)S(1)} %shard_map.145.after.refs_1_), channel_id=1, source_target_pairs={{0,4},{1,5},{2,6},{3,7},{4,0},{5,1},{6,2},{7,3},{8,12},{9,13},{10,... | collective-permute-start | bytes 24584 | tf_op jit(solution)/shard_map/ppermute | solution.py:529
  9.9 2.4 %copy-start.2 = (s32[2]{0:T(128)S(1)}, s32[2]{0:T(128)}, u32[]{:S(2)}) copy-start(s32[2]{0:T(128)} %refs_0_.1) | copy-start | bytes 28
  14.9 1.5 %collective-permute-start.4 = (f32[2,168,128]{2,1,0:T(8,128)S(1)}, f32[2,168,128]{2,1,0:T(8,128)S(1)}, u32[]{:S(2)}, u32[]{:S(2)}) collective-permute-start(f32[2,168,128]{2,1,0:T(8,128)S(1)} %get-tuple-element.79), channel_id=1, source_target_pairs={{0,1},{1,0},{2,3},{3,2},{4,5},{5,4},{6,7},{7,6},{8,9},{9,8},{10,11... | collective-permute-start | bytes 516104 | tf_op jit(solution)/shard_map/ppermute | solution.py:529
  15.9 2.2 %collective-permute-start.6 = (f32[2,240,128]{2,1,0:T(8,128)S(1)}, f32[2,240,128]{2,1,0:T(8,128)S(1)}, u32[]{:S(2)}, u32[]{:S(2)}) collective-permute-start(f32[2,240,128]{2,1,0:T(8,128)S(1)} %get-tuple-element.85), channel_id=1, source_target_pairs={{0,1},{1,0},{2,3},{3,2},{4,5},{5,4},{6,7},{7,6},{8,9},{9,8},{10,11... | collective-permute-start | bytes 737288 | tf_op jit(solution)/shard_map/ppermute | solution.py:529
  16.5 5.1 %collective-permute-start.5 = (f32[168,128]{1,0:T(8,128)S(1)}, f32[168,128]{1,0:T(8,128)S(1)}, u32[]{:S(2)}, u32[]{:S(2)}) collective-permute-start(f32[168,128]{1,0:T(8,128)S(1)} %get-tuple-element.84), channel_id=1, source_target_pairs={{0,2},{1,3},{2,0},{3,1},{4,6},{5,7},{6,4},{7,5},{8,10},{9,11},{10,... | collective-permute-start | bytes 258056 | tf_op jit(solution)/shard_map/ppermute | solution.py:529
  18.1 7.5 %collective-permute-start.7 = (f32[240,128]{1,0:T(8,128)S(1)}, f32[240,128]{1,0:T(8,128)S(1)}, u32[]{:S(2)}, u32[]{:S(2)}) collective-permute-start(f32[240,128]{1,0:T(8,128)S(1)} %get-tuple-element.89), channel_id=1, source_target_pairs={{0,2},{1,3},{2,0},{3,1},{4,6},{5,7},{6,4},{7,5},{8,10},{9,11},{10,... | collective-permute-start | bytes 368648 | tf_op jit(solution)/shard_map/ppermute | solution.py:529
  21.6 6.2 %collective-permute-start.9 = (f32[168,128]{1,0:T(8,128)S(1)}, f32[168,128]{1,0:T(8,128)S(1)}, u32[]{:S(2)}, u32[]{:S(2)}) collective-permute-start(f32[168,128]{1,0:T(8,128)S(1)} %shard_map.151.after.mine), channel_id=1, source_target_pairs={{0,4},{1,5},{2,6},{3,7},{4,0},{5,1},{6,2},{7,3},{8,12},{9,13},{10,... | collective-permute-start | bytes 258056 | tf_op jit(solution)/shard_map/ppermute | solution.py:529
  25.7 7.6 %collective-permute-start.8 = (f32[240,128]{1,0:T(8,128)S(1)}, f32[240,128]{1,0:T(8,128)S(1)}, u32[]{:S(2)}, u32[]{:S(2)}) collective-permute-start(f32[240,128]{1,0:T(8,128)S(1)} %shard_map.153.after.mine), channel_id=1, source_target_pairs={{0,4},{1,5},{2,6},{3,7},{4,0},{5,1},{6,2},{7,3},{8,12},{9,13},{10,... | collective-permute-start | bytes 368648 | tf_op jit(solution)/shard_map/ppermute | solution.py:529
  27.8 6.9 %collective-permute-start.12 = (f32[176,128]{1,0:T(8,128)S(1)}, f32[176,128]{1,0:T(8,128)S(1)}, u32[]{:S(2)}, u32[]{:S(2)}) collective-permute-start(f32[176,128]{1,0:T(8,128)S(1)} %shard_map.155.after.piece_00), channel_id=1, source_target_pairs={{0,2},{1,3},{2,0},{3,1},{4,6},{5,7},{6,4},{7,5},{8,10},{9,11},{10,... | collective-permute-start | bytes 270344 | tf_op jit(solution)/shard_map/ppermute | solution.py:529
  33.4 5.2 %collective-permute-start.10 = (f32[288,128]{1,0:T(8,128)S(1)}, f32[288,128]{1,0:T(8,128)S(1)}, u32[]{:S(2)}, u32[]{:S(2)}) collective-permute-start(f32[288,128]{1,0:T(8,128)S(1)} %shard_map.156.value.own_piece), channel_id=1, source_target_pairs={{0,2},{1,3},{2,0},{3,1},{4,6},{5,7},{6,4},{7,5},{8,10},{9,11},{10,... | collective-permute-start | bytes 442376 | tf_op jit(solution)/shard_map/ppermute | solution.py:529
  34.7 3.8 %collective-permute-start.13 = (f32[176,128]{1,0:T(8,128)S(1)}, f32[176,128]{1,0:T(8,128)S(1)}, u32[]{:S(2)}, u32[]{:S(2)}) collective-permute-start(f32[176,128]{1,0:T(8,128)S(1)} %collective-permute-done.12.after.piece_01), channel_id=1, source_target_pairs={{0,1},{1,0},{2,3},{3,2},{4,5},{5,4},{6,7},{7,6},{8,9},{9,8},{10,11... | collective-permute-start | bytes 270344 | tf_op jit(solution)/shard_map/ppermute | solution.py:529
  34.7 3.8 %collective-permute-start.11 = (f32[176,128]{1,0:T(8,128)S(1)}, f32[176,128]{1,0:T(8,128)S(1)}, u32[]{:S(2)}, u32[]{:S(2)}) collective-permute-start(f32[176,128]{1,0:T(8,128)S(1)} %shard_map.155.after.piece_00), channel_id=1, source_target_pairs={{0,1},{1,0},{2,3},{3,2},{4,5},{5,4},{6,7},{7,6},{8,9},{9,8},{10,11... | collective-permute-start | bytes 270344 | tf_op jit(solution)/shard_map/ppermute | solution.py:529
  35.3 1.3 %collective-permute-start.14 = (f32[144,128]{1,0:T(8,128)S(1)}, f32[144,128]{1,0:T(8,128)S(1)}, u32[]{:S(2)}, u32[]{:S(2)}) collective-permute-start(f32[144,128]{1,0:T(8,128)S(1)} %get-tuple-element.97), channel_id=1, source_target_pairs={{0,1},{1,0},{2,3},{3,2},{4,5},{5,4},{6,7},{7,6},{8,9},{9,8},{10,11... | collective-permute-start | bytes 221192 | tf_op jit(solution)/shard_map/ppermute | solution.py:529
  35.3 1.4 %collective-permute-start.15 = (f32[144,128]{1,0:T(8,128)S(1)}, f32[144,128]{1,0:T(8,128)S(1)}, u32[]{:S(2)}, u32[]{:S(2)}) collective-permute-start(f32[144,128]{1,0:T(8,128)S(1)} %get-tuple-element.98), channel_id=1, source_target_pairs={{0,1},{1,0},{2,3},{3,2},{4,5},{5,4},{6,7},{7,6},{8,9},{9,8},{10,11... | collective-permute-start | bytes 221192 | tf_op jit(solution)/shard_map/ppermute | solution.py:529
  38.6 1.7 %collective-permute-start.16 = (f32[288,128]{1,0:T(8,128)S(1)}, f32[288,128]{1,0:T(8,128)S(1)}, u32[]{:S(2)}, u32[]{:S(2)}) collective-permute-start(f32[288,128]{1,0:T(8,128)S(1)} %shard_map.161), channel_id=1, source_target_pairs={{0,1},{1,0},{2,3},{3,2},{4,5},{5,4},{6,7},{7,6},{8,9},{9,8},{10,11... | collective-permute-start | bytes 442376 | tf_op jit(solution)/shard_map/ppermute | solution.py:529

commit v2 on v1

--- a/solution.py
+++ b/solution.py
@@ -383,16 +383,22 @@
             begin += rows
 
 
-def quarter_columns(taps, column, levels, seconds, g_conv, g_mix, bias):
+def tap_pairs(taps):
+    return [split(taps[k * CONTEXTS : (k + 1) * CONTEXTS, :]) for k in range(3)]
+
+
+def quarter_weights(pairs, taps, levels, g_conv, g_mix, bias):
     level_high, level_low, partner_high, partner_low = levels
     level = (level_high[...], level_low[...])
     partner = (partner_high[...], partner_low[...])
-    weights = [tuple(ref[k, pl.ds(column, 128), :] for ref in seconds) for k in range(4)]
-    pairs = [split(taps[k * CONTEXTS : (k + 1) * CONTEXTS, :]) for k in range(3)]
     for k, pair in enumerate(pairs):
         g_conv[k] = dot3(level, pair, 0, 0)
     g_mix[...] = dot3(partner, pairs[1], 0, 0)
     bias[...] = jnp.sum(taps[CONTEXTS : 2 * CONTEXTS, :], axis=0, keepdims=True)
+
+
+def quarter_part(pairs, column, seconds):
+    weights = [tuple(ref[k, pl.ds(column, 128), :] for ref in seconds) for k in range(4)]
     part = dot2(permutation(), split(dot3_few(pairs[1], weights[3])))
     for k, pair in enumerate(pairs):
         part = part + dot3_few(pair, weights[k])
@@ -416,28 +422,34 @@
     levels, seconds, refs = refs[:4], refs[4:6], refs[6:]
     g_conv_out, g_mix_out, bias, total, taps, g_conv, g_mix, out_sems = refs
     store = Fetch(out_sems)
-    half = core_first.shape[0]
     taps[0] = own_piece[...]
-    taps[1, :half, :] = core_first[...]
-    taps[1, half:, :] = core_second[...]
+    fill(taps.at[1], core_first, core_second)
     grad_level = None
     for core in range(2):
         column = column_of(core, 0)
-        part = quarter_columns(
-            taps.at[core], column, levels, seconds, g_conv.at[core], g_mix.at[core], bias.at[core : core + 1]
-        )
+        pairs = tap_pairs(taps.at[core])
+        quarter_weights(pairs, taps.at[core], levels, g_conv.at[core], g_mix.at[core], bias.at[core : core + 1])
+        part = quarter_part(pairs, column, seconds)
         store_columns(store, column, g_conv.at[core], g_mix.at[core], g_conv_out, g_mix_out)
         grad_level = part if grad_level is None else grad_level + part
     total[...] = grad_level
     store.wait(*range(len(store.copies)))
 
 
-def other_columns_kernel(piece, *refs):
+def fill(taps, first, second):
+    half = first.shape[0]
+    taps[:half, :] = first[...]
+    taps[half:, :] = second[...]
+
+
+def other_columns_kernel(taps, *refs):
     levels, seconds, refs = refs[:4], refs[4:6], refs[6:]
     partial, g_conv_in, g_mix_in, g_conv_out, g_mix_out, bias, total, g_conv, g_mix, out_sems = refs
     store = Fetch(out_sems)
     column = column_of(0, 1)
-    total[...] = partial[...] + quarter_columns(piece, column, levels, seconds, g_conv, g_mix, bias)
+    pairs = tap_pairs(taps)
+    quarter_weights(pairs, taps, levels, g_conv, g_mix, bias)
+    total[...] = partial[...] + quarter_part(pairs, column, seconds)
     store_columns(store, column, g_conv, g_mix, g_conv_out, g_mix_out)
     store.wait(*range(len(store.copies)))
 
@@ -452,8 +464,8 @@
     channels = embed.shape[1]
     store = Fetch(out_sems)
     column = column_of(1, 1)
-    levels = (level_high, level_low, partner_high, partner_low)
-    far_part = quarter_columns(far_piece, column, levels, (second_high, second_low), far_conv, far_mix, bias_far)
+    pairs = tap_pairs(far_piece)
+    far_part = quarter_part(pairs, column, (second_high, second_low))
     gather_quarters([(piece,) for piece in (piece_00, piece_01, piece_10, piece_11)], quarters)
     side = channels // 4
     rest = []
@@ -464,6 +476,8 @@
     grad_level = split(partial[...] + far_part + jnp.concatenate(rest, axis=0))
     grad_hidden = dot3_few(grad_level, (turn_high[...], turn_low[...]))
     grad_mixed = slopes[...] * jnp.concatenate([grad_hidden, grad_hidden], axis=1)
+    levels = (level_high, level_low, partner_high, partner_low)
+    quarter_weights(pairs, far_piece, levels, far_conv, far_mix, bias_far)
     store_columns(store, column, far_conv, far_mix, g_conv_out, g_mix_out)
     hot = hot_in[...]
     by_letter = dot2(hot, split(grad_mixed), 0, 0)
@@ -634,11 +648,12 @@
 
     merged_x, merged_y = 3 * CONTEXTS, rows_y + EDGE // 2
     piece_y = crossed(sum_y, count, lambda x, y: merged(merge_rest_kernel, merged_y, x, y, turn_low))
-    piece_x = crossed(sum_x, count, lambda x, y: merged(merge_taps_kernel, merged_x, x, y, piece_y))
+    core_y = swapped(piece_y, 1)
+    piece_x = crossed(sum_x, count, lambda x, y: merged(merge_taps_kernel, merged_x, x, y, core_y))
     other_y = swapped(piece_y, 2)
     core_x = [swapped(x, 1) for x in touched(piece_x, other_y, 2)]
 
-    core_y, far_y = swapped(piece_y, 1), swapped(other_y, 1)
+    far_y = swapped(other_y, 1)
     shared = (*levels, second_high, second_low)
     large = [(conv_weight.shape, F32, HBM), (mix_weight.shape, F32, HBM)]
     level_out = ((CONTEXTS, channels), F32, VMEM)
@@ -657,8 +672,7 @@
     )(piece_x, *core_x, *shared)
     other_x = swapped(piece_x, 2)
     rest_y = touched(far_y, partial)[0]
-    core_y = touched(core_y, rest_y)[0]
-    far_x = swapped(touched(other_x, core_y)[0], 1)
+    far_x = swapped(touched(other_x, rest_y)[0], 1)
     g_conv, g_mix, bias_other, partial = call(
         other_columns_kernel,
         [VMEM] * 8 + [HBM] * 2,

time: 44.1 us -> 43.8 us (level)
  waiting for transfers between devices: 6.18 us -> 6.79 us
    ppermute x17, waiting for transfers between devices: 6.18 us -> 6.79 us  [swapped(): return lax.ppermute(value, 'seq', pairs)]
    pallas_call x20 -> x19, Pallas kernels: 18.5 us -> 18.2 us  [placed(): run(*[pltpu.with_memory_space_constraint(x, HBM) if space is HBM else x f...]
where the time goes in v2:
time: 43.8 us; the launch traced here: 43.4 us
  Pallas kernels  18.2 us (42%)
  starting transfers between devices  17.5 us (40%)
  waiting for transfers between devices  6.79 us (16%)
  between operations  0.86 us (2%)
    pallas_call x19, Pallas kernels, placed(): run(*[pltpu.with_memory_space_constraint(x, HBM) if space is HBM else x f...  18.2 us
    ppermute x17, starting transfers between devices, swapped(): return lax.ppermute(value, 'seq', pairs)  17.5 us
    ppermute x17, waiting for transfers between devices, swapped(): return lax.ppermute(value, 'seq', pairs)  6.79 us
  transfers between devices with their start and end apart: 17, of which 5 were waited for; matrix products, arithmetic and copies ran while one was open for 0% of the time, Pallas kernels for 29%

profile of v2, /device:TPU:0, one launch (start us, length us, event | category | flops | bytes accessed | tf_op | source)
XLA Modules:
  0.0 43.4 jit_solution(16429946878191045002)
XLA Ops:
  0.7 2.5 %collective-permute-start.2 = (s32[1,512]{1,0:T(1,128)}, s32[1,512]{1,0:T(1,128)S(1)}, u32[]{:S(2)}, u32[]{:S(2)}) collective-permute-start(s32[1,512]{1,0:T(1,128)} %bitcast.1), channel_id=1, source_target_pairs={{0,3},{1,2},{2,1},{3,0},{4,7},{5,6},{6,5},{7,4},{8,11},{9,10},{10,... | collective-permute-start | bytes 6152 | tf_op jit(solution)/shard_map/ppermute | solution.py:543
  3.2 0.6 %collective-permute-start.1 = (s32[1,512]{1,0:T(1,128)}, s32[1,512]{1,0:T(1,128)S(1)}, u32[]{:S(2)}, u32[]{:S(2)}) collective-permute-start(s32[1,512]{1,0:T(1,128)} %bitcast.2), channel_id=1, source_target_pairs={{0,2},{1,3},{2,0},{3,1},{4,6},{5,7},{6,4},{7,5},{8,10},{9,11},{10,... | collective-permute-start | bytes 6152 | tf_op jit(solution)/shard_map/ppermute | solution.py:543
  3.9 3.2 %shard_map.144 = (s32[1,512]{1,0:T(1,128)S(1)}, f32[32,512]{1,0:T(8,128)S(1)}, f32[3,256,512]{2,1,0:T(8,128)S(1)}, f32[256,512]{1,0:T(8,128)S(1)}, f32[256,256]{...) custom-call(s32[1,512]{1,0:T(1,128)} %bitcast.4, ...), custom_call_target="tpu_custom_call" | custom-call | flops 2969999872 | bytes 8100000 | tf_op jit(solution)/shard_map/pallas_call | solution.py:536
  7.1 2.8 %collective-permute-start.3 = (s32[4,512]{1,0:T(4,128)S(1)}, s32[4,512]{1,0:T(4,128)S(1)}, u32[]{:S(2)}, u32[]{:S(2)}) collective-permute-start(s32[4,512]{1,0:T(4,128)S(1)} %shard_map.145.after.refs_1_), channel_id=1, source_target_pairs={{0,4},{1,5},{2,6},{3,7},{4,0},{5,1},{6,2},{7,3},{8,12},{9,13},{10,... | collective-permute-start | bytes 24584 | tf_op jit(solution)/shard_map/ppermute | solution.py:543
  9.9 2.4 %shard_map.146 = (f32[96,256]{1,0:T(8,128)S(1)}, f32[80,256]{1,0:T(8,128)S(1)}, f32[96,512]{1,0:T(8,128)S(1)}, bf16[256,512]{1,0:T(8,128)(2,1)S(1)}, bf16[256,51...) custom-call(f32[32,512]{1,0:T(8,128)S(1)} %get-tuple-element.67.after.taps, ...), custom_call_target="tpu_custom_call" | custom-call | flops 2750000128 | bytes 7500000 | tf_op jit(solution)/shard_map/pallas_call | solution.py:536
  12.3 2.6 %shard_map.147 = (f32[2,168,128]{2,1,0:T(8,128)S(1)}, f32[2,168,128]{2,1,0:T(8,128)S(1)}, bf16[1024,256]{1,0:T(8,128)(2,1)S(1)}, bf16[1024,256]{1,0:T(8,128)(2,1...) custom-call(s32[2]{0:T(128)S(1)} %copy-done.2, s32[4,512]{1,0:T(4,128)S(1)} %shard_map.145.after.refs_1_, ...), custom_call_target="tpu_custom_call" | custom-call | flops 2200000000 | bytes 6000000 | tf_op jit(solution)/shard_map/pallas_call | solution.py:536
  15.0 0.9 %shard_map.148 = (f32[2,240,128]{2,1,0:T(8,128)S(1)}, f32[2,240,128]{2,1,0:T(8,128)S(1)}) custom-call(bf16[2,256,512]{2,1,0:T(8,128)(2,1)S(1)} %get-tuple-element.73.hots, f32[1024,512]{1,0:T(8,128)S(1)} %get-tuple-element.80.slopes, f32[1024,256]{1,0:T(8,128)S(1)} %get-tuple-element.81.grad_hidden), custom_call_target="tpu_custom_call" | custom-call | flops 1650000000 | bytes 4500000 | tf_op jit(solution)/shard_map/pallas_call | solution.py:536
  15.9 0.6 %collective-permute-start.6 = (f32[2,240,128]{2,1,0:T(8,128)S(1)}, f32[2,240,128]{2,1,0:T(8,128)S(1)}, u32[]{:S(2)}, u32[]{:S(2)}) collective-permute-start(f32[2,240,128]{2,1,0:T(8,128)S(1)} %get-tuple-element.85), channel_id=1, source_target_pairs={{0,1},{1,0},{2,3},{3,2},{4,5},{5,4},{6,7},{7,6},{8,9},{9,8},{10,11... | collective-permute-start | bytes 737288 | tf_op jit(solution)/shard_map/ppermute | solution.py:543
  16.5 1.6 %collective-permute-start.5 = (f32[168,128]{1,0:T(8,128)S(1)}, f32[168,128]{1,0:T(8,128)S(1)}, u32[]{:S(2)}, u32[]{:S(2)}) collective-permute-start(f32[168,128]{1,0:T(8,128)S(1)} %get-tuple-element.84), channel_id=1, source_target_pairs={{0,2},{1,3},{2,0},{3,1},{4,6},{5,7},{6,4},{7,5},{8,10},{9,11},{10,... | collective-permute-start | bytes 258056 | tf_op jit(solution)/shard_map/ppermute | solution.py:543
  18.1 1.1 %collective-permute-start.7 = (f32[240,128]{1,0:T(8,128)S(1)}, f32[240,128]{1,0:T(8,128)S(1)}, u32[]{:S(2)}, u32[]{:S(2)}) collective-permute-start(f32[240,128]{1,0:T(8,128)S(1)} %get-tuple-element.89), channel_id=1, source_target_pairs={{0,2},{1,3},{2,0},{3,1},{4,6},{5,7},{6,4},{7,5},{8,10},{9,11},{10,... | collective-permute-start | bytes 368648 | tf_op jit(solution)/shard_map/ppermute | solution.py:543
  19.3 2.3 %collective-permute-done.5.received = f32[168,128]{1,0:T(8,128)S(1)} collective-permute-done((f32[168,128]{1,0:T(8,128)S(1)}, f32[168,128]{1,0:T(8,128)S(1)}, u32[]{:S(2)}, u32[]{:S(2)}) %collective-permute-start.5) | collective-permute-done | bytes 86048 | tf_op jit(solution)/shard_map/ppermute | solution.py:543
  21.6 2.2 %collective-permute-start.9 = (f32[168,128]{1,0:T(8,128)S(1)}, f32[168,128]{1,0:T(8,128)S(1)}, u32[]{:S(2)}, u32[]{:S(2)}) collective-permute-start(f32[168,128]{1,0:T(8,128)S(1)} %shard_map.151.after.mine), channel_id=1, source_target_pairs={{0,4},{1,5},{2,6},{3,7},{4,0},{5,1},{6,2},{7,3},{8,12},{9,13},{10,... | collective-permute-start | bytes 258056 | tf_op jit(solution)/shard_map/ppermute | solution.py:543
  23.8 1.9 %shard_map.152 = (f32[512,256]{1,0:T(8,128)}, f32[512,256]{1,0:T(8,128)}) custom-call(bf16[2,256,512]{2,1,0:T(8,128)(2,1)S(1)} %get-tuple-element.73.hots, bf16[1024,256]{1,0:T(8,128)(2,1)S(1)} %get-tuple-element.74.hidden_high, bf16[1024,256]{1,0:T(8,128)(2,1)S(1)} %get-tuple-element.75.hidden_low, f32[80,256]{1,0:T(8,128)S(1)} %get-tuple-element.76.local, ...), custom_call_target="tpu_custom_call" | custom-call | flops 2200000000 | bytes 6000000 | tf_op jit(solution)/shard_map/pallas_call | solution.py:536
  25.7 0.8 %collective-permute-start.8 = (f32[240,128]{1,0:T(8,128)S(1)}, f32[240,128]{1,0:T(8,128)S(1)}, u32[]{:S(2)}, u32[]{:S(2)}) collective-permute-start(f32[240,128]{1,0:T(8,128)S(1)} %shard_map.153.after.mine), channel_id=1, source_target_pairs={{0,4},{1,5},{2,6},{3,7},{4,0},{5,1},{6,2},{7,3},{8,12},{9,13},{10,... | collective-permute-start | bytes 368648 | tf_op jit(solution)/shard_map/ppermute | solution.py:543
  26.5 1.2 %shard_map.154 = (bf16[4,512,256]{2,1,0:T(8,128)(2,1)S(1)}, bf16[4,512,256]{2,1,0:T(8,128)(2,1)S(1)}, bf16[4,512,256]{2,1,0:T(8,128)(2,1)S(1)}, bf16[4,512,256]{...) custom-call(f32[3,256,512]{2,1,0:T(8,128)S(1)} %get-tuple-element.90, ...), custom_call_target="tpu_custom_call" | custom-call | flops 1540000000 | bytes 4200000 | tf_op jit(solution)/shard_map/pallas_call | solution.py:536
  27.9 3.9 %collective-permute-start.12 = (f32[176,128]{1,0:T(8,128)S(1)}, f32[176,128]{1,0:T(8,128)S(1)}, u32[]{:S(2)}, u32[]{:S(2)}) collective-permute-start(f32[176,128]{1,0:T(8,128)S(1)} %shard_map.155.piece_00), channel_id=1, source_target_pairs={{0,2},{1,3},{2,0},{3,1},{4,6},{5,7},{6,4},{7,5},{8,10},{9,11},{10,... | collective-permute-start | bytes 270344 | tf_op jit(solution)/shard_map/ppermute | solution.py:543
  31.8 1.5 %collective-permute-done.8.theirs = f32[240,128]{1,0:T(8,128)S(1)} collective-permute-done((f32[240,128]{1,0:T(8,128)S(1)}, f32[240,128]{1,0:T(8,128)S(1)}, u32[]{:S(2)}, u32[]{:S(2)}) %collective-permute-start.8) | collective-permute-done | bytes 122912 | tf_op jit(solution)/shard_map/ppermute | solution.py:543
  33.5 1.8 %collective-permute-done.12.after.piece_01 = f32[176,128]{1,0:T(8,128)S(1)} collective-permute-done((f32[176,128]{1,0:T(8,128)S(1)}, f32[176,128]{1,0:T(8,128)S(1)}, u32[]{:S(2)}, u32[]{:S(2)}) %collective-permute-start.12) | collective-permute-done | bytes 90144 | tf_op jit(solution)/shard_map/ppermute | solution.py:543
  35.3 0.5 %collective-permute-start.14 = (f32[144,128]{1,0:T(8,128)S(1)}, f32[144,128]{1,0:T(8,128)S(1)}, u32[]{:S(2)}, u32[]{:S(2)}) collective-permute-start(f32[144,128]{1,0:T(8,128)S(1)} %get-tuple-element.97), channel_id=1, source_target_pairs={{0,1},{1,0},{2,3},{3,2},{4,5},{5,4},{6,7},{7,6},{8,9},{9,8},{10,11... | collective-permute-start | bytes 221192 | tf_op jit(solution)/shard_map/ppermute | solution.py:543
  36.0 0.8 %collective-permute-done.14.core_first = f32[144,128]{1,0:T(8,128)S(1)} collective-permute-done((f32[144,128]{1,0:T(8,128)S(1)}, f32[144,128]{1,0:T(8,128)S(1)}, u32[]{:S(2)}, u32[]{:S(2)}) %collective-permute-start.14) | collective-permute-done | bytes 73760 | tf_op jit(solution)/shard_map/ppermute | solution.py:543
  36.8 0.4 collective-permute-done.15.core_second
  37.1 1.7 %shard_map.158 = (f32[2,3,256,512]{3,2,1,0:T(8,128)}, f32[2,256,512]{2,1,0:T(8,128)}, f32[2,128]{1,0:T(2,128)S(1)}, f32[96,256]{1,0:T(8,128)S(1)}) custom-call(f32[288,128]{1,0:T(8,128)S(1)} %shard_map.156.value.own_piece, f32[144,128]{1,0:T(8,128)S(1)} %collective-permute-done.14.core_first, f32[144,128]{1,0:T(8,128)S(1)} %collective-permute-done.15.core_second, ...), custom_call_target="tpu_custom_call" | custom-call | flops 55000000 | bytes 150000 | tf_op jit(solution)/shard_map/pallas_call | solution.py:536
  39.2 1.3 %shard_map.161 = (f32[2,3,256,512]{3,2,1,0:T(8,128)}, f32[2,256,512]{2,1,0:T(8,128)}, f32[1,128]{1,0:T(1,128)S(1)}, f32[96,256]{1,0:T(8,128)S(1)}) custom-call(f32[288,128]{1,0:T(8,128)S(1)} %collective-permute-done.11.value.taps, bf16[96,256]{1,0:T(8,128)(2,1)S(1)} %get-tuple-element.99.refs_0_.level_high, ...), custom_call_target="tpu_custom_call", output_to_operand_aliasing={{0}: (8, {}), {1}: (9, {})} | custom-call | flops 55000000 | bytes 150000 | tf_op jit(solution)/shard_map/pallas_call | solution.py:536
  40.5 2.9 %shard_map.162 = (f32[2,3,256,512]{3,2,1,0:T(8,128)}, f32[2,256,512]{2,1,0:T(8,128)}, f32[4,256]{1,0:T(4,128)}, f32[2,512]{1,0:T(2,128)}, f32[2,256,256]{2,1,0:T(8,128)}) custom-call(f32[288,128]{1,0:T(8,128)S(1)} %collective-permute-done.16.far_piece, ...), custom_call_target="tpu_custom_call", output_to_operand_aliasing={{0}: (23, {}), {1}: (24, {})} | custom-call | flops 2969999872 | bytes 8100000 | tf_op jit(solution)/shard_map/pallas_call | solution.py:536
  (35 shorter events, 0.9 us)
Async XLA Ops:
  0.6 9.3 %copy-start = (f32[2,512]{1,0:T(2,128)S(1)}, f32[2,512]{1,0:T(2,128)}, u32[]{:S(2)}) copy-start(f32[2,512]{1,0:T(2,128)} %bias.1) | copy-start | bytes 12292
  0.6 9.3 %copy-start.1 = (f32[4,256]{1,0:T(4,128)S(1)}, f32[4,256]{1,0:T(4,128)}, u32[]{:S(2)}) copy-start(f32[4,256]{1,0:T(4,128)} %embed.3) | copy-start | bytes 12292
  0.7 6.4 %collective-permute-start.2 = (s32[1,512]{1,0:T(1,128)}, s32[1,512]{1,0:T(1,128)S(1)}, u32[]{:S(2)}, u32[]{:S(2)}) collective-permute-start(s32[1,512]{1,0:T(1,128)} %bitcast.1), channel_id=1, source_target_pairs={{0,3},{1,2},{2,1},{3,0},{4,7},{5,6},{6,5},{7,4},{8,11},{9,10},{10,... | collective-permute-start | bytes 6152 | tf_op jit(solution)/shard_map/ppermute | solution.py:543
  3.2 3.9 %collective-permute-start.1 = (s32[1,512]{1,0:T(1,128)}, s32[1,512]{1,0:T(1,128)S(1)}, u32[]{:S(2)}, u32[]{:S(2)}) collective-permute-start(s32[1,512]{1,0:T(1,128)} %bitcast.2), channel_id=1, source_target_pairs={{0,2},{1,3},{2,0},{3,1},{4,6},{5,7},{6,4},{7,5},{8,10},{9,11},{10,... | collective-permute-start | bytes 6152 | tf_op jit(solution)/shard_map/ppermute | solution.py:543
  3.8 3.2 %collective-permute-start = (s32[1,512]{1,0:T(1,128)}, s32[1,512]{1,0:T(1,128)S(1)}, u32[]{:S(2)}, u32[]{:S(2)}) collective-permute-start(s32[1,512]{1,0:T(1,128)} %bitcast.3), channel_id=1, source_target_pairs={{0,1},{1,0},{2,3},{3,2},{4,5},{5,4},{6,7},{7,6},{8,9},{9,8},{10,11... | collective-permute-start | bytes 6152 | tf_op jit(solution)/shard_map/ppermute | solution.py:543
  7.1 5.2 %collective-permute-start.3 = (s32[4,512]{1,0:T(4,128)S(1)}, s32[4,512]{1,0:T(4,128)S(1)}, u32[]{:S(2)}, u32[]{:S(2)}) collective-permute-start(s32[4,512]{1,0:T(4,128)S(1)} %shard_map.145.after.refs_1_), channel_id=1, source_target_pairs={{0,4},{1,5},{2,6},{3,7},{4,0},{5,1},{6,2},{7,3},{8,12},{9,13},{10,... | collective-permute-start | bytes 24584 | tf_op jit(solution)/shard_map/ppermute | solution.py:543
  9.9 2.4 %copy-start.2 = (s32[2]{0:T(128)S(1)}, s32[2]{0:T(128)}, u32[]{:S(2)}) copy-start(s32[2]{0:T(128)} %refs_0_.1) | copy-start | bytes 28
  14.9 1.5 %collective-permute-start.4 = (f32[2,168,128]{2,1,0:T(8,128)S(1)}, f32[2,168,128]{2,1,0:T(8,128)S(1)}, u32[]{:S(2)}, u32[]{:S(2)}) collective-permute-start(f32[2,168,128]{2,1,0:T(8,128)S(1)} %get-tuple-element.79), channel_id=1, source_target_pairs={{0,1},{1,0},{2,3},{3,2},{4,5},{5,4},{6,7},{7,6},{8,9},{9,8},{10,11... | collective-permute-start | bytes 516104 | tf_op jit(solution)/shard_map/ppermute | solution.py:543
  15.9 2.2 %collective-permute-start.6 = (f32[2,240,128]{2,1,0:T(8,128)S(1)}, f32[2,240,128]{2,1,0:T(8,128)S(1)}, u32[]{:S(2)}, u32[]{:S(2)}) collective-permute-start(f32[2,240,128]{2,1,0:T(8,128)S(1)} %get-tuple-element.85), channel_id=1, source_target_pairs={{0,1},{1,0},{2,3},{3,2},{4,5},{5,4},{6,7},{7,6},{8,9},{9,8},{10,11... | collective-permute-start | bytes 737288 | tf_op jit(solution)/shard_map/ppermute | solution.py:543
  16.5 5.1 %collective-permute-start.5 = (f32[168,128]{1,0:T(8,128)S(1)}, f32[168,128]{1,0:T(8,128)S(1)}, u32[]{:S(2)}, u32[]{:S(2)}) collective-permute-start(f32[168,128]{1,0:T(8,128)S(1)} %get-tuple-element.84), channel_id=1, source_target_pairs={{0,2},{1,3},{2,0},{3,1},{4,6},{5,7},{6,4},{7,5},{8,10},{9,11},{10,... | collective-permute-start | bytes 258056 | tf_op jit(solution)/shard_map/ppermute | solution.py:543
  18.1 7.5 %collective-permute-start.7 = (f32[240,128]{1,0:T(8,128)S(1)}, f32[240,128]{1,0:T(8,128)S(1)}, u32[]{:S(2)}, u32[]{:S(2)}) collective-permute-start(f32[240,128]{1,0:T(8,128)S(1)} %get-tuple-element.89), channel_id=1, source_target_pairs={{0,2},{1,3},{2,0},{3,1},{4,6},{5,7},{6,4},{7,5},{8,10},{9,11},{10,... | collective-permute-start | bytes 368648 | tf_op jit(solution)/shard_map/ppermute | solution.py:543
  21.6 6.2 %collective-permute-start.9 = (f32[168,128]{1,0:T(8,128)S(1)}, f32[168,128]{1,0:T(8,128)S(1)}, u32[]{:S(2)}, u32[]{:S(2)}) collective-permute-start(f32[168,128]{1,0:T(8,128)S(1)} %shard_map.151.after.mine), channel_id=1, source_target_pairs={{0,4},{1,5},{2,6},{3,7},{4,0},{5,1},{6,2},{7,3},{8,12},{9,13},{10,... | collective-permute-start | bytes 258056 | tf_op jit(solution)/shard_map/ppermute | solution.py:543
  25.7 7.6 %collective-permute-start.8 = (f32[240,128]{1,0:T(8,128)S(1)}, f32[240,128]{1,0:T(8,128)S(1)}, u32[]{:S(2)}, u32[]{:S(2)}) collective-permute-start(f32[240,128]{1,0:T(8,128)S(1)} %shard_map.153.after.mine), channel_id=1, source_target_pairs={{0,4},{1,5},{2,6},{3,7},{4,0},{5,1},{6,2},{7,3},{8,12},{9,13},{10,... | collective-permute-start | bytes 368648 | tf_op jit(solution)/shard_map/ppermute | solution.py:543
  27.8 4.0 %collective-permute-start.10 = (f32[176,128]{1,0:T(8,128)S(1)}, f32[176,128]{1,0:T(8,128)S(1)}, u32[]{:S(2)}, u32[]{:S(2)}) collective-permute-start(f32[176,128]{1,0:T(8,128)S(1)} %shard_map.155.piece_00), channel_id=1, source_target_pairs={{0,1},{1,0},{2,3},{3,2},{4,5},{5,4},{6,7},{7,6},{8,9},{9,8},{10,11... | collective-permute-start | bytes 270344 | tf_op jit(solution)/shard_map/ppermute | solution.py:543
  27.9 7.4 %collective-permute-start.12 = (f32[176,128]{1,0:T(8,128)S(1)}, f32[176,128]{1,0:T(8,128)S(1)}, u32[]{:S(2)}, u32[]{:S(2)}) collective-permute-start(f32[176,128]{1,0:T(8,128)S(1)} %shard_map.155.piece_00), channel_id=1, source_target_pairs={{0,2},{1,3},{2,0},{3,1},{4,6},{5,7},{6,4},{7,5},{8,10},{9,11},{10,... | collective-permute-start | bytes 270344 | tf_op jit(solution)/shard_map/ppermute | solution.py:543
  33.4 5.6 %collective-permute-start.11 = (f32[288,128]{1,0:T(8,128)S(1)}, f32[288,128]{1,0:T(8,128)S(1)}, u32[]{:S(2)}, u32[]{:S(2)}) collective-permute-start(f32[288,128]{1,0:T(8,128)S(1)} %shard_map.156.value.own_piece), channel_id=1, source_target_pairs={{0,2},{1,3},{2,0},{3,1},{4,6},{5,7},{6,4},{7,5},{8,10},{9,11},{10,... | collective-permute-start | bytes 442376 | tf_op jit(solution)/shard_map/ppermute | solution.py:543
  35.3 3.6 %collective-permute-start.13 = (f32[176,128]{1,0:T(8,128)S(1)}, f32[176,128]{1,0:T(8,128)S(1)}, u32[]{:S(2)}, u32[]{:S(2)}) collective-permute-start(f32[176,128]{1,0:T(8,128)S(1)} %collective-permute-done.12.after.piece_01), channel_id=1, source_target_pairs={{0,1},{1,0},{2,3},{3,2},{4,5},{5,4},{6,7},{7,6},{8,9},{9,8},{10,11... | collective-permute-start | bytes 270344 | tf_op jit(solution)/shard_map/ppermute | solution.py:543
  35.3 1.5 %collective-permute-start.14 = (f32[144,128]{1,0:T(8,128)S(1)}, f32[144,128]{1,0:T(8,128)S(1)}, u32[]{:S(2)}, u32[]{:S(2)}) collective-permute-start(f32[144,128]{1,0:T(8,128)S(1)} %get-tuple-element.97), channel_id=1, source_target_pairs={{0,1},{1,0},{2,3},{3,2},{4,5},{5,4},{6,7},{7,6},{8,9},{9,8},{10,11... | collective-permute-start | bytes 221192 | tf_op jit(solution)/shard_map/ppermute | solution.py:543
  35.9 1.3 %collective-permute-start.15 = (f32[144,128]{1,0:T(8,128)S(1)}, f32[144,128]{1,0:T(8,128)S(1)}, u32[]{:S(2)}, u32[]{:S(2)}) collective-permute-start(f32[144,128]{1,0:T(8,128)S(1)} %get-tuple-element.98), channel_id=1, source_target_pairs={{0,1},{1,0},{2,3},{3,2},{4,5},{5,4},{6,7},{7,6},{8,9},{9,8},{10,11... | collective-permute-start | bytes 221192 | tf_op jit(solution)/shard_map/ppermute | solution.py:543
  39.0 1.5 %collective-permute-start.16 = (f32[288,128]{1,0:T(8,128)S(1)}, f32[288,128]{1,0:T(8,128)S(1)}, u32[]{:S(2)}, u32[]{:S(2)}) collective-permute-start(f32[288,128]{1,0:T(8,128)S(1)} %shard_map.160), channel_id=1, source_target_pairs={{0,1},{1,0},{2,3},{3,2},{4,5},{5,4},{6,7},{7,6},{8,9},{9,8},{10,11... | collective-permute-start | bytes 442376 | tf_op jit(solution)/shard_map/ppermute | solution.py:543

commit v3 on v2

--- a/solution.py
+++ b/solution.py
@@ -418,28 +418,35 @@
     store.start(g_mix, g_mix_out.at[1, :, block])
 
 
-def own_columns_kernel(own_piece, core_first, core_second, *refs):
-    levels, seconds, refs = refs[:4], refs[4:6], refs[6:]
-    g_conv_out, g_mix_out, bias, total, taps, g_conv, g_mix, out_sems = refs
-    store = Fetch(out_sems)
-    taps[0] = own_piece[...]
-    fill(taps.at[1], core_first, core_second)
-    grad_level = None
-    for core in range(2):
-        column = column_of(core, 0)
-        pairs = tap_pairs(taps.at[core])
-        quarter_weights(pairs, taps.at[core], levels, g_conv.at[core], g_mix.at[core], bias.at[core : core + 1])
-        part = quarter_part(pairs, column, seconds)
-        store_columns(store, column, g_conv.at[core], g_mix.at[core], g_conv_out, g_mix_out)
-        grad_level = part if grad_level is None else grad_level + part
-    total[...] = grad_level
-    store.wait(*range(len(store.copies)))
-
-
 def fill(taps, first, second):
     half = first.shape[0]
     taps[:half, :] = first[...]
     taps[half:, :] = second[...]
+
+
+def own_columns_kernel(taps, *refs):
+    levels, seconds, refs = refs[:4], refs[4:6], refs[6:]
+    after, g_conv_out, g_mix_out, bias, total, g_conv, g_mix, out_sems = refs
+    store = Fetch(out_sems)
+    column = column_of(0, 0)
+    pairs = tap_pairs(taps)
+    quarter_weights(pairs, taps, levels, g_conv, g_mix, bias)
+    total[...] = quarter_part(pairs, column, seconds)
+    store_columns(store, column, g_conv, g_mix, g_conv_out, g_mix_out)
+    store.wait(*range(len(store.copies)))
+
+
+def core_columns_kernel(first, second, *refs):
+    levels, seconds, refs = refs[:4], refs[4:6], refs[6:]
+    partial, g_conv_in, g_mix_in, g_conv_out, g_mix_out, bias, total, taps, g_conv, g_mix, out_sems = refs
+    fill(taps, first, second)
+    store = Fetch(out_sems)
+    column = column_of(1, 0)
+    pairs = tap_pairs(taps)
+    quarter_weights(pairs, taps, levels, g_conv, g_mix, bias)
+    total[...] = partial[...] + quarter_part(pairs, column, seconds)
+    store_columns(store, column, g_conv, g_mix, g_conv_out, g_mix_out)
+    store.wait(*range(len(store.copies)))
 
 
 def other_columns_kernel(taps, *refs):
@@ -456,7 +463,7 @@
 
 def first_layer_kernel(
     far_piece, level_high, level_low, partner_high, partner_low, second_high, second_low,
-    piece_00, piece_01, piece_10, piece_11, partial, bias_own, bias_other, embed,
+    piece_00, piece_01, piece_10, piece_11, partial, bias_own, bias_core, bias_other, embed,
     first_high, first_low, turn_high, turn_low, hidden_high, hidden_low, slopes, hot_in,
     g_conv_in, g_mix_in, g_conv_out, g_mix_out, g_embed_out, g_bias_out, g_out_out,
     quarters, bias_rows, bias_far, far_conv, far_mix, g_conv, g_mix, g_embed, g_bias, g_out, out_sems,
@@ -503,7 +510,7 @@
     place = lax.axis_index("seq")
     low, high = place & 1, (place >> 1) & 1
     for row, x, y in (
-        (bias_own[0:1, :], 0, 0), (bias_own[1:2, :], 1, 0), (bias_other[...], 0, 1), (bias_far[...], 1, 1)
+        (bias_own[...], 0, 0), (bias_core[...], 1, 0), (bias_other[...], 0, 1), (bias_far[...], 1, 1)
     ):
         bias_rows[(low ^ x) * 2 + (high ^ y)] = row
     g_bias[0:1, :] = jnp.sum(grad_mixed, axis=0, keepdims=True)
@@ -651,28 +658,33 @@
     core_y = swapped(piece_y, 1)
     piece_x = crossed(sum_x, count, lambda x, y: merged(merge_taps_kernel, merged_x, x, y, core_y))
     other_y = swapped(piece_y, 2)
-    core_x = [swapped(x, 1) for x in touched(piece_x, other_y, 2)]
-
-    far_y = swapped(other_y, 1)
+    halves_x = touched(piece_x, other_y, 2)
+    core_x = [swapped(x, 1) for x in halves_x]
+
     shared = (*levels, second_high, second_low)
     large = [(conv_weight.shape, F32, HBM), (mix_weight.shape, F32, HBM)]
     level_out = ((CONTEXTS, channels), F32, VMEM)
     quarter_conv, quarter_mix = (3, channels, 128), (channels, 128)
+    bias_out = ((1, 128), F32, VMEM)
     g_conv, g_mix, bias_own, partial = call(
         own_columns_kernel,
-        [VMEM] * 9,
-        [*large, ((2, 128), F32, VMEM), level_out],
-        [
-            VMEM((2, merged_x, 128), F32),
-            VMEM((2, *quarter_conv), F32),
-            VMEM((2, *quarter_mix), F32),
-            sems((8,)),
-        ],
+        [VMEM] * 8,
+        [*large, bias_out, level_out],
+        [VMEM(quarter_conv, F32), VMEM(quarter_mix, F32), sems((4,))],
+        micros=1.2,
+    )(piece_x, *shared, halves_x[0])
+    g_conv, g_mix, bias_core, partial = call(
+        core_columns_kernel,
+        [VMEM] * 9 + [HBM] * 2,
+        [*large, bias_out, level_out],
+        [VMEM((merged_x, 128), F32), VMEM(quarter_conv, F32), VMEM(quarter_mix, F32), sems((4,))],
+        aliases={9: 0, 10: 1},
         micros=0.05,
-    )(piece_x, *core_x, *shared)
+    )(*core_x, *shared, partial, g_conv, g_mix)
     other_x = swapped(piece_x, 2)
-    rest_y = touched(far_y, partial)[0]
-    far_x = swapped(touched(other_x, rest_y)[0], 1)
+    late_y = touched(other_y, partial)[0]
+    rest_y = swapped(late_y, 1)
+    far_x = swapped(touched(other_x, late_y)[0], 1)
     g_conv, g_mix, bias_other, partial = call(
         other_columns_kernel,
         [VMEM] * 8 + [HBM] * 2,
@@ -683,7 +695,7 @@
     )(other_x, *shared, partial, g_conv, g_mix)
     g_conv, g_mix, g_embed, g_bias, g_out = call(
         first_layer_kernel,
-        [VMEM] * 23 + [HBM] * 2,
+        [VMEM] * 24 + [HBM] * 2,
         [*large] + [(shape, F32, HBM) for shape in (embed.shape, gate_bias.shape, out_weight.shape)],
         [
             VMEM((4, merged_y, 128), F32),
@@ -698,10 +710,10 @@
             VMEM(out_weight.shape, F32),
             sems((11,)),
         ],
-        aliases={23: 0, 24: 1},
+        aliases={24: 0, 25: 1},
         micros=2.7,
     )(
-        far_x, *shared, piece_y, other_y, core_y, rest_y, partial, bias_own, bias_other, embed,
+        far_x, *shared, piece_y, other_y, core_y, rest_y, partial, bias_own, bias_core, bias_other, embed,
         first_high, first_low, turn_high, turn_low, *tables, g_conv, g_mix,
     )
     return (out_fwd, out_rev, g_embed, g_conv, g_mix, g_bias, g_out)

time: 43.8 us -> 43.5 us (level)
  waiting for transfers between devices: 6.79 us -> 5.63 us
  Pallas kernels: 18.2 us -> 19.1 us
    ppermute x17, waiting for transfers between devices: 6.79 us -> 5.63 us  [swapped(): return lax.ppermute(value, 'seq', pairs)]
    pallas_call x19 -> x20, Pallas kernels: 18.2 us -> 19.1 us  [placed(): run(*[pltpu.with_memory_space_constraint(x, HBM) if space is HBM else x f...]
  transfers between devices with their start and end apart: 17 -> 17, of which waited for: 5 -> 3; matrix products, arithmetic and copies ran while one was open for 0% -> 0% of each run, Pallas kernels for 29% -> 31%
where the time goes in v3:
time: 43.5 us; the launch traced here: 43.4 us
  Pallas kernels  19.1 us (44%)
  starting transfers between devices  17.8 us (41%)
  waiting for transfers between devices  5.63 us (13%)
  between operations  0.87 us (2%)
    pallas_call x20, Pallas kernels, placed(): run(*[pltpu.with_memory_space_constraint(x, HBM) if space is HBM else x f...  19.1 us
    ppermute x17, starting transfers between devices, swapped(): return lax.ppermute(value, 'seq', pairs)  17.8 us
    ppermute x17, waiting for transfers between devices, swapped(): return lax.ppermute(value, 'seq', pairs)  5.63 us
  transfers between devices with their start and end apart: 17, of which 3 were waited for; matrix products, arithmetic and copies ran while one was open for 0% of the time, Pallas kernels for 31%

profile of v3, /device:TPU:0, one launch (start us, length us, event | category | flops | bytes accessed | tf_op | source)
XLA Modules:
  0.0 43.4 jit_solution(17948619429794361678)
XLA Ops:
  0.7 2.5 %collective-permute-start.2 = (s32[1,512]{1,0:T(1,128)}, s32[1,512]{1,0:T(1,128)S(1)}, u32[]{:S(2)}, u32[]{:S(2)}) collective-permute-start(s32[1,512]{1,0:T(1,128)} %bitcast.1), channel_id=1, source_target_pairs={{0,3},{1,2},{2,1},{3,0},{4,7},{5,6},{6,5},{7,4},{8,11},{9,10},{10,... | collective-permute-start | bytes 6152 | tf_op jit(solution)/shard_map/ppermute | solution.py:550
  3.2 0.6 %collective-permute-start.1 = (s32[1,512]{1,0:T(1,128)}, s32[1,512]{1,0:T(1,128)S(1)}, u32[]{:S(2)}, u32[]{:S(2)}) collective-permute-start(s32[1,512]{1,0:T(1,128)} %bitcast.2), channel_id=1, source_target_pairs={{0,2},{1,3},{2,0},{3,1},{4,6},{5,7},{6,4},{7,5},{8,10},{9,11},{10,... | collective-permute-start | bytes 6152 | tf_op jit(solution)/shard_map/ppermute | solution.py:550
  3.9 3.2 %shard_map.144 = (s32[1,512]{1,0:T(1,128)S(1)}, f32[32,512]{1,0:T(8,128)S(1)}, f32[3,256,512]{2,1,0:T(8,128)S(1)}, f32[256,512]{1,0:T(8,128)S(1)}, f32[256,256]{...) custom-call(s32[1,512]{1,0:T(1,128)} %bitcast.4, ...), custom_call_target="tpu_custom_call" | custom-call | flops 2969999872 | bytes 8100000 | tf_op jit(solution)/shard_map/pallas_call | solution.py:543
  7.1 2.8 %collective-permute-start.3 = (s32[4,512]{1,0:T(4,128)S(1)}, s32[4,512]{1,0:T(4,128)S(1)}, u32[]{:S(2)}, u32[]{:S(2)}) collective-permute-start(s32[4,512]{1,0:T(4,128)S(1)} %shard_map.145.after.refs_1_), channel_id=1, source_target_pairs={{0,4},{1,5},{2,6},{3,7},{4,0},{5,1},{6,2},{7,3},{8,12},{9,13},{10,... | collective-permute-start | bytes 24584 | tf_op jit(solution)/shard_map/ppermute | solution.py:550
  9.9 2.3 %shard_map.146 = (f32[96,256]{1,0:T(8,128)S(1)}, f32[80,256]{1,0:T(8,128)S(1)}, f32[96,512]{1,0:T(8,128)S(1)}, bf16[256,512]{1,0:T(8,128)(2,1)S(1)}, bf16[256,51...) custom-call(f32[32,512]{1,0:T(8,128)S(1)} %get-tuple-element.71.after.taps, ...), custom_call_target="tpu_custom_call" | custom-call | flops 2750000128 | bytes 7500000 | tf_op jit(solution)/shard_map/pallas_call | solution.py:543
  12.3 2.6 %shard_map.147 = (f32[2,168,128]{2,1,0:T(8,128)S(1)}, f32[2,168,128]{2,1,0:T(8,128)S(1)}, bf16[1024,256]{1,0:T(8,128)(2,1)S(1)}, bf16[1024,256]{1,0:T(8,128)(2,1...) custom-call(s32[2]{0:T(128)S(1)} %copy-done.2, s32[4,512]{1,0:T(4,128)S(1)} %shard_map.145.after.refs_1_, ...), custom_call_target="tpu_custom_call" | custom-call | flops 2200000000 | bytes 6000000 | tf_op jit(solution)/shard_map/pallas_call | solution.py:543
  15.0 0.9 %shard_map.148 = (f32[2,240,128]{2,1,0:T(8,128)S(1)}, f32[2,240,128]{2,1,0:T(8,128)S(1)}) custom-call(bf16[2,256,512]{2,1,0:T(8,128)(2,1)S(1)} %get-tuple-element.77.hots, f32[1024,512]{1,0:T(8,128)S(1)} %get-tuple-element.84.slopes, f32[1024,256]{1,0:T(8,128)S(1)} %get-tuple-element.85.grad_hidden), custom_call_target="tpu_custom_call" | custom-call | flops 1650000000 | bytes 4500000 | tf_op jit(solution)/shard_map/pallas_call | solution.py:543
  15.9 0.5 %collective-permute-start.6 = (f32[2,240,128]{2,1,0:T(8,128)S(1)}, f32[2,240,128]{2,1,0:T(8,128)S(1)}, u32[]{:S(2)}, u32[]{:S(2)}) collective-permute-start(f32[2,240,128]{2,1,0:T(8,128)S(1)} %get-tuple-element.89), channel_id=1, source_target_pairs={{0,1},{1,0},{2,3},{3,2},{4,5},{5,4},{6,7},{7,6},{8,9},{9,8},{10,11... | collective-permute-start | bytes 737288 | tf_op jit(solution)/shard_map/ppermute | solution.py:550
  16.5 1.6 %collective-permute-start.5 = (f32[168,128]{1,0:T(8,128)S(1)}, f32[168,128]{1,0:T(8,128)S(1)}, u32[]{:S(2)}, u32[]{:S(2)}) collective-permute-start(f32[168,128]{1,0:T(8,128)S(1)} %get-tuple-element.88), channel_id=1, source_target_pairs={{0,2},{1,3},{2,0},{3,1},{4,6},{5,7},{6,4},{7,5},{8,10},{9,11},{10,... | collective-permute-start | bytes 258056 | tf_op jit(solution)/shard_map/ppermute | solution.py:550
  18.1 1.1 %collective-permute-start.7 = (f32[240,128]{1,0:T(8,128)S(1)}, f32[240,128]{1,0:T(8,128)S(1)}, u32[]{:S(2)}, u32[]{:S(2)}) collective-permute-start(f32[240,128]{1,0:T(8,128)S(1)} %get-tuple-element.93), channel_id=1, source_target_pairs={{0,2},{1,3},{2,0},{3,1},{4,6},{5,7},{6,4},{7,5},{8,10},{9,11},{10,... | collective-permute-start | bytes 368648 | tf_op jit(solution)/shard_map/ppermute | solution.py:550
  19.3 2.3 %collective-permute-done.5.received = f32[168,128]{1,0:T(8,128)S(1)} collective-permute-done((f32[168,128]{1,0:T(8,128)S(1)}, f32[168,128]{1,0:T(8,128)S(1)}, u32[]{:S(2)}, u32[]{:S(2)}) %collective-permute-start.5) | collective-permute-done | bytes 86048 | tf_op jit(solution)/shard_map/ppermute | solution.py:550
  21.5 2.2 %collective-permute-start.9 = (f32[168,128]{1,0:T(8,128)S(1)}, f32[168,128]{1,0:T(8,128)S(1)}, u32[]{:S(2)}, u32[]{:S(2)}) collective-permute-start(f32[168,128]{1,0:T(8,128)S(1)} %shard_map.151.after.mine), channel_id=1, source_target_pairs={{0,4},{1,5},{2,6},{3,7},{4,0},{5,1},{6,2},{7,3},{8,12},{9,13},{10,... | collective-permute-start | bytes 258056 | tf_op jit(solution)/shard_map/ppermute | solution.py:550
  23.8 1.9 %shard_map.152 = (f32[512,256]{1,0:T(8,128)}, f32[512,256]{1,0:T(8,128)}) custom-call(bf16[2,256,512]{2,1,0:T(8,128)(2,1)S(1)} %get-tuple-element.77.hots, bf16[1024,256]{1,0:T(8,128)(2,1)S(1)} %get-tuple-element.78.hidden_high, bf16[1024,256]{1,0:T(8,128)(2,1)S(1)} %get-tuple-element.79.hidden_low, f32[80,256]{1,0:T(8,128)S(1)} %get-tuple-element.80.local, ...), custom_call_target="tpu_custom_call" | custom-call | flops 2200000000 | bytes 6000000 | tf_op jit(solution)/shard_map/pallas_call | solution.py:543
  25.7 0.8 %collective-permute-start.8 = (f32[240,128]{1,0:T(8,128)S(1)}, f32[240,128]{1,0:T(8,128)S(1)}, u32[]{:S(2)}, u32[]{:S(2)}) collective-permute-start(f32[240,128]{1,0:T(8,128)S(1)} %shard_map.153.after.mine), channel_id=1, source_target_pairs={{0,4},{1,5},{2,6},{3,7},{4,0},{5,1},{6,2},{7,3},{8,12},{9,13},{10,... | collective-permute-start | bytes 368648 | tf_op jit(solution)/shard_map/ppermute | solution.py:550
  26.5 1.2 %shard_map.154 = (bf16[4,512,256]{2,1,0:T(8,128)(2,1)S(1)}, bf16[4,512,256]{2,1,0:T(8,128)(2,1)S(1)}, bf16[4,512,256]{2,1,0:T(8,128)(2,1)S(1)}, bf16[4,512,256]{...) custom-call(f32[3,256,512]{2,1,0:T(8,128)S(1)} %get-tuple-element.94, ...), custom_call_target="tpu_custom_call" | custom-call | flops 1540000000 | bytes 4200000 | tf_op jit(solution)/shard_map/pallas_call | solution.py:543
  27.9 3.9 %collective-permute-start.12 = (f32[176,128]{1,0:T(8,128)S(1)}, f32[176,128]{1,0:T(8,128)S(1)}, u32[]{:S(2)}, u32[]{:S(2)}) collective-permute-start(f32[176,128]{1,0:T(8,128)S(1)} %shard_map.155.piece_00), channel_id=1, source_target_pairs={{0,2},{1,3},{2,0},{3,1},{4,6},{5,7},{6,4},{7,5},{8,10},{9,11},{10,... | collective-permute-start | bytes 270344 | tf_op jit(solution)/shard_map/ppermute | solution.py:550
  31.8 1.5 %collective-permute-done.8.theirs = f32[240,128]{1,0:T(8,128)S(1)} collective-permute-done((f32[240,128]{1,0:T(8,128)S(1)}, f32[240,128]{1,0:T(8,128)S(1)}, u32[]{:S(2)}, u32[]{:S(2)}) %collective-permute-start.8) | collective-permute-done | bytes 122912 | tf_op jit(solution)/shard_map/ppermute | solution.py:550
  33.5 1.8 %collective-permute-done.12.after.value.piece_01 = f32[176,128]{1,0:T(8,128)S(1)} collective-permute-done((f32[176,128]{1,0:T(8,128)S(1)}, f32[176,128]{1,0:T(8,128)S(1)}, u32[]{:S(2)}, u32[]{:S(2)}) %collective-permute-start.12) | collective-permute-done | bytes 90144 | tf_op jit(solution)/shard_map/ppermute | solution.py:550
  35.4 0.4 collective-permute-start.13
  35.9 1.3 %shard_map.158 = (f32[2,3,256,512]{3,2,1,0:T(8,128)}, f32[2,256,512]{2,1,0:T(8,128)}, f32[1,128]{1,0:T(1,128)S(1)}, f32[96,256]{1,0:T(8,128)S(1)}) custom-call(f32[288,128]{1,0:T(8,128)S(1)} %shard_map.156.value.taps, bf16[96,256]{1,0:T(8,128)(2,1)S(1)} %get-tuple-element.103.refs_0_.level_high, bf16[96,256]{1,0:T(8,128)(2,1)S(1)} %get-tuple-element.104.refs_1_.level_low, ...), custom_call_target="tpu_custom_call" | custom-call | flops 1320000000 | bytes 3600000 | tf_op jit(solution)/shard_map/pallas_call | solution.py:543
  37.2 1.3 %shard_map.159 = (f32[2,3,256,512]{3,2,1,0:T(8,128)}, f32[2,256,512]{2,1,0:T(8,128)}, f32[1,128]{1,0:T(1,128)S(1)}, f32[96,256]{1,0:T(8,128)S(1)}) custom-call(f32[144,128]{1,0:T(8,128)S(1)} %collective-permute-done.13.first, f32[144,128]{1,0:T(8,128)S(1)} %collective-permute-done.14.second, ...), custom_call_target="tpu_custom_call", output_to_operand_aliasing={{0}: (9, {}), {1}: (10, {})} | custom-call | flops 55000000 | bytes 150000 | tf_op jit(solution)/shard_map/pallas_call | solution.py:543
  38.7 0.5 %collective-permute-start.16 = (f32[176,128]{1,0:T(8,128)S(1)}, f32[176,128]{1,0:T(8,128)S(1)}, u32[]{:S(2)}, u32[]{:S(2)}) collective-permute-start(f32[176,128]{1,0:T(8,128)S(1)} %shard_map.160.after), channel_id=1, source_target_pairs={{0,1},{1,0},{2,3},{3,2},{4,5},{5,4},{6,7},{7,6},{8,9},{9,8},{10,11... | collective-permute-start | bytes 270344 | tf_op jit(solution)/shard_map/ppermute | solution.py:550
  39.2 1.3 %shard_map.162 = (f32[2,3,256,512]{3,2,1,0:T(8,128)}, f32[2,256,512]{2,1,0:T(8,128)}, f32[1,128]{1,0:T(1,128)S(1)}, f32[96,256]{1,0:T(8,128)S(1)}) custom-call(f32[288,128]{1,0:T(8,128)S(1)} %collective-permute-done.11.value.taps, bf16[96,256]{1,0:T(8,128)(2,1)S(1)} %get-tuple-element.103.refs_0_.level_high, ...), custom_call_target="tpu_custom_call", output_to_operand_aliasing={{0}: (8, {}), {1}: (9, {})} | custom-call | flops 55000000 | bytes 150000 | tf_op jit(solution)/shard_map/pallas_call | solution.py:543
  40.5 2.9 %shard_map.163 = (f32[2,3,256,512]{3,2,1,0:T(8,128)}, f32[2,256,512]{2,1,0:T(8,128)}, f32[4,256]{1,0:T(4,128)}, f32[2,512]{1,0:T(2,128)}, f32[2,256,256]{2,1,0:T(8,128)}) custom-call(f32[288,128]{1,0:T(8,128)S(1)} %collective-permute-done.15.far_piece, ...), custom_call_target="tpu_custom_call", output_to_operand_aliasing={{0}: (24, {}), {1}: (25, {})} | custom-call | flops 2969999872 | bytes 8100000 | tf_op jit(solution)/shard_map/pallas_call | solution.py:543
  (36 shorter events, 0.9 us)
Async XLA Ops:
  0.6 9.3 %copy-start = (f32[2,512]{1,0:T(2,128)S(1)}, f32[2,512]{1,0:T(2,128)}, u32[]{:S(2)}) copy-start(f32[2,512]{1,0:T(2,128)} %bias.1) | copy-start | bytes 12292
  0.6 9.3 %copy-start.1 = (f32[4,256]{1,0:T(4,128)S(1)}, f32[4,256]{1,0:T(4,128)}, u32[]{:S(2)}) copy-start(f32[4,256]{1,0:T(4,128)} %embed.3) | copy-start | bytes 12292
  0.7 6.4 %collective-permute-start.2 = (s32[1,512]{1,0:T(1,128)}, s32[1,512]{1,0:T(1,128)S(1)}, u32[]{:S(2)}, u32[]{:S(2)}) collective-permute-start(s32[1,512]{1,0:T(1,128)} %bitcast.1), channel_id=1, source_target_pairs={{0,3},{1,2},{2,1},{3,0},{4,7},{5,6},{6,5},{7,4},{8,11},{9,10},{10,... | collective-permute-start | bytes 6152 | tf_op jit(solution)/shard_map/ppermute | solution.py:550
  3.2 3.9 %collective-permute-start.1 = (s32[1,512]{1,0:T(1,128)}, s32[1,512]{1,0:T(1,128)S(1)}, u32[]{:S(2)}, u32[]{:S(2)}) collective-permute-start(s32[1,512]{1,0:T(1,128)} %bitcast.2), channel_id=1, source_target_pairs={{0,2},{1,3},{2,0},{3,1},{4,6},{5,7},{6,4},{7,5},{8,10},{9,11},{10,... | collective-permute-start | bytes 6152 | tf_op jit(solution)/shard_map/ppermute | solution.py:550
  3.8 3.2 %collective-permute-start = (s32[1,512]{1,0:T(1,128)}, s32[1,512]{1,0:T(1,128)S(1)}, u32[]{:S(2)}, u32[]{:S(2)}) collective-permute-start(s32[1,512]{1,0:T(1,128)} %bitcast.3), channel_id=1, source_target_pairs={{0,1},{1,0},{2,3},{3,2},{4,5},{5,4},{6,7},{7,6},{8,9},{9,8},{10,11... | collective-permute-start | bytes 6152 | tf_op jit(solution)/shard_map/ppermute | solution.py:550
  7.1 5.2 %collective-permute-start.3 = (s32[4,512]{1,0:T(4,128)S(1)}, s32[4,512]{1,0:T(4,128)S(1)}, u32[]{:S(2)}, u32[]{:S(2)}) collective-permute-start(s32[4,512]{1,0:T(4,128)S(1)} %shard_map.145.after.refs_1_), channel_id=1, source_target_pairs={{0,4},{1,5},{2,6},{3,7},{4,0},{5,1},{6,2},{7,3},{8,12},{9,13},{10,... | collective-permute-start | bytes 24584 | tf_op jit(solution)/shard_map/ppermute | solution.py:550
  9.9 2.4 %copy-start.2 = (s32[2]{0:T(128)S(1)}, s32[2]{0:T(128)}, u32[]{:S(2)}) copy-start(s32[2]{0:T(128)} %refs_0_.1) | copy-start | bytes 28
  14.9 1.5 %collective-permute-start.4 = (f32[2,168,128]{2,1,0:T(8,128)S(1)}, f32[2,168,128]{2,1,0:T(8,128)S(1)}, u32[]{:S(2)}, u32[]{:S(2)}) collective-permute-start(f32[2,168,128]{2,1,0:T(8,128)S(1)} %get-tuple-element.83), channel_id=1, source_target_pairs={{0,1},{1,0},{2,3},{3,2},{4,5},{5,4},{6,7},{7,6},{8,9},{9,8},{10,11... | collective-permute-start | bytes 516104 | tf_op jit(solution)/shard_map/ppermute | solution.py:550
  15.9 2.2 %collective-permute-start.6 = (f32[2,240,128]{2,1,0:T(8,128)S(1)}, f32[2,240,128]{2,1,0:T(8,128)S(1)}, u32[]{:S(2)}, u32[]{:S(2)}) collective-permute-start(f32[2,240,128]{2,1,0:T(8,128)S(1)} %get-tuple-element.89), channel_id=1, source_target_pairs={{0,1},{1,0},{2,3},{3,2},{4,5},{5,4},{6,7},{7,6},{8,9},{9,8},{10,11... | collective-permute-start | bytes 737288 | tf_op jit(solution)/shard_map/ppermute | solution.py:550
  16.5 5.1 %collective-permute-start.5 = (f32[168,128]{1,0:T(8,128)S(1)}, f32[168,128]{1,0:T(8,128)S(1)}, u32[]{:S(2)}, u32[]{:S(2)}) collective-permute-start(f32[168,128]{1,0:T(8,128)S(1)} %get-tuple-element.88), channel_id=1, source_target_pairs={{0,2},{1,3},{2,0},{3,1},{4,6},{5,7},{6,4},{7,5},{8,10},{9,11},{10,... | collective-permute-start | bytes 258056 | tf_op jit(solution)/shard_map/ppermute | solution.py:550
  18.1 7.5 %collective-permute-start.7 = (f32[240,128]{1,0:T(8,128)S(1)}, f32[240,128]{1,0:T(8,128)S(1)}, u32[]{:S(2)}, u32[]{:S(2)}) collective-permute-start(f32[240,128]{1,0:T(8,128)S(1)} %get-tuple-element.93), channel_id=1, source_target_pairs={{0,2},{1,3},{2,0},{3,1},{4,6},{5,7},{6,4},{7,5},{8,10},{9,11},{10,... | collective-permute-start | bytes 368648 | tf_op jit(solution)/shard_map/ppermute | solution.py:550
  21.5 6.2 %collective-permute-start.9 = (f32[168,128]{1,0:T(8,128)S(1)}, f32[168,128]{1,0:T(8,128)S(1)}, u32[]{:S(2)}, u32[]{:S(2)}) collective-permute-start(f32[168,128]{1,0:T(8,128)S(1)} %shard_map.151.after.mine), channel_id=1, source_target_pairs={{0,4},{1,5},{2,6},{3,7},{4,0},{5,1},{6,2},{7,3},{8,12},{9,13},{10,... | collective-permute-start | bytes 258056 | tf_op jit(solution)/shard_map/ppermute | solution.py:550
  25.7 7.7 %collective-permute-start.8 = (f32[240,128]{1,0:T(8,128)S(1)}, f32[240,128]{1,0:T(8,128)S(1)}, u32[]{:S(2)}, u32[]{:S(2)}) collective-permute-start(f32[240,128]{1,0:T(8,128)S(1)} %shard_map.153.after.mine), channel_id=1, source_target_pairs={{0,4},{1,5},{2,6},{3,7},{4,0},{5,1},{6,2},{7,3},{8,12},{9,13},{10,... | collective-permute-start | bytes 368648 | tf_op jit(solution)/shard_map/ppermute | solution.py:550
  27.8 4.0 %collective-permute-start.10 = (f32[176,128]{1,0:T(8,128)S(1)}, f32[176,128]{1,0:T(8,128)S(1)}, u32[]{:S(2)}, u32[]{:S(2)}) collective-permute-start(f32[176,128]{1,0:T(8,128)S(1)} %shard_map.155.piece_00), channel_id=1, source_target_pairs={{0,1},{1,0},{2,3},{3,2},{4,5},{5,4},{6,7},{7,6},{8,9},{9,8},{10,11... | collective-permute-start | bytes 270344 | tf_op jit(solution)/shard_map/ppermute | solution.py:550
  27.9 7.4 %collective-permute-start.12 = (f32[176,128]{1,0:T(8,128)S(1)}, f32[176,128]{1,0:T(8,128)S(1)}, u32[]{:S(2)}, u32[]{:S(2)}) collective-permute-start(f32[176,128]{1,0:T(8,128)S(1)} %shard_map.155.piece_00), channel_id=1, source_target_pairs={{0,2},{1,3},{2,0},{3,1},{4,6},{5,7},{6,4},{7,5},{8,10},{9,11},{10,... | collective-permute-start | bytes 270344 | tf_op jit(solution)/shard_map/ppermute | solution.py:550
  33.4 5.2 %collective-permute-start.11 = (f32[288,128]{1,0:T(8,128)S(1)}, f32[288,128]{1,0:T(8,128)S(1)}, u32[]{:S(2)}, u32[]{:S(2)}) collective-permute-start(f32[288,128]{1,0:T(8,128)S(1)} %shard_map.156.value.taps), channel_id=1, source_target_pairs={{0,2},{1,3},{2,0},{3,1},{4,6},{5,7},{6,4},{7,5},{8,10},{9,11},{10,... | collective-permute-start | bytes 442376 | tf_op jit(solution)/shard_map/ppermute | solution.py:550
  35.3 1.9 %collective-permute-start.14 = (f32[144,128]{1,0:T(8,128)S(1)}, f32[144,128]{1,0:T(8,128)S(1)}, u32[]{:S(2)}, u32[]{:S(2)}) collective-permute-start(f32[144,128]{1,0:T(8,128)S(1)} %get-tuple-element.102), channel_id=1, source_target_pairs={{0,1},{1,0},{2,3},{3,2},{4,5},{5,4},{6,7},{7,6},{8,9},{9,8},{10,11... | collective-permute-start | bytes 221192 | tf_op jit(solution)/shard_map/ppermute | solution.py:550
  35.4 1.8 %collective-permute-start.13 = (f32[144,128]{1,0:T(8,128)S(1)}, f32[144,128]{1,0:T(8,128)S(1)}, u32[]{:S(2)}, u32[]{:S(2)}) collective-permute-start(f32[144,128]{1,0:T(8,128)S(1)} %get-tuple-element.101.refs_6_), channel_id=1, source_target_pairs={{0,1},{1,0},{2,3},{3,2},{4,5},{5,4},{6,7},{7,6},{8,9},{9,8},{10,11... | collective-permute-start | bytes 221192 | tf_op jit(solution)/shard_map/ppermute | solution.py:550
  38.6 1.9 %collective-permute-start.15 = (f32[288,128]{1,0:T(8,128)S(1)}, f32[288,128]{1,0:T(8,128)S(1)}, u32[]{:S(2)}, u32[]{:S(2)}) collective-permute-start(f32[288,128]{1,0:T(8,128)S(1)} %shard_map.161), channel_id=1, source_target_pairs={{0,1},{1,0},{2,3},{3,2},{4,5},{5,4},{6,7},{7,6},{8,9},{9,8},{10,11... | collective-permute-start | bytes 442376 | tf_op jit(solution)/shard_map/ppermute | solution.py:550
  38.7 1.8 %collective-permute-start.16 = (f32[176,128]{1,0:T(8,128)S(1)}, f32[176,128]{1,0:T(8,128)S(1)}, u32[]{:S(2)}, u32[]{:S(2)}) collective-permute-start(f32[176,128]{1,0:T(8,128)S(1)} %shard_map.160.after), channel_id=1, source_target_pairs={{0,1},{1,0},{2,3},{3,2},{4,5},{5,4},{6,7},{7,6},{8,9},{9,8},{10,11... | collective-permute-start | bytes 270344 | tf_op jit(solution)/shard_map/ppermute | solution.py:550

commit v4 on v2

--- a/solution.py
+++ b/solution.py
@@ -653,7 +653,6 @@
     other_y = swapped(piece_y, 2)
     core_x = [swapped(x, 1) for x in touched(piece_x, other_y, 2)]
 
-    far_y = swapped(other_y, 1)
     shared = (*levels, second_high, second_low)
     large = [(conv_weight.shape, F32, HBM), (mix_weight.shape, F32, HBM)]
     level_out = ((CONTEXTS, channels), F32, VMEM)
@@ -671,8 +670,9 @@
         micros=0.05,
     )(piece_x, *core_x, *shared)
     other_x = swapped(piece_x, 2)
-    rest_y = touched(far_y, partial)[0]
-    far_x = swapped(touched(other_x, rest_y)[0], 1)
+    late_y = touched(other_y, partial)[0]
+    rest_y = swapped(late_y, 1)
+    far_x = swapped(touched(other_x, late_y)[0], 1)
     g_conv, g_mix, bias_other, partial = call(
         other_columns_kernel,
         [VMEM] * 8 + [HBM] * 2,

time: 43.8 us -> 43.8 us (level)
  no operation moved by 1% of the time
where the time goes in v4:
time: 43.8 us; the launch traced here: 43.4 us
  Pallas kernels  18.2 us (42%)
  starting transfers between devices  17.8 us (41%)
  waiting for transfers between devices  6.53 us (15%)
  between operations  0.84 us (2%)
    pallas_call x19, Pallas kernels, placed(): run(*[pltpu.with_memory_space_constraint(x, HBM) if space is HBM else x f...  18.2 us
    ppermute x17, starting transfers between devices, swapped(): return lax.ppermute(value, 'seq', pairs)  17.8 us
    ppermute x17, waiting for transfers between devices, swapped(): return lax.ppermute(value, 'seq', pairs)  6.53 us
  transfers between devices with their start and end apart: 17, of which 5 were waited for; matrix products, arithmetic and copies ran while one was open for 0% of the time, Pallas kernels for 29%

profile of v4, /device:TPU:0, one launch (start us, length us, event | category | flops | bytes accessed | tf_op | source)
XLA Modules:
  0.0 43.4 jit_solution(2736137307704081506)
XLA Ops:
  0.7 2.5 %collective-permute-start.2 = (s32[1,512]{1,0:T(1,128)}, s32[1,512]{1,0:T(1,128)S(1)}, u32[]{:S(2)}, u32[]{:S(2)}) collective-permute-start(s32[1,512]{1,0:T(1,128)} %bitcast.1), channel_id=1, source_target_pairs={{0,3},{1,2},{2,1},{3,0},{4,7},{5,6},{6,5},{7,4},{8,11},{9,10},{10,... | collective-permute-start | bytes 6152 | tf_op jit(solution)/shard_map/ppermute | solution.py:543
  3.2 0.6 %collective-permute-start.1 = (s32[1,512]{1,0:T(1,128)}, s32[1,512]{1,0:T(1,128)S(1)}, u32[]{:S(2)}, u32[]{:S(2)}) collective-permute-start(s32[1,512]{1,0:T(1,128)} %bitcast.2), channel_id=1, source_target_pairs={{0,2},{1,3},{2,0},{3,1},{4,6},{5,7},{6,4},{7,5},{8,10},{9,11},{10,... | collective-permute-start | bytes 6152 | tf_op jit(solution)/shard_map/ppermute | solution.py:543
  3.9 3.2 %shard_map.144 = (s32[1,512]{1,0:T(1,128)S(1)}, f32[32,512]{1,0:T(8,128)S(1)}, f32[3,256,512]{2,1,0:T(8,128)S(1)}, f32[256,512]{1,0:T(8,128)S(1)}, f32[256,256]{...) custom-call(s32[1,512]{1,0:T(1,128)} %bitcast.4, ...), custom_call_target="tpu_custom_call" | custom-call | flops 2969999872 | bytes 8100000 | tf_op jit(solution)/shard_map/pallas_call | solution.py:536
  7.1 2.8 %collective-permute-start.3 = (s32[4,512]{1,0:T(4,128)S(1)}, s32[4,512]{1,0:T(4,128)S(1)}, u32[]{:S(2)}, u32[]{:S(2)}) collective-permute-start(s32[4,512]{1,0:T(4,128)S(1)} %shard_map.145.after.refs_1_), channel_id=1, source_target_pairs={{0,4},{1,5},{2,6},{3,7},{4,0},{5,1},{6,2},{7,3},{8,12},{9,13},{10,... | collective-permute-start | bytes 24584 | tf_op jit(solution)/shard_map/ppermute | solution.py:543
  9.9 2.4 %shard_map.146 = (f32[96,256]{1,0:T(8,128)S(1)}, f32[80,256]{1,0:T(8,128)S(1)}, f32[96,512]{1,0:T(8,128)S(1)}, bf16[256,512]{1,0:T(8,128)(2,1)S(1)}, bf16[256,51...) custom-call(f32[32,512]{1,0:T(8,128)S(1)} %get-tuple-element.67.after.taps, ...), custom_call_target="tpu_custom_call" | custom-call | flops 2750000128 | bytes 7500000 | tf_op jit(solution)/shard_map/pallas_call | solution.py:536
  12.3 2.6 %shard_map.147 = (f32[2,168,128]{2,1,0:T(8,128)S(1)}, f32[2,168,128]{2,1,0:T(8,128)S(1)}, bf16[1024,256]{1,0:T(8,128)(2,1)S(1)}, bf16[1024,256]{1,0:T(8,128)(2,1...) custom-call(s32[2]{0:T(128)S(1)} %copy-done.2, s32[4,512]{1,0:T(4,128)S(1)} %shard_map.145.after.refs_1_, ...), custom_call_target="tpu_custom_call" | custom-call | flops 2200000000 | bytes 6000000 | tf_op jit(solution)/shard_map/pallas_call | solution.py:536
  15.0 0.9 %shard_map.148 = (f32[2,240,128]{2,1,0:T(8,128)S(1)}, f32[2,240,128]{2,1,0:T(8,128)S(1)}) custom-call(bf16[2,256,512]{2,1,0:T(8,128)(2,1)S(1)} %get-tuple-element.73.hots, f32[1024,512]{1,0:T(8,128)S(1)} %get-tuple-element.80.slopes, f32[1024,256]{1,0:T(8,128)S(1)} %get-tuple-element.81.grad_hidden), custom_call_target="tpu_custom_call" | custom-call | flops 1650000000 | bytes 4500000 | tf_op jit(solution)/shard_map/pallas_call | solution.py:536
  15.9 0.6 %collective-permute-start.6 = (f32[2,240,128]{2,1,0:T(8,128)S(1)}, f32[2,240,128]{2,1,0:T(8,128)S(1)}, u32[]{:S(2)}, u32[]{:S(2)}) collective-permute-start(f32[2,240,128]{2,1,0:T(8,128)S(1)} %get-tuple-element.85), channel_id=1, source_target_pairs={{0,1},{1,0},{2,3},{3,2},{4,5},{5,4},{6,7},{7,6},{8,9},{9,8},{10,11... | collective-permute-start | bytes 737288 | tf_op jit(solution)/shard_map/ppermute | solution.py:543
  16.5 1.6 %collective-permute-start.5 = (f32[168,128]{1,0:T(8,128)S(1)}, f32[168,128]{1,0:T(8,128)S(1)}, u32[]{:S(2)}, u32[]{:S(2)}) collective-permute-start(f32[168,128]{1,0:T(8,128)S(1)} %get-tuple-element.84), channel_id=1, source_target_pairs={{0,2},{1,3},{2,0},{3,1},{4,6},{5,7},{6,4},{7,5},{8,10},{9,11},{10,... | collective-permute-start | bytes 258056 | tf_op jit(solution)/shard_map/ppermute | solution.py:543
  18.2 1.1 %collective-permute-start.7 = (f32[240,128]{1,0:T(8,128)S(1)}, f32[240,128]{1,0:T(8,128)S(1)}, u32[]{:S(2)}, u32[]{:S(2)}) collective-permute-start(f32[240,128]{1,0:T(8,128)S(1)} %get-tuple-element.89), channel_id=1, source_target_pairs={{0,2},{1,3},{2,0},{3,1},{4,6},{5,7},{6,4},{7,5},{8,10},{9,11},{10,... | collective-permute-start | bytes 368648 | tf_op jit(solution)/shard_map/ppermute | solution.py:543
  19.3 2.3 %collective-permute-done.5.received = f32[168,128]{1,0:T(8,128)S(1)} collective-permute-done((f32[168,128]{1,0:T(8,128)S(1)}, f32[168,128]{1,0:T(8,128)S(1)}, u32[]{:S(2)}, u32[]{:S(2)}) %collective-permute-start.5) | collective-permute-done | bytes 86048 | tf_op jit(solution)/shard_map/ppermute | solution.py:543
  21.6 2.2 %collective-permute-start.9 = (f32[168,128]{1,0:T(8,128)S(1)}, f32[168,128]{1,0:T(8,128)S(1)}, u32[]{:S(2)}, u32[]{:S(2)}) collective-permute-start(f32[168,128]{1,0:T(8,128)S(1)} %shard_map.151.after.mine), channel_id=1, source_target_pairs={{0,4},{1,5},{2,6},{3,7},{4,0},{5,1},{6,2},{7,3},{8,12},{9,13},{10,... | collective-permute-start | bytes 258056 | tf_op jit(solution)/shard_map/ppermute | solution.py:543
  23.8 1.9 %shard_map.152 = (f32[512,256]{1,0:T(8,128)}, f32[512,256]{1,0:T(8,128)}) custom-call(bf16[2,256,512]{2,1,0:T(8,128)(2,1)S(1)} %get-tuple-element.73.hots, bf16[1024,256]{1,0:T(8,128)(2,1)S(1)} %get-tuple-element.74.hidden_high, bf16[1024,256]{1,0:T(8,128)(2,1)S(1)} %get-tuple-element.75.hidden_low, f32[80,256]{1,0:T(8,128)S(1)} %get-tuple-element.76.local, ...), custom_call_target="tpu_custom_call" | custom-call | flops 2200000000 | bytes 6000000 | tf_op jit(solution)/shard_map/pallas_call | solution.py:536
  25.7 0.8 %collective-permute-start.8 = (f32[240,128]{1,0:T(8,128)S(1)}, f32[240,128]{1,0:T(8,128)S(1)}, u32[]{:S(2)}, u32[]{:S(2)}) collective-permute-start(f32[240,128]{1,0:T(8,128)S(1)} %shard_map.153.after.mine), channel_id=1, source_target_pairs={{0,4},{1,5},{2,6},{3,7},{4,0},{5,1},{6,2},{7,3},{8,12},{9,13},{10,... | collective-permute-start | bytes 368648 | tf_op jit(solution)/shard_map/ppermute | solution.py:543
  26.5 1.3 %shard_map.154 = (bf16[4,512,256]{2,1,0:T(8,128)(2,1)S(1)}, bf16[4,512,256]{2,1,0:T(8,128)(2,1)S(1)}, bf16[4,512,256]{2,1,0:T(8,128)(2,1)S(1)}, bf16[4,512,256]{...) custom-call(f32[3,256,512]{2,1,0:T(8,128)S(1)} %get-tuple-element.90, ...), custom_call_target="tpu_custom_call" | custom-call | flops 1540000000 | bytes 4200000 | tf_op jit(solution)/shard_map/pallas_call | solution.py:536
  27.9 3.9 %collective-permute-start.12 = (f32[176,128]{1,0:T(8,128)S(1)}, f32[176,128]{1,0:T(8,128)S(1)}, u32[]{:S(2)}, u32[]{:S(2)}) collective-permute-start(f32[176,128]{1,0:T(8,128)S(1)} %shard_map.155.piece_00), channel_id=1, source_target_pairs={{0,2},{1,3},{2,0},{3,1},{4,6},{5,7},{6,4},{7,5},{8,10},{9,11},{10,... | collective-permute-start | bytes 270344 | tf_op jit(solution)/shard_map/ppermute | solution.py:543
  31.8 1.5 %collective-permute-done.8.theirs = f32[240,128]{1,0:T(8,128)S(1)} collective-permute-done((f32[240,128]{1,0:T(8,128)S(1)}, f32[240,128]{1,0:T(8,128)S(1)}, u32[]{:S(2)}, u32[]{:S(2)}) %collective-permute-start.8) | collective-permute-done | bytes 122912 | tf_op jit(solution)/shard_map/ppermute | solution.py:543
  33.5 1.8 %collective-permute-done.12.after.value.piece_01 = f32[176,128]{1,0:T(8,128)S(1)} collective-permute-done((f32[176,128]{1,0:T(8,128)S(1)}, f32[176,128]{1,0:T(8,128)S(1)}, u32[]{:S(2)}, u32[]{:S(2)}) %collective-permute-start.12) | collective-permute-done | bytes 90144 | tf_op jit(solution)/shard_map/ppermute | solution.py:543
  35.4 0.4 collective-permute-start.14
  35.9 0.8 %collective-permute-done.13.core_first = f32[144,128]{1,0:T(8,128)S(1)} collective-permute-done((f32[144,128]{1,0:T(8,128)S(1)}, f32[144,128]{1,0:T(8,128)S(1)}, u32[]{:S(2)}, u32[]{:S(2)}) %collective-permute-start.13) | collective-permute-done | bytes 73760 | tf_op jit(solution)/shard_map/ppermute | solution.py:543
  36.8 1.7 %shard_map.158 = (f32[2,3,256,512]{3,2,1,0:T(8,128)}, f32[2,256,512]{2,1,0:T(8,128)}, f32[2,128]{1,0:T(2,128)S(1)}, f32[96,256]{1,0:T(8,128)S(1)}) custom-call(f32[288,128]{1,0:T(8,128)S(1)} %shard_map.156.value.own_piece, f32[144,128]{1,0:T(8,128)S(1)} %collective-permute-done.13.core_first, f32[144,128]{1,0:T(8,128)S(1)} %collective-permute-done.14.core_second, ...), custom_call_target="tpu_custom_call" | custom-call | flops 55000000 | bytes 150000 | tf_op jit(solution)/shard_map/pallas_call | solution.py:536
  38.6 0.4 collective-permute-start.15
  39.2 1.3 %shard_map.161 = (f32[2,3,256,512]{3,2,1,0:T(8,128)}, f32[2,256,512]{2,1,0:T(8,128)}, f32[1,128]{1,0:T(1,128)S(1)}, f32[96,256]{1,0:T(8,128)S(1)}) custom-call(f32[288,128]{1,0:T(8,128)S(1)} %collective-permute-done.11.value.taps, bf16[96,256]{1,0:T(8,128)(2,1)S(1)} %get-tuple-element.99.refs_0_.level_high, ...), custom_call_target="tpu_custom_call", output_to_operand_aliasing={{0}: (8, {}), {1}: (9, {})} | custom-call | flops 55000000 | bytes 150000 | tf_op jit(solution)/shard_map/pallas_call | solution.py:536
  40.5 2.9 %shard_map.162 = (f32[2,3,256,512]{3,2,1,0:T(8,128)}, f32[2,256,512]{2,1,0:T(8,128)}, f32[4,256]{1,0:T(4,128)}, f32[2,512]{1,0:T(2,128)}, f32[2,256,256]{2,1,0:T(8,128)}) custom-call(f32[288,128]{1,0:T(8,128)S(1)} %collective-permute-done.15.far_piece, ...), custom_call_target="tpu_custom_call", output_to_operand_aliasing={{0}: (23, {}), {1}: (24, {})} | custom-call | flops 2969999872 | bytes 8100000 | tf_op jit(solution)/shard_map/pallas_call | solution.py:536
  (35 shorter events, 1.0 us)
Async XLA Ops:
  0.6 9.3 %copy-start = (f32[2,512]{1,0:T(2,128)S(1)}, f32[2,512]{1,0:T(2,128)}, u32[]{:S(2)}) copy-start(f32[2,512]{1,0:T(2,128)} %bias.1) | copy-start | bytes 12292
  0.6 9.3 %copy-start.1 = (f32[4,256]{1,0:T(4,128)S(1)}, f32[4,256]{1,0:T(4,128)}, u32[]{:S(2)}) copy-start(f32[4,256]{1,0:T(4,128)} %embed.3) | copy-start | bytes 12292
  0.7 6.4 %collective-permute-start.2 = (s32[1,512]{1,0:T(1,128)}, s32[1,512]{1,0:T(1,128)S(1)}, u32[]{:S(2)}, u32[]{:S(2)}) collective-permute-start(s32[1,512]{1,0:T(1,128)} %bitcast.1), channel_id=1, source_target_pairs={{0,3},{1,2},{2,1},{3,0},{4,7},{5,6},{6,5},{7,4},{8,11},{9,10},{10,... | collective-permute-start | bytes 6152 | tf_op jit(solution)/shard_map/ppermute | solution.py:543
  3.2 3.9 %collective-permute-start.1 = (s32[1,512]{1,0:T(1,128)}, s32[1,512]{1,0:T(1,128)S(1)}, u32[]{:S(2)}, u32[]{:S(2)}) collective-permute-start(s32[1,512]{1,0:T(1,128)} %bitcast.2), channel_id=1, source_target_pairs={{0,2},{1,3},{2,0},{3,1},{4,6},{5,7},{6,4},{7,5},{8,10},{9,11},{10,... | collective-permute-start | bytes 6152 | tf_op jit(solution)/shard_map/ppermute | solution.py:543
  3.8 3.2 %collective-permute-start = (s32[1,512]{1,0:T(1,128)}, s32[1,512]{1,0:T(1,128)S(1)}, u32[]{:S(2)}, u32[]{:S(2)}) collective-permute-start(s32[1,512]{1,0:T(1,128)} %bitcast.3), channel_id=1, source_target_pairs={{0,1},{1,0},{2,3},{3,2},{4,5},{5,4},{6,7},{7,6},{8,9},{9,8},{10,11... | collective-permute-start | bytes 6152 | tf_op jit(solution)/shard_map/ppermute | solution.py:543
  7.1 5.2 %collective-permute-start.3 = (s32[4,512]{1,0:T(4,128)S(1)}, s32[4,512]{1,0:T(4,128)S(1)}, u32[]{:S(2)}, u32[]{:S(2)}) collective-permute-start(s32[4,512]{1,0:T(4,128)S(1)} %shard_map.145.after.refs_1_), channel_id=1, source_target_pairs={{0,4},{1,5},{2,6},{3,7},{4,0},{5,1},{6,2},{7,3},{8,12},{9,13},{10,... | collective-permute-start | bytes 24584 | tf_op jit(solution)/shard_map/ppermute | solution.py:543
  9.9 2.4 %copy-start.2 = (s32[2]{0:T(128)S(1)}, s32[2]{0:T(128)}, u32[]{:S(2)}) copy-start(s32[2]{0:T(128)} %refs_0_.1) | copy-start | bytes 28
  14.9 1.5 %collective-permute-start.4 = (f32[2,168,128]{2,1,0:T(8,128)S(1)}, f32[2,168,128]{2,1,0:T(8,128)S(1)}, u32[]{:S(2)}, u32[]{:S(2)}) collective-permute-start(f32[2,168,128]{2,1,0:T(8,128)S(1)} %get-tuple-element.79), channel_id=1, source_target_pairs={{0,1},{1,0},{2,3},{3,2},{4,5},{5,4},{6,7},{7,6},{8,9},{9,8},{10,11... | collective-permute-start | bytes 516104 | tf_op jit(solution)/shard_map/ppermute | solution.py:543
  15.9 2.2 %collective-permute-start.6 = (f32[2,240,128]{2,1,0:T(8,128)S(1)}, f32[2,240,128]{2,1,0:T(8,128)S(1)}, u32[]{:S(2)}, u32[]{:S(2)}) collective-permute-start(f32[2,240,128]{2,1,0:T(8,128)S(1)} %get-tuple-element.85), channel_id=1, source_target_pairs={{0,1},{1,0},{2,3},{3,2},{4,5},{5,4},{6,7},{7,6},{8,9},{9,8},{10,11... | collective-permute-start | bytes 737288 | tf_op jit(solution)/shard_map/ppermute | solution.py:543
  16.5 5.1 %collective-permute-start.5 = (f32[168,128]{1,0:T(8,128)S(1)}, f32[168,128]{1,0:T(8,128)S(1)}, u32[]{:S(2)}, u32[]{:S(2)}) collective-permute-start(f32[168,128]{1,0:T(8,128)S(1)} %get-tuple-element.84), channel_id=1, source_target_pairs={{0,2},{1,3},{2,0},{3,1},{4,6},{5,7},{6,4},{7,5},{8,10},{9,11},{10,... | collective-permute-start | bytes 258056 | tf_op jit(solution)/shard_map/ppermute | solution.py:543
  18.2 7.5 %collective-permute-start.7 = (f32[240,128]{1,0:T(8,128)S(1)}, f32[240,128]{1,0:T(8,128)S(1)}, u32[]{:S(2)}, u32[]{:S(2)}) collective-permute-start(f32[240,128]{1,0:T(8,128)S(1)} %get-tuple-element.89), channel_id=1, source_target_pairs={{0,2},{1,3},{2,0},{3,1},{4,6},{5,7},{6,4},{7,5},{8,10},{9,11},{10,... | collective-permute-start | bytes 368648 | tf_op jit(solution)/shard_map/ppermute | solution.py:543
  21.6 6.2 %collective-permute-start.9 = (f32[168,128]{1,0:T(8,128)S(1)}, f32[168,128]{1,0:T(8,128)S(1)}, u32[]{:S(2)}, u32[]{:S(2)}) collective-permute-start(f32[168,128]{1,0:T(8,128)S(1)} %shard_map.151.after.mine), channel_id=1, source_target_pairs={{0,4},{1,5},{2,6},{3,7},{4,0},{5,1},{6,2},{7,3},{8,12},{9,13},{10,... | collective-permute-start | bytes 258056 | tf_op jit(solution)/shard_map/ppermute | solution.py:543
  25.7 7.7 %collective-permute-start.8 = (f32[240,128]{1,0:T(8,128)S(1)}, f32[240,128]{1,0:T(8,128)S(1)}, u32[]{:S(2)}, u32[]{:S(2)}) collective-permute-start(f32[240,128]{1,0:T(8,128)S(1)} %shard_map.153.after.mine), channel_id=1, source_target_pairs={{0,4},{1,5},{2,6},{3,7},{4,0},{5,1},{6,2},{7,3},{8,12},{9,13},{10,... | collective-permute-start | bytes 368648 | tf_op jit(solution)/shard_map/ppermute | solution.py:543
  27.8 4.0 %collective-permute-start.10 = (f32[176,128]{1,0:T(8,128)S(1)}, f32[176,128]{1,0:T(8,128)S(1)}, u32[]{:S(2)}, u32[]{:S(2)}) collective-permute-start(f32[176,128]{1,0:T(8,128)S(1)} %shard_map.155.piece_00), channel_id=1, source_target_pairs={{0,1},{1,0},{2,3},{3,2},{4,5},{5,4},{6,7},{7,6},{8,9},{9,8},{10,11... | collective-permute-start | bytes 270344 | tf_op jit(solution)/shard_map/ppermute | solution.py:543
  27.9 7.4 %collective-permute-start.12 = (f32[176,128]{1,0:T(8,128)S(1)}, f32[176,128]{1,0:T(8,128)S(1)}, u32[]{:S(2)}, u32[]{:S(2)}) collective-permute-start(f32[176,128]{1,0:T(8,128)S(1)} %shard_map.155.piece_00), channel_id=1, source_target_pairs={{0,2},{1,3},{2,0},{3,1},{4,6},{5,7},{6,4},{7,5},{8,10},{9,11},{10,... | collective-permute-start | bytes 270344 | tf_op jit(solution)/shard_map/ppermute | solution.py:543
  33.4 5.2 %collective-permute-start.11 = (f32[288,128]{1,0:T(8,128)S(1)}, f32[288,128]{1,0:T(8,128)S(1)}, u32[]{:S(2)}, u32[]{:S(2)}) collective-permute-start(f32[288,128]{1,0:T(8,128)S(1)} %shard_map.156.value.own_piece), channel_id=1, source_target_pairs={{0,2},{1,3},{2,0},{3,1},{4,6},{5,7},{6,4},{7,5},{8,10},{9,11},{10,... | collective-permute-start | bytes 442376 | tf_op jit(solution)/shard_map/ppermute | solution.py:543
  35.3 1.3 %collective-permute-start.13 = (f32[144,128]{1,0:T(8,128)S(1)}, f32[144,128]{1,0:T(8,128)S(1)}, u32[]{:S(2)}, u32[]{:S(2)}) collective-permute-start(f32[144,128]{1,0:T(8,128)S(1)} %get-tuple-element.97), channel_id=1, source_target_pairs={{0,1},{1,0},{2,3},{3,2},{4,5},{5,4},{6,7},{7,6},{8,9},{9,8},{10,11... | collective-permute-start | bytes 221192 | tf_op jit(solution)/shard_map/ppermute | solution.py:543
  35.4 1.3 %collective-permute-start.14 = (f32[144,128]{1,0:T(8,128)S(1)}, f32[144,128]{1,0:T(8,128)S(1)}, u32[]{:S(2)}, u32[]{:S(2)}) collective-permute-start(f32[144,128]{1,0:T(8,128)S(1)} %get-tuple-element.98), channel_id=1, source_target_pairs={{0,1},{1,0},{2,3},{3,2},{4,5},{5,4},{6,7},{7,6},{8,9},{9,8},{10,11... | collective-permute-start | bytes 221192 | tf_op jit(solution)/shard_map/ppermute | solution.py:543
  38.6 1.9 %collective-permute-start.15 = (f32[288,128]{1,0:T(8,128)S(1)}, f32[288,128]{1,0:T(8,128)S(1)}, u32[]{:S(2)}, u32[]{:S(2)}) collective-permute-start(f32[288,128]{1,0:T(8,128)S(1)} %shard_map.160), channel_id=1, source_target_pairs={{0,1},{1,0},{2,3},{3,2},{4,5},{5,4},{6,7},{7,6},{8,9},{9,8},{10,11... | collective-permute-start | bytes 442376 | tf_op jit(solution)/shard_map/ppermute | solution.py:543
  39.0 1.5 %collective-permute-start.16 = (f32[176,128]{1,0:T(8,128)S(1)}, f32[176,128]{1,0:T(8,128)S(1)}, u32[]{:S(2)}, u32[]{:S(2)}) collective-permute-start(f32[176,128]{1,0:T(8,128)S(1)} %shard_map.159.after), channel_id=1, source_target_pairs={{0,1},{1,0},{2,3},{3,2},{4,5},{5,4},{6,7},{7,6},{8,9},{9,8},{10,11... | collective-permute-start | bytes 270344 | tf_op jit(solution)/shard_map/ppermute | solution.py:543

commit v5 on v3

--- a/solution.py
+++ b/solution.py
@@ -683,7 +683,7 @@
     )(*core_x, *shared, partial, g_conv, g_mix)
     other_x = swapped(piece_x, 2)
     late_y = touched(other_y, partial)[0]
-    rest_y = swapped(late_y, 1)
+    rest_y = swapped(other_y, 1)
     far_x = swapped(touched(other_x, late_y)[0], 1)
     g_conv, g_mix, bias_other, partial = call(
         other_columns_kernel,

time: 43.5 us -> 43.5 us (level)
  no operation moved by 1% of the time
where the time goes in v5:
time: 43.5 us; the launch traced here: 43.4 us
  Pallas kernels  19.1 us (44%)
  starting transfers between devices  17.8 us (41%)
  waiting for transfers between devices  5.63 us (13%)
  between operations  0.87 us (2%)
    pallas_call x20, Pallas kernels, placed(): run(*[pltpu.with_memory_space_constraint(x, HBM) if space is HBM else x f...  19.1 us
    ppermute x17, starting transfers between devices, swapped(): return lax.ppermute(value, 'seq', pairs)  17.8 us
    ppermute x17, waiting for transfers between devices, swapped(): return lax.ppermute(value, 'seq', pairs)  5.63 us
  transfers between devices with their start and end apart: 17, of which 3 were waited for; matrix products, arithmetic and copies ran while one was open for 0% of the time, Pallas kernels for 31%

profile of v5, /device:TPU:0, one launch (start us, length us, event | category | flops | bytes accessed | tf_op | source)
XLA Modules:
  0.0 43.4 jit_solution(15095754536946236024)
XLA Ops:
  0.7 2.5 %collective-permute-start.2 = (s32[1,512]{1,0:T(1,128)}, s32[1,512]{1,0:T(1,128)S(1)}, u32[]{:S(2)}, u32[]{:S(2)}) collective-permute-start(s32[1,512]{1,0:T(1,128)} %bitcast.1), channel_id=1, source_target_pairs={{0,3},{1,2},{2,1},{3,0},{4,7},{5,6},{6,5},{7,4},{8,11},{9,10},{10,... | collective-permute-start | bytes 6152 | tf_op jit(solution)/shard_map/ppermute | solution.py:550
  3.2 0.6 %collective-permute-start.1 = (s32[1,512]{1,0:T(1,128)}, s32[1,512]{1,0:T(1,128)S(1)}, u32[]{:S(2)}, u32[]{:S(2)}) collective-permute-start(s32[1,512]{1,0:T(1,128)} %bitcast.2), channel_id=1, source_target_pairs={{0,2},{1,3},{2,0},{3,1},{4,6},{5,7},{6,4},{7,5},{8,10},{9,11},{10,... | collective-permute-start | bytes 6152 | tf_op jit(solution)/shard_map/ppermute | solution.py:550
  3.9 3.2 %shard_map.144 = (s32[1,512]{1,0:T(1,128)S(1)}, f32[32,512]{1,0:T(8,128)S(1)}, f32[3,256,512]{2,1,0:T(8,128)S(1)}, f32[256,512]{1,0:T(8,128)S(1)}, f32[256,256]{...) custom-call(s32[1,512]{1,0:T(1,128)} %bitcast.4, ...), custom_call_target="tpu_custom_call" | custom-call | flops 2969999872 | bytes 8100000 | tf_op jit(solution)/shard_map/pallas_call | solution.py:543
  7.1 2.8 %collective-permute-start.3 = (s32[4,512]{1,0:T(4,128)S(1)}, s32[4,512]{1,0:T(4,128)S(1)}, u32[]{:S(2)}, u32[]{:S(2)}) collective-permute-start(s32[4,512]{1,0:T(4,128)S(1)} %shard_map.145.after.refs_1_), channel_id=1, source_target_pairs={{0,4},{1,5},{2,6},{3,7},{4,0},{5,1},{6,2},{7,3},{8,12},{9,13},{10,... | collective-permute-start | bytes 24584 | tf_op jit(solution)/shard_map/ppermute | solution.py:550
  9.9 2.3 %shard_map.146 = (f32[96,256]{1,0:T(8,128)S(1)}, f32[80,256]{1,0:T(8,128)S(1)}, f32[96,512]{1,0:T(8,128)S(1)}, bf16[256,512]{1,0:T(8,128)(2,1)S(1)}, bf16[256,51...) custom-call(f32[32,512]{1,0:T(8,128)S(1)} %get-tuple-element.71.after.taps, ...), custom_call_target="tpu_custom_call" | custom-call | flops 2750000128 | bytes 7500000 | tf_op jit(solution)/shard_map/pallas_call | solution.py:543
  12.3 2.6 %shard_map.147 = (f32[2,168,128]{2,1,0:T(8,128)S(1)}, f32[2,168,128]{2,1,0:T(8,128)S(1)}, bf16[1024,256]{1,0:T(8,128)(2,1)S(1)}, bf16[1024,256]{1,0:T(8,128)(2,1...) custom-call(s32[2]{0:T(128)S(1)} %copy-done.2, s32[4,512]{1,0:T(4,128)S(1)} %shard_map.145.after.refs_1_, ...), custom_call_target="tpu_custom_call" | custom-call | flops 2200000000 | bytes 6000000 | tf_op jit(solution)/shard_map/pallas_call | solution.py:543
  15.0 0.9 %shard_map.148 = (f32[2,240,128]{2,1,0:T(8,128)S(1)}, f32[2,240,128]{2,1,0:T(8,128)S(1)}) custom-call(bf16[2,256,512]{2,1,0:T(8,128)(2,1)S(1)} %get-tuple-element.77.hots, f32[1024,512]{1,0:T(8,128)S(1)} %get-tuple-element.84.slopes, f32[1024,256]{1,0:T(8,128)S(1)} %get-tuple-element.85.grad_hidden), custom_call_target="tpu_custom_call" | custom-call | flops 1650000000 | bytes 4500000 | tf_op jit(solution)/shard_map/pallas_call | solution.py:543
  15.9 0.5 %collective-permute-start.6 = (f32[2,240,128]{2,1,0:T(8,128)S(1)}, f32[2,240,128]{2,1,0:T(8,128)S(1)}, u32[]{:S(2)}, u32[]{:S(2)}) collective-permute-start(f32[2,240,128]{2,1,0:T(8,128)S(1)} %get-tuple-element.89), channel_id=1, source_target_pairs={{0,1},{1,0},{2,3},{3,2},{4,5},{5,4},{6,7},{7,6},{8,9},{9,8},{10,11... | collective-permute-start | bytes 737288 | tf_op jit(solution)/shard_map/ppermute | solution.py:550
  16.5 1.6 %collective-permute-start.5 = (f32[168,128]{1,0:T(8,128)S(1)}, f32[168,128]{1,0:T(8,128)S(1)}, u32[]{:S(2)}, u32[]{:S(2)}) collective-permute-start(f32[168,128]{1,0:T(8,128)S(1)} %get-tuple-element.88), channel_id=1, source_target_pairs={{0,2},{1,3},{2,0},{3,1},{4,6},{5,7},{6,4},{7,5},{8,10},{9,11},{10,... | collective-permute-start | bytes 258056 | tf_op jit(solution)/shard_map/ppermute | solution.py:550
  18.1 1.1 %collective-permute-start.7 = (f32[240,128]{1,0:T(8,128)S(1)}, f32[240,128]{1,0:T(8,128)S(1)}, u32[]{:S(2)}, u32[]{:S(2)}) collective-permute-start(f32[240,128]{1,0:T(8,128)S(1)} %get-tuple-element.93), channel_id=1, source_target_pairs={{0,2},{1,3},{2,0},{3,1},{4,6},{5,7},{6,4},{7,5},{8,10},{9,11},{10,... | collective-permute-start | bytes 368648 | tf_op jit(solution)/shard_map/ppermute | solution.py:550
  19.3 2.3 %collective-permute-done.5.received = f32[168,128]{1,0:T(8,128)S(1)} collective-permute-done((f32[168,128]{1,0:T(8,128)S(1)}, f32[168,128]{1,0:T(8,128)S(1)}, u32[]{:S(2)}, u32[]{:S(2)}) %collective-permute-start.5) | collective-permute-done | bytes 86048 | tf_op jit(solution)/shard_map/ppermute | solution.py:550
  21.5 2.2 %collective-permute-start.9 = (f32[168,128]{1,0:T(8,128)S(1)}, f32[168,128]{1,0:T(8,128)S(1)}, u32[]{:S(2)}, u32[]{:S(2)}) collective-permute-start(f32[168,128]{1,0:T(8,128)S(1)} %shard_map.151.after.mine), channel_id=1, source_target_pairs={{0,4},{1,5},{2,6},{3,7},{4,0},{5,1},{6,2},{7,3},{8,12},{9,13},{10,... | collective-permute-start | bytes 258056 | tf_op jit(solution)/shard_map/ppermute | solution.py:550
  23.8 1.9 %shard_map.152 = (f32[512,256]{1,0:T(8,128)}, f32[512,256]{1,0:T(8,128)}) custom-call(bf16[2,256,512]{2,1,0:T(8,128)(2,1)S(1)} %get-tuple-element.77.hots, bf16[1024,256]{1,0:T(8,128)(2,1)S(1)} %get-tuple-element.78.hidden_high, bf16[1024,256]{1,0:T(8,128)(2,1)S(1)} %get-tuple-element.79.hidden_low, f32[80,256]{1,0:T(8,128)S(1)} %get-tuple-element.80.local, ...), custom_call_target="tpu_custom_call" | custom-call | flops 2200000000 | bytes 6000000 | tf_op jit(solution)/shard_map/pallas_call | solution.py:543
  25.7 0.8 %collective-permute-start.8 = (f32[240,128]{1,0:T(8,128)S(1)}, f32[240,128]{1,0:T(8,128)S(1)}, u32[]{:S(2)}, u32[]{:S(2)}) collective-permute-start(f32[240,128]{1,0:T(8,128)S(1)} %shard_map.153.after.mine), channel_id=1, source_target_pairs={{0,4},{1,5},{2,6},{3,7},{4,0},{5,1},{6,2},{7,3},{8,12},{9,13},{10,... | collective-permute-start | bytes 368648 | tf_op jit(solution)/shard_map/ppermute | solution.py:550
  26.5 1.2 %shard_map.154 = (bf16[4,512,256]{2,1,0:T(8,128)(2,1)S(1)}, bf16[4,512,256]{2,1,0:T(8,128)(2,1)S(1)}, bf16[4,512,256]{2,1,0:T(8,128)(2,1)S(1)}, bf16[4,512,256]{...) custom-call(f32[3,256,512]{2,1,0:T(8,128)S(1)} %get-tuple-element.94, ...), custom_call_target="tpu_custom_call" | custom-call | flops 1540000000 | bytes 4200000 | tf_op jit(solution)/shard_map/pallas_call | solution.py:543
  27.9 3.9 %collective-permute-start.12 = (f32[176,128]{1,0:T(8,128)S(1)}, f32[176,128]{1,0:T(8,128)S(1)}, u32[]{:S(2)}, u32[]{:S(2)}) collective-permute-start(f32[176,128]{1,0:T(8,128)S(1)} %shard_map.155.piece_00), channel_id=1, source_target_pairs={{0,2},{1,3},{2,0},{3,1},{4,6},{5,7},{6,4},{7,5},{8,10},{9,11},{10,... | collective-permute-start | bytes 270344 | tf_op jit(solution)/shard_map/ppermute | solution.py:550
  31.8 1.5 %collective-permute-done.8.theirs = f32[240,128]{1,0:T(8,128)S(1)} collective-permute-done((f32[240,128]{1,0:T(8,128)S(1)}, f32[240,128]{1,0:T(8,128)S(1)}, u32[]{:S(2)}, u32[]{:S(2)}) %collective-permute-start.8) | collective-permute-done | bytes 122912 | tf_op jit(solution)/shard_map/ppermute | solution.py:550
  33.5 1.8 %collective-permute-done.12.after.value.piece_01 = f32[176,128]{1,0:T(8,128)S(1)} collective-permute-done((f32[176,128]{1,0:T(8,128)S(1)}, f32[176,128]{1,0:T(8,128)S(1)}, u32[]{:S(2)}, u32[]{:S(2)}) %collective-permute-start.12) | collective-permute-done | bytes 90144 | tf_op jit(solution)/shard_map/ppermute | solution.py:550
  35.4 0.4 collective-permute-start.13
  35.9 1.3 %shard_map.158 = (f32[2,3,256,512]{3,2,1,0:T(8,128)}, f32[2,256,512]{2,1,0:T(8,128)}, f32[1,128]{1,0:T(1,128)S(1)}, f32[96,256]{1,0:T(8,128)S(1)}) custom-call(f32[288,128]{1,0:T(8,128)S(1)} %shard_map.156.value.taps, bf16[96,256]{1,0:T(8,128)(2,1)S(1)} %get-tuple-element.103.refs_0_.level_high, bf16[96,256]{1,0:T(8,128)(2,1)S(1)} %get-tuple-element.104.refs_1_.level_low, ...), custom_call_target="tpu_custom_call" | custom-call | flops 1320000000 | bytes 3600000 | tf_op jit(solution)/shard_map/pallas_call | solution.py:543
  37.2 1.3 %shard_map.159 = (f32[2,3,256,512]{3,2,1,0:T(8,128)}, f32[2,256,512]{2,1,0:T(8,128)}, f32[1,128]{1,0:T(1,128)S(1)}, f32[96,256]{1,0:T(8,128)S(1)}) custom-call(f32[144,128]{1,0:T(8,128)S(1)} %collective-permute-done.13.first, f32[144,128]{1,0:T(8,128)S(1)} %collective-permute-done.14.second, ...), custom_call_target="tpu_custom_call", output_to_operand_aliasing={{0}: (9, {}), {1}: (10, {})} | custom-call | flops 55000000 | bytes 150000 | tf_op jit(solution)/shard_map/pallas_call | solution.py:543
  38.7 0.5 %collective-permute-start.16 = (f32[176,128]{1,0:T(8,128)S(1)}, f32[176,128]{1,0:T(8,128)S(1)}, u32[]{:S(2)}, u32[]{:S(2)}) collective-permute-start(f32[176,128]{1,0:T(8,128)S(1)} %collective-permute-done.12.after.value.piece_01), channel_id=1, source_target_pairs={{0,1},{1,0},{2,3},{3,2},{4,5},{5,4},{6,7},{7,6},{8,9},{9,8},{10,11... | collective-permute-start | bytes 270344 | tf_op jit(solution)/shard_map/ppermute | solution.py:550
  39.2 1.3 %shard_map.162 = (f32[2,3,256,512]{3,2,1,0:T(8,128)}, f32[2,256,512]{2,1,0:T(8,128)}, f32[1,128]{1,0:T(1,128)S(1)}, f32[96,256]{1,0:T(8,128)S(1)}) custom-call(f32[288,128]{1,0:T(8,128)S(1)} %collective-permute-done.11.value.taps, bf16[96,256]{1,0:T(8,128)(2,1)S(1)} %get-tuple-element.103.refs_0_.level_high, ...), custom_call_target="tpu_custom_call", output_to_operand_aliasing={{0}: (8, {}), {1}: (9, {})} | custom-call | flops 55000000 | bytes 150000 | tf_op jit(solution)/shard_map/pallas_call | solution.py:543
  40.5 2.9 %shard_map.163 = (f32[2,3,256,512]{3,2,1,0:T(8,128)}, f32[2,256,512]{2,1,0:T(8,128)}, f32[4,256]{1,0:T(4,128)}, f32[2,512]{1,0:T(2,128)}, f32[2,256,256]{2,1,0:T(8,128)}) custom-call(f32[288,128]{1,0:T(8,128)S(1)} %collective-permute-done.15.far_piece, ...), custom_call_target="tpu_custom_call", output_to_operand_aliasing={{0}: (24, {}), {1}: (25, {})} | custom-call | flops 2969999872 | bytes 8100000 | tf_op jit(solution)/shard_map/pallas_call | solution.py:543
  (36 shorter events, 0.9 us)
Async XLA Ops:
  0.6 9.3 %copy-start = (f32[2,512]{1,0:T(2,128)S(1)}, f32[2,512]{1,0:T(2,128)}, u32[]{:S(2)}) copy-start(f32[2,512]{1,0:T(2,128)} %bias.1) | copy-start | bytes 12292
  0.6 9.3 %copy-start.1 = (f32[4,256]{1,0:T(4,128)S(1)}, f32[4,256]{1,0:T(4,128)}, u32[]{:S(2)}) copy-start(f32[4,256]{1,0:T(4,128)} %embed.3) | copy-start | bytes 12292
  0.7 6.4 %collective-permute-start.2 = (s32[1,512]{1,0:T(1,128)}, s32[1,512]{1,0:T(1,128)S(1)}, u32[]{:S(2)}, u32[]{:S(2)}) collective-permute-start(s32[1,512]{1,0:T(1,128)} %bitcast.1), channel_id=1, source_target_pairs={{0,3},{1,2},{2,1},{3,0},{4,7},{5,6},{6,5},{7,4},{8,11},{9,10},{10,... | collective-permute-start | bytes 6152 | tf_op jit(solution)/shard_map/ppermute | solution.py:550
  3.2 3.9 %collective-permute-start.1 = (s32[1,512]{1,0:T(1,128)}, s32[1,512]{1,0:T(1,128)S(1)}, u32[]{:S(2)}, u32[]{:S(2)}) collective-permute-start(s32[1,512]{1,0:T(1,128)} %bitcast.2), channel_id=1, source_target_pairs={{0,2},{1,3},{2,0},{3,1},{4,6},{5,7},{6,4},{7,5},{8,10},{9,11},{10,... | collective-permute-start | bytes 6152 | tf_op jit(solution)/shard_map/ppermute | solution.py:550
  3.8 3.2 %collective-permute-start = (s32[1,512]{1,0:T(1,128)}, s32[1,512]{1,0:T(1,128)S(1)}, u32[]{:S(2)}, u32[]{:S(2)}) collective-permute-start(s32[1,512]{1,0:T(1,128)} %bitcast.3), channel_id=1, source_target_pairs={{0,1},{1,0},{2,3},{3,2},{4,5},{5,4},{6,7},{7,6},{8,9},{9,8},{10,11... | collective-permute-start | bytes 6152 | tf_op jit(solution)/shard_map/ppermute | solution.py:550
  7.1 5.2 %collective-permute-start.3 = (s32[4,512]{1,0:T(4,128)S(1)}, s32[4,512]{1,0:T(4,128)S(1)}, u32[]{:S(2)}, u32[]{:S(2)}) collective-permute-start(s32[4,512]{1,0:T(4,128)S(1)} %shard_map.145.after.refs_1_), channel_id=1, source_target_pairs={{0,4},{1,5},{2,6},{3,7},{4,0},{5,1},{6,2},{7,3},{8,12},{9,13},{10,... | collective-permute-start | bytes 24584 | tf_op jit(solution)/shard_map/ppermute | solution.py:550
  9.9 2.4 %copy-start.2 = (s32[2]{0:T(128)S(1)}, s32[2]{0:T(128)}, u32[]{:S(2)}) copy-start(s32[2]{0:T(128)} %refs_0_.1) | copy-start | bytes 28
  14.9 1.5 %collective-permute-start.4 = (f32[2,168,128]{2,1,0:T(8,128)S(1)}, f32[2,168,128]{2,1,0:T(8,128)S(1)}, u32[]{:S(2)}, u32[]{:S(2)}) collective-permute-start(f32[2,168,128]{2,1,0:T(8,128)S(1)} %get-tuple-element.83), channel_id=1, source_target_pairs={{0,1},{1,0},{2,3},{3,2},{4,5},{5,4},{6,7},{7,6},{8,9},{9,8},{10,11... | collective-permute-start | bytes 516104 | tf_op jit(solution)/shard_map/ppermute | solution.py:550
  15.9 2.2 %collective-permute-start.6 = (f32[2,240,128]{2,1,0:T(8,128)S(1)}, f32[2,240,128]{2,1,0:T(8,128)S(1)}, u32[]{:S(2)}, u32[]{:S(2)}) collective-permute-start(f32[2,240,128]{2,1,0:T(8,128)S(1)} %get-tuple-element.89), channel_id=1, source_target_pairs={{0,1},{1,0},{2,3},{3,2},{4,5},{5,4},{6,7},{7,6},{8,9},{9,8},{10,11... | collective-permute-start | bytes 737288 | tf_op jit(solution)/shard_map/ppermute | solution.py:550
  16.5 5.1 %collective-permute-start.5 = (f32[168,128]{1,0:T(8,128)S(1)}, f32[168,128]{1,0:T(8,128)S(1)}, u32[]{:S(2)}, u32[]{:S(2)}) collective-permute-start(f32[168,128]{1,0:T(8,128)S(1)} %get-tuple-element.88), channel_id=1, source_target_pairs={{0,2},{1,3},{2,0},{3,1},{4,6},{5,7},{6,4},{7,5},{8,10},{9,11},{10,... | collective-permute-start | bytes 258056 | tf_op jit(solution)/shard_map/ppermute | solution.py:550
  18.1 7.5 %collective-permute-start.7 = (f32[240,128]{1,0:T(8,128)S(1)}, f32[240,128]{1,0:T(8,128)S(1)}, u32[]{:S(2)}, u32[]{:S(2)}) collective-permute-start(f32[240,128]{1,0:T(8,128)S(1)} %get-tuple-element.93), channel_id=1, source_target_pairs={{0,2},{1,3},{2,0},{3,1},{4,6},{5,7},{6,4},{7,5},{8,10},{9,11},{10,... | collective-permute-start | bytes 368648 | tf_op jit(solution)/shard_map/ppermute | solution.py:550
  21.5 6.2 %collective-permute-start.9 = (f32[168,128]{1,0:T(8,128)S(1)}, f32[168,128]{1,0:T(8,128)S(1)}, u32[]{:S(2)}, u32[]{:S(2)}) collective-permute-start(f32[168,128]{1,0:T(8,128)S(1)} %shard_map.151.after.mine), channel_id=1, source_target_pairs={{0,4},{1,5},{2,6},{3,7},{4,0},{5,1},{6,2},{7,3},{8,12},{9,13},{10,... | collective-permute-start | bytes 258056 | tf_op jit(solution)/shard_map/ppermute | solution.py:550
  25.7 7.7 %collective-permute-start.8 = (f32[240,128]{1,0:T(8,128)S(1)}, f32[240,128]{1,0:T(8,128)S(1)}, u32[]{:S(2)}, u32[]{:S(2)}) collective-permute-start(f32[240,128]{1,0:T(8,128)S(1)} %shard_map.153.after.mine), channel_id=1, source_target_pairs={{0,4},{1,5},{2,6},{3,7},{4,0},{5,1},{6,2},{7,3},{8,12},{9,13},{10,... | collective-permute-start | bytes 368648 | tf_op jit(solution)/shard_map/ppermute | solution.py:550
  27.8 4.0 %collective-permute-start.10 = (f32[176,128]{1,0:T(8,128)S(1)}, f32[176,128]{1,0:T(8,128)S(1)}, u32[]{:S(2)}, u32[]{:S(2)}) collective-permute-start(f32[176,128]{1,0:T(8,128)S(1)} %shard_map.155.piece_00), channel_id=1, source_target_pairs={{0,1},{1,0},{2,3},{3,2},{4,5},{5,4},{6,7},{7,6},{8,9},{9,8},{10,11... | collective-permute-start | bytes 270344 | tf_op jit(solution)/shard_map/ppermute | solution.py:550
  27.9 7.4 %collective-permute-start.12 = (f32[176,128]{1,0:T(8,128)S(1)}, f32[176,128]{1,0:T(8,128)S(1)}, u32[]{:S(2)}, u32[]{:S(2)}) collective-permute-start(f32[176,128]{1,0:T(8,128)S(1)} %shard_map.155.piece_00), channel_id=1, source_target_pairs={{0,2},{1,3},{2,0},{3,1},{4,6},{5,7},{6,4},{7,5},{8,10},{9,11},{10,... | collective-permute-start | bytes 270344 | tf_op jit(solution)/shard_map/ppermute | solution.py:550
  33.4 5.2 %collective-permute-start.11 = (f32[288,128]{1,0:T(8,128)S(1)}, f32[288,128]{1,0:T(8,128)S(1)}, u32[]{:S(2)}, u32[]{:S(2)}) collective-permute-start(f32[288,128]{1,0:T(8,128)S(1)} %shard_map.156.value.taps), channel_id=1, source_target_pairs={{0,2},{1,3},{2,0},{3,1},{4,6},{5,7},{6,4},{7,5},{8,10},{9,11},{10,... | collective-permute-start | bytes 442376 | tf_op jit(solution)/shard_map/ppermute | solution.py:550
  35.3 1.9 %collective-permute-start.14 = (f32[144,128]{1,0:T(8,128)S(1)}, f32[144,128]{1,0:T(8,128)S(1)}, u32[]{:S(2)}, u32[]{:S(2)}) collective-permute-start(f32[144,128]{1,0:T(8,128)S(1)} %get-tuple-element.102), channel_id=1, source_target_pairs={{0,1},{1,0},{2,3},{3,2},{4,5},{5,4},{6,7},{7,6},{8,9},{9,8},{10,11... | collective-permute-start | bytes 221192 | tf_op jit(solution)/shard_map/ppermute | solution.py:550
  35.4 1.8 %collective-permute-start.13 = (f32[144,128]{1,0:T(8,128)S(1)}, f32[144,128]{1,0:T(8,128)S(1)}, u32[]{:S(2)}, u32[]{:S(2)}) collective-permute-start(f32[144,128]{1,0:T(8,128)S(1)} %get-tuple-element.101.refs_6_), channel_id=1, source_target_pairs={{0,1},{1,0},{2,3},{3,2},{4,5},{5,4},{6,7},{7,6},{8,9},{9,8},{10,11... | collective-permute-start | bytes 221192 | tf_op jit(solution)/shard_map/ppermute | solution.py:550
  38.6 1.9 %collective-permute-start.15 = (f32[288,128]{1,0:T(8,128)S(1)}, f32[288,128]{1,0:T(8,128)S(1)}, u32[]{:S(2)}, u32[]{:S(2)}) collective-permute-start(f32[288,128]{1,0:T(8,128)S(1)} %shard_map.161), channel_id=1, source_target_pairs={{0,1},{1,0},{2,3},{3,2},{4,5},{5,4},{6,7},{7,6},{8,9},{9,8},{10,11... | collective-permute-start | bytes 442376 | tf_op jit(solution)/shard_map/ppermute | solution.py:550
  38.7 1.8 %collective-permute-start.16 = (f32[176,128]{1,0:T(8,128)S(1)}, f32[176,128]{1,0:T(8,128)S(1)}, u32[]{:S(2)}, u32[]{:S(2)}) collective-permute-start(f32[176,128]{1,0:T(8,128)S(1)} %collective-permute-done.12.after.value.piece_01), channel_id=1, source_target_pairs={{0,1},{1,0},{2,3},{3,2},{4,5},{5,4},{6,7},{7,6},{8,9},{9,8},{10,11... | collective-permute-start | bytes 270344 | tf_op jit(solution)/shard_map/ppermute | solution.py:550
